TPU v7x, 128 devices: a whole 4x4x4 slice. The times are simulated.
128 devices in a mesh: span: 8 (over x_lo, z), tensor: 16 (over x_hi, y, core).
Axes of the slice: x: 4 (x_hi: 2, x_lo: 2; x = x_hi * 2 + x_lo), y: 4, z: 4, core: 2. Of those that a mesh axis runs over, the one named last changes fastest.
Arguments:
- inputs: bfloat16 [8192, 2048], P('span'), may hold values from -6 to 6
- out_grad: bfloat16 [8192, 2048], P('span'), may hold values from -6 to 6
- lengths: int32 [2, 3], replicated, may hold values from 1 to 2560, 4096 in all within a row
- span_order: int32 [64], replicated, may hold values from 0 to 63, as said below
- w_query: bfloat16 [2048, 2048], P('span', 'tensor'), may hold values from -0.125 to 0.125
- w_key: bfloat16 [2048, 1024], P('span', 'tensor'), may hold values from -0.125 to 0.125
- w_value: bfloat16 [2048, 1024], P('span', 'tensor'), may hold values from -0.125 to 0.125
- w_out: bfloat16 [2048, 2048], P('tensor', 'span'), may hold values from -4 to 4
- w_gate: bfloat16 [2048, 6144], P('span', 'tensor'), may hold values from -0.125 to 0.125
- w_up: bfloat16 [2048, 6144], P('span', 'tensor'), may hold values from -0.125 to 0.125
- w_down: bfloat16 [6144, 2048], P('tensor', 'span'), may hold values from -0.078125 to 0.078125
- norm_attn: bfloat16 [2048], P('span'), may hold values from 0.5 to 1.5
- norm_mlp: bfloat16 [2048], P('span'), may hold values from 0.5 to 1.5
- norm_query: bfloat16 [128], P('span'), may hold values from 0.5 to 1.5
- norm_key: bfloat16 [128], P('span'), may hold values from 0.5 to 1.5
Outputs:
- layer_out: float32 [8192, 2048], P('span', 'tensor')
- in_grad: float32 [8192, 2048], P('span', 'tensor')
- grad_query: float32 [2048, 2048], P('span', 'tensor')
- grad_key: float32 [2048, 1024], P('span', 'tensor')
- grad_value: float32 [2048, 1024], P('span', 'tensor')
- grad_out: float32 [2048, 2048], P('tensor', 'span')
- grad_gate: float32 [2048, 6144], P('span', 'tensor')
- grad_up: float32 [2048, 6144], P('span', 'tensor')
- grad_down: float32 [6144, 2048], P('tensor', 'span')
- grad_norm_attn: float32 [2048], P('span')
- grad_norm_mlp: float32 [2048], P('span')
- grad_norm_query: float32 [128], P('span')
- grad_norm_key: float32 [128], P('span')
Inputs may be any that keep to these rules, and one draw needn't show every extreme that they name: Row m holds the lengths of the documents of micro-batch m, laid end to end from its first token; each row sums to 4096. `span_order`: every span number appears exactly once; slot s lies on index s // 8 of span.
All inputs are finite; a program needn't handle non-finite values.
Results may differ from a plain program's by a relative error of at most 0.035.
Values may be sent and summed in bfloat16 or wider, within the bound.
No kernel may reach another device: no remote copies, remote signals or barrier semaphores. Data moves between devices by JAX's collectives and lax.ppermute only.
A program may use at most 192 MiB of HBM per device.

v0:
```python
import jax
import jax.numpy as jnp
from jax import lax
from jax.sharding import PartitionSpec as P

SPAN = 128
MICRO = 2


epsilon = 1e-06
rope_base = 1000000.0
neg_large = -1e30
block_limit = 1024


def from_partner(block, axis, bit):
    count = lax.axis_size(axis)
    route = []
    for low in range(count):
        high = low | 1 << bit
        if high != low and high < count:
            route += [(low, high), (high, low)]
    return lax.ppermute(block, axis, route)


def inverse_rms(values):
    return lax.rsqrt(jnp.mean(values * values, axis=-1, keepdims=True) + epsilon)


def rotate(values, cos_table, sin_table):
    middle = values.shape[-1] // 2
    former = values[..., :middle]
    latter = values[..., middle:]
    return jnp.concatenate(
        [former * cos_table - latter * sin_table, latter * cos_table + former * sin_table], axis=-1
    )


def rotate_back(values, cos_table, sin_table):
    middle = values.shape[-1] // 2
    former = values[..., :middle]
    latter = values[..., middle:]
    return jnp.concatenate(
        [former * cos_table + latter * sin_table, latter * cos_table - former * sin_table], axis=-1
    )


def norm_back(incoming, normal, inverse):
    return inverse * (incoming - normal * jnp.mean(incoming * normal, axis=-1, keepdims=True))


def plain_dot(first_op, second_op):
    return jnp.dot(first_op, second_op, preferred_element_type=jnp.float32)


def left_dot(first_op, second_op):
    return lax.dot_general(
        first_op, second_op, (((0,), (0,)), ((), ())), preferred_element_type=jnp.float32
    )


def right_dot(first_op, second_op):
    return lax.dot_general(
        first_op, second_op, (((1,), (1,)), ((), ())), preferred_element_type=jnp.float32
    )


def token_layout(lengths, tokens, micro_tokens):
    doc_count = lengths.shape[1]
    batch_of = tokens // micro_tokens
    offset = tokens % micro_tokens
    doc_ends = jnp.cumsum(lengths, axis=1, dtype=jnp.int32)
    row_ends = jnp.take(doc_ends, batch_of, axis=0)
    row_lengths = jnp.take(lengths, batch_of, axis=0)
    document = jnp.sum((offset[:, None] >= row_ends).astype(jnp.int32), axis=1, dtype=jnp.int32)
    picker = jnp.arange(doc_count, dtype=jnp.int32)[None, :] == document[:, None]
    doc_start = jnp.sum(jnp.where(picker, row_ends - row_lengths, 0), axis=1, dtype=jnp.int32)
    return (batch_of * doc_count + document, offset - doc_start)


def rope_tables(positions, head_size):
    frequency = jnp.power(
        rope_base, -2.0 * jnp.arange(head_size // 2, dtype=jnp.float32) / head_size
    )
    angles = positions.astype(jnp.float32)[:, None] * frequency[None, :]
    return (jnp.cos(angles), jnp.sin(angles))


def slot_tokens(span_order, slots):
    picked = jnp.take(span_order, slots, axis=0)
    return (picked[:, None] * SPAN + jnp.arange(SPAN, dtype=jnp.int32)[None, :]).reshape(-1)


def body(
    inputs,
    out_grad,
    lengths,
    span_order,
    w_query,
    w_key,
    w_value,
    w_out,
    w_gate,
    w_up,
    w_down,
    norm_attn,
    norm_mlp,
    norm_query,
    norm_key,
):
    span_count = lax.axis_size("span")
    tensor_count = lax.axis_size("tensor")
    span_place = lax.axis_index("span")
    tensor_place = lax.axis_index("tensor")
    all_spans = span_order.shape[0]
    per_device = all_spans // span_count
    local_rows = per_device * SPAN
    total_rows = all_spans * SPAN
    micro_tokens = total_rows // MICRO
    model_width = inputs.shape[1]
    slice_width = model_width // tensor_count
    own_slots = span_place * per_device + jnp.arange(per_device, dtype=jnp.int32)
    own_spans = jnp.take(span_order, own_slots, axis=0)
    gathered = lax.all_gather(inputs, "span", axis=0, tiled=True)
    picked = jnp.take(gathered.reshape(all_spans, SPAN, model_width), own_spans, axis=0)
    layer_in = picked.reshape(local_rows, model_width)
    (
        full_query,
        own_key,
        own_value,
        full_out,
        full_gate,
        full_up,
        full_down,
        gain_attn,
        gain_mlp,
        gain_query,
        gain_key,
    ) = (
        lax.all_gather(w_query, "span", axis=0, tiled=True),
        lax.all_gather(w_key, "span", axis=0, tiled=True),
        lax.all_gather(w_value, "span", axis=0, tiled=True),
        lax.all_gather(w_out, "span", axis=1, tiled=True),
        lax.all_gather(w_gate, "span", axis=0, tiled=True),
        lax.all_gather(w_up, "span", axis=0, tiled=True),
        lax.all_gather(w_down, "span", axis=1, tiled=True),
        lax.all_gather(norm_attn, "span", axis=0, tiled=True),
        lax.all_gather(norm_mlp, "span", axis=0, tiled=True),
        lax.all_gather(norm_query, "span", axis=0, tiled=True),
        lax.all_gather(norm_key, "span", axis=0, tiled=True),
    )
    gain_attn = gain_attn.astype(jnp.float32)
    gain_mlp = gain_mlp.astype(jnp.float32)
    gain_query = gain_query.astype(jnp.float32)
    gain_key = gain_key.astype(jnp.float32)
    head_size = gain_query.shape[0]
    own_cols = own_key.shape[1]
    shared = own_cols < head_size
    pair_bit = tensor_place % 2
    other_key, other_value = from_partner((own_key, own_value), "tensor", 0)
    lower_half = pair_bit == 0
    key_weight = jnp.where(
        lower_half,
        jnp.concatenate([own_key, other_key], 1),
        jnp.concatenate([other_key, own_key], 1),
    )
    value_weight = jnp.where(
        lower_half,
        jnp.concatenate([own_value, other_value], 1),
        jnp.concatenate([other_value, own_value], 1),
    )
    key_share = 0.5
    col_start = pair_bit * own_cols
    own_tokens = slot_tokens(span_order, own_slots)
    all_tokens = slot_tokens(span_order, jnp.arange(all_spans, dtype=jnp.int32))
    own_docs, own_pos = token_layout(lengths, own_tokens, micro_tokens)
    all_docs, unused_pos = token_layout(lengths, all_tokens, micro_tokens)
    cos_table, sin_table = rope_tables(own_pos, head_size)
    input_rows = layer_in.astype(jnp.float32)
    inverse_one = inverse_rms(input_rows)
    normal_one = input_rows * inverse_one
    normed = (normal_one * gain_attn).astype(jnp.bfloat16)
    query_local = full_query.shape[1] // head_size
    kv_local = key_weight.shape[1] // head_size
    group_size = query_local // kv_local
    query_proj = plain_dot(normed, full_query).reshape(local_rows, kv_local, group_size, head_size)
    key_proj = plain_dot(normed, key_weight).reshape(local_rows, kv_local, head_size)
    value_bf = plain_dot(normed, value_weight).astype(jnp.bfloat16)
    query_inv = inverse_rms(query_proj)
    query_hat = query_proj * query_inv
    cos_four = cos_table[:, None, None, :]
    sin_four = sin_table[:, None, None, :]
    cos_three = cos_table[:, None, :]
    sin_three = sin_table[:, None, :]
    query_bf = rotate(query_hat * gain_query, cos_four, sin_four).astype(jnp.bfloat16)
    key_inv = inverse_rms(key_proj)
    key_hat = key_proj * key_inv
    key_bf = (
        rotate(key_hat * gain_key, cos_three, sin_three)
        .astype(jnp.bfloat16)
        .reshape(local_rows, kv_local * head_size)
    )
    all_keys, all_values = (
        lax.all_gather(key_bf, "span", axis=0, tiled=True),
        lax.all_gather(value_bf, "span", axis=0, tiled=True),
    )
    score_scale = head_size ** (-0.5)
    block_rows = min(block_limit, total_rows)
    block_count = total_rows // block_rows
    block_steps = jnp.arange(block_count, dtype=jnp.int32)

    def block_scores(block_index):
        block_start = block_index * block_rows
        key_part = lax.dynamic_slice_in_dim(all_keys, block_start, block_rows, 0).reshape(
            block_rows, kv_local, head_size
        )
        doc_part = lax.dynamic_slice_in_dim(all_docs, block_start, block_rows, 0)
        token_part = lax.dynamic_slice_in_dim(all_tokens, block_start, block_rows, 0)
        raw_scores = (
            jnp.einsum("tkgd,skd->kgts", query_bf, key_part, preferred_element_type=jnp.float32)
            * score_scale
        )
        allowed = (own_docs[:, None] == doc_part[None, :]) & (
            own_tokens[:, None] >= token_part[None, :]
        )
        return (jnp.where(allowed[None, None], raw_scores, neg_large), key_part)

    def value_block(block_index):
        block_start = block_index * block_rows
        return lax.dynamic_slice_in_dim(all_values, block_start, block_rows, 0).reshape(
            block_rows, kv_local, head_size
        )

    def stats_step(block_state, block_index):
        run_max, run_sum = block_state
        scores, unused_keys = block_scores(block_index)
        new_max = jnp.maximum(run_max, jnp.max(scores, axis=-1))
        run_sum = run_sum * jnp.exp(run_max - new_max) + jnp.sum(
            jnp.exp(scores - new_max[..., None]), axis=-1
        )
        return ((new_max, run_sum), None)

    stat_shape = (kv_local, group_size, local_rows)
    (run_max, run_sum), unused_stats = lax.scan(
        stats_step,
        (jnp.full(stat_shape, neg_large, jnp.float32), jnp.zeros(stat_shape, jnp.float32)),
        block_steps,
    )
    log_total = run_max + jnp.log(run_sum)

    def soft_weights(block_index):
        scores, key_part = block_scores(block_index)
        return (jnp.exp(scores - log_total[..., None]), key_part)

    def output_step(accumulated, block_index):
        weights, unused_keys = soft_weights(block_index)
        accumulated = accumulated + jnp.einsum(
            "kgts,skd->tkgd",
            weights.astype(jnp.bfloat16),
            value_block(block_index),
            preferred_element_type=jnp.float32,
        )
        return (accumulated, None)

    attended_full, unused_out = lax.scan(
        output_step,
        jnp.zeros((local_rows, kv_local, group_size, head_size), jnp.float32),
        block_steps,
    )
    attended_bf = attended_full.reshape(local_rows, query_local * head_size).astype(jnp.bfloat16)
    hidden_rows = input_rows + lax.psum(
        plain_dot(attended_bf, full_out).astype(jnp.bfloat16), "tensor"
    ).astype(jnp.float32)
    inverse_two = inverse_rms(hidden_rows)
    normal_two = hidden_rows * inverse_two
    normed_mlp = (normal_two * gain_mlp).astype(jnp.bfloat16)
    gate_proj = plain_dot(normed_mlp, full_gate)
    up_proj = plain_dot(normed_mlp, full_up)
    sigmoid_gate = jax.nn.sigmoid(gate_proj)
    silu_gate = gate_proj * sigmoid_gate
    activated = (silu_gate * up_proj).astype(jnp.bfloat16)
    branch_share = lax.psum_scatter(
        plain_dot(activated, full_down).astype(jnp.bfloat16),
        "tensor",
        scatter_dimension=1,
        tiled=True,
    ).astype(jnp.float32)
    layer_out = (
        lax.dynamic_slice_in_dim(hidden_rows, tensor_place * slice_width, slice_width, 1)
        + branch_share
    )
    grad_down = left_dot(activated, out_grad)
    grad_act = right_dot(out_grad, full_down)
    grad_gate_bf = (
        grad_act * up_proj * sigmoid_gate * (1.0 + gate_proj * (1.0 - sigmoid_gate))
    ).astype(jnp.bfloat16)
    grad_up_bf = (grad_act * silu_gate).astype(jnp.bfloat16)
    grad_gate = left_dot(normed_mlp, grad_gate_bf)
    grad_up = left_dot(normed_mlp, grad_up_bf)
    mlp_part = right_dot(grad_gate_bf, full_gate) + right_dot(grad_up_bf, full_up)
    grad_normed_mlp = lax.psum(mlp_part.astype(jnp.bfloat16), "tensor").astype(jnp.float32)
    grad_gain_mlp = jnp.sum(grad_normed_mlp * normal_two, axis=0)
    grad_hidden = out_grad.astype(jnp.float32) + norm_back(
        grad_normed_mlp * gain_mlp, normal_two, inverse_two
    )
    branch_bf = grad_hidden.astype(jnp.bfloat16)
    grad_out = left_dot(attended_bf, branch_bf)
    grad_attended = (
        right_dot(branch_bf, full_out)
        .astype(jnp.bfloat16)
        .reshape(local_rows, kv_local, group_size, head_size)
    )
    row_delta = jnp.einsum("tkgd,tkgd->kgt", grad_attended.astype(jnp.float32), attended_full)

    def grad_step(query_acc, block_index):
        weights, key_part = soft_weights(block_index)
        value_part = value_block(block_index)
        grad_weights = jnp.einsum(
            "tkgd,skd->kgts", grad_attended, value_part, preferred_element_type=jnp.float32
        )
        grad_scores = (weights * (grad_weights - row_delta[..., None])).astype(jnp.bfloat16)
        query_acc = query_acc + jnp.einsum(
            "kgts,skd->tkgd", grad_scores, key_part, preferred_element_type=jnp.float32
        )
        key_piece = jnp.einsum(
            "kgts,tkgd->skd", grad_scores, query_bf, preferred_element_type=jnp.float32
        )
        value_piece = jnp.einsum(
            "kgts,tkgd->skd",
            weights.astype(jnp.bfloat16),
            grad_attended,
            preferred_element_type=jnp.float32,
        )
        return (query_acc, (key_piece, value_piece))

    query_acc, (key_pieces, value_pieces) = lax.scan(
        grad_step,
        jnp.zeros((local_rows, kv_local, group_size, head_size), jnp.float32),
        block_steps,
    )
    keys_grad_all = key_pieces.reshape(total_rows, kv_local * head_size) * score_scale
    values_grad_all = value_pieces.reshape(total_rows, kv_local * head_size)
    key_rot_grad, value_rows_grad = (
        lax.psum_scatter(
            keys_grad_all.astype(jnp.bfloat16), "span", scatter_dimension=0, tiled=True
        ).astype(jnp.float32),
        lax.psum_scatter(
            values_grad_all.astype(jnp.bfloat16), "span", scatter_dimension=0, tiled=True
        ).astype(jnp.float32),
    )
    partner_key, partner_value = (
        from_partner(key_rot_grad.astype(jnp.bfloat16), "tensor", 0).astype(key_rot_grad.dtype),
        from_partner(value_rows_grad.astype(jnp.bfloat16), "tensor", 0).astype(
            value_rows_grad.dtype
        ),
    )
    key_rot_grad = key_rot_grad + partner_key
    value_rows_grad = value_rows_grad + partner_value
    query_norm_grad = rotate_back(query_acc * score_scale, cos_four, sin_four)
    gain_query_part = jnp.sum(query_norm_grad * query_hat, axis=(0, 1, 2))
    query_grad_bf = (
        norm_back(query_norm_grad * gain_query, query_hat, query_inv)
        .astype(jnp.bfloat16)
        .reshape(local_rows, query_local * head_size)
    )
    key_norm_grad = rotate_back(
        key_rot_grad.reshape(local_rows, kv_local, head_size), cos_three, sin_three
    )
    gain_key_part = jnp.sum(key_norm_grad * key_hat, axis=(0, 1)) * key_share
    key_grad_bf = (
        norm_back(key_norm_grad * gain_key, key_hat, key_inv)
        .astype(jnp.bfloat16)
        .reshape(local_rows, kv_local * head_size)
    )
    value_grad_bf = value_rows_grad.astype(jnp.bfloat16)
    key_own_grad = lax.dynamic_slice_in_dim(key_grad_bf, col_start, own_cols, 1)
    value_own_grad = lax.dynamic_slice_in_dim(value_grad_bf, col_start, own_cols, 1)
    grad_query = left_dot(normed, query_grad_bf)
    grad_key = left_dot(normed, key_own_grad)
    grad_value = left_dot(normed, value_own_grad)
    normed_part = (
        right_dot(query_grad_bf, full_query)
        + right_dot(key_own_grad, own_key)
        + right_dot(value_own_grad, own_value)
    )
    grad_normed, grad_gain_query, grad_gain_key = (
        lax.psum(normed_part.astype(jnp.bfloat16), "tensor").astype(jnp.float32),
        lax.psum(gain_query_part.astype(jnp.bfloat16), "tensor").astype(jnp.float32),
        lax.psum(gain_key_part.astype(jnp.bfloat16), "tensor").astype(jnp.float32),
    )
    grad_gain_attn = jnp.sum(grad_normed * normal_one, axis=0)
    grad_input = grad_hidden + norm_back(grad_normed * gain_attn, normal_one, inverse_one)
    grad_slice = lax.dynamic_slice_in_dim(grad_input, tensor_place * slice_width, slice_width, 1)
    outgoing = (
        jnp.zeros((all_spans, SPAN, slice_width), jnp.float32)
        .at[own_spans]
        .set(grad_slice.reshape(per_device, SPAN, slice_width))
    )
    incoming = lax.all_to_all(
        outgoing.astype(jnp.bfloat16), "span", split_axis=0, concat_axis=0, tiled=True
    ).astype(outgoing.dtype)
    in_grad = jnp.sum(incoming.reshape(span_count, per_device, SPAN, slice_width), axis=0).reshape(
        local_rows, slice_width
    )
    (
        grad_query,
        grad_key,
        grad_value,
        grad_out,
        grad_gate,
        grad_up,
        grad_down,
        grad_gain_attn,
        grad_gain_mlp,
        grad_gain_query,
        grad_gain_key,
    ) = (
        lax.psum_scatter(
            grad_query.astype(jnp.bfloat16), "span", scatter_dimension=0, tiled=True
        ).astype(jnp.float32),
        lax.psum_scatter(
            grad_key.astype(jnp.bfloat16), "span", scatter_dimension=0, tiled=True
        ).astype(jnp.float32),
        lax.psum_scatter(
            grad_value.astype(jnp.bfloat16), "span", scatter_dimension=0, tiled=True
        ).astype(jnp.float32),
        lax.psum_scatter(
            grad_out.astype(jnp.bfloat16), "span", scatter_dimension=1, tiled=True
        ).astype(jnp.float32),
        lax.psum_scatter(
            grad_gate.astype(jnp.bfloat16), "span", scatter_dimension=0, tiled=True
        ).astype(jnp.float32),
        lax.psum_scatter(
            grad_up.astype(jnp.bfloat16), "span", scatter_dimension=0, tiled=True
        ).astype(jnp.float32),
        lax.psum_scatter(
            grad_down.astype(jnp.bfloat16), "span", scatter_dimension=1, tiled=True
        ).astype(jnp.float32),
        lax.psum_scatter(
            grad_gain_attn.astype(jnp.bfloat16), "span", scatter_dimension=0, tiled=True
        ).astype(jnp.float32),
        lax.psum_scatter(
            grad_gain_mlp.astype(jnp.bfloat16), "span", scatter_dimension=0, tiled=True
        ).astype(jnp.float32),
        lax.psum_scatter(
            grad_gain_query.astype(jnp.bfloat16), "span", scatter_dimension=0, tiled=True
        ).astype(jnp.float32),
        lax.psum_scatter(
            grad_gain_key.astype(jnp.bfloat16), "span", scatter_dimension=0, tiled=True
        ).astype(jnp.float32),
    )
    return (
        layer_out,
        in_grad,
        grad_query,
        grad_key,
        grad_value,
        grad_out,
        grad_gate,
        grad_up,
        grad_down,
        grad_gain_attn,
        grad_gain_mlp,
        grad_gain_query,
        grad_gain_key,
    )


def solution(mesh):
    return jax.shard_map(
        body,
        mesh=mesh,
        in_specs=(
            P("span", None),
            P("span", None),
            P(),
            P(),
            P("span", "tensor"),
            P("span", "tensor"),
            P("span", "tensor"),
            P("tensor", "span"),
            P("span", "tensor"),
            P("span", "tensor"),
            P("tensor", "span"),
            P("span"),
            P("span"),
            P("span"),
            P("span"),
        ),
        out_specs=(
            P("span", "tensor"),
            P("span", "tensor"),
            P("span", "tensor"),
            P("span", "tensor"),
            P("span", "tensor"),
            P("tensor", "span"),
            P("span", "tensor"),
            P("span", "tensor"),
            P("tensor", "span"),
            P("span"),
            P("span"),
            P("span"),
            P("span"),
        ),
        check_vma=False,
    )
```

profile of v0, /device:TPU:1, one launch (start us, length us, event | category | flops | bytes accessed | tf_op | source)
XLA Modules:
  0.0 1805.7 jit_solution(2579706219049325185)
XLA Ops:
  8.0 26.0 %all_gather.44 = bf16[2048,64]{0,1:T(8,128)(2,1)S(1)} all-gather(bf16[256,64]{0,1:T(8,128)(2,1)S(1)} %copy-done.43), channel_id=1, replica_groups=mesh['span'=8,'tensor'=16] {'span'}, dimensions={0}, use_global_device_ids=true | all-gather | bytes 294912 | tf_op jit(solution)/shard_map/all_gather | solution.py:142
  34.0 5.7 collective-permute-start
  39.8 25.7 %all_gather.46 = bf16[2048,64]{0,1:T(8,128)(2,1)S(1)} all-gather(bf16[256,64]{0,1:T(8,128)(2,1)S(1)} %copy-done.44), channel_id=1, replica_groups=mesh['span'=8,'tensor'=16] {'span'}, dimensions={0}, use_global_device_ids=true | all-gather | bytes 294912 | tf_op jit(solution)/shard_map/all_gather | solution.py:141
  68.8 16.7 all-gather
  94.8 14.3 all-reduce.8
  110.9 234.2 %all-gather.9.cloned.1.call-done = bf16[8192,2048]{1,0:T(8,128)(2,1)} async-done(((bf16[1024,2048]{1,0:T(8,128)(2,1)}), bf16[8192,2048]{1,0:T(8,128)(2,1)}) %all-gather.9.cloned.1.call-update) | async-done | bytes 33554448 | tf_op jit(solution)/shard_map/all_gather | solution.py:124
  345.1 5.0 gather_fusion
  350.1 3.6 multiply_reduce_fusion.2
  360.3 27.8 %gather_fusion.2 = s32[8192,3]{1,0:T(8,128)} fusion(s32[2,3]{1,0:T(2,128)S(1)} %reduce_window_sum.12, s32[8192]{0:T(1024)S(1)} %broadcast_clamp_fusion), kind=kCustom, calls=%fused_computation.5 | custom fusion | bytes 229376 | tf_op jit(solution)/shard_map/jit(_take)/gather | solution.py:73
  388.3 7.0 convert_reduce_fusion.1
  395.4 24.9 %all_gather.51 = bf16[128,2048]{1,0:T(8,128)(2,1)} all-gather(bf16[128,256]{1,0:T(8,128)(2,1)S(1)} %copy-done.39), channel_id=1, replica_groups=mesh['span'=8,'tensor'=16] {'span'}, dimensions={1}, use_global_device_ids=true | all-gather | bytes 589824 | tf_op jit(solution)/shard_map/all_gather | solution.py:143
  420.3 23.4 %all_gather.49 = bf16[2048,128]{1,0:T(8,128)(2,1)S(1)} all-gather(bf16[256,128]{1,0:T(8,128)(2,1)S(1)} %copy-done.40), channel_id=1, replica_groups=mesh['span'=8,'tensor'=16] {'span'}, dimensions={0}, use_global_device_ids=true | all-gather | bytes 589824 | tf_op jit(solution)/shard_map/all_gather | solution.py:140
  446.7 4.2 convolution_convert_fusion.9
  454.3 56.7 %while.39 = (s32[]{:T(128)}, f32[1,1,1024]{2,1,0:T(1,128)S(1)}, f32[1,1,1024]{2,1,0:T(1,128)S(1)}, s32[1024]{0:T(1024)S(1)}, s32[8]{0:T(128)S(1)}, /*index=5*/s3...) while((s32[]{:T(128)}, f32[1,1,1024]{2,1,0:T(1,128)S(1)}, ...), condition=%wide.region_10.13_spmd.clone, body=%wide.region_7.12_spmd.clone.sunk | while | flops 282073088 | bytes 9019646 | solution.py:244
  511.1 33.4 %while.40 = (s32[]{:T(128)}, f32[1024,1,1,128]{0,3,2,1:T(8,128)S(1)}, s32[8]{0:T(128)S(1)}, bf16[8192,128]{1,0:T(8,128)(2,1)}, s32[1024]{0:T(1024)S(1)}, /*index...) while((s32[]{:T(128)}, ...), condition=%wide.region_12.15_spmd.clone, body=%wide.region_11.14_spmd.clone.sunk | while | flops 544474112 | bytes 1877760 | solution.py:265
  544.6 4.7 fusion.163
  551.3 13.1 all-gather.1
  564.4 145.6 %all-reduce.13.cloned.1.call-done = bf16[1024,2048]{1,0:T(8,128)(2,1)} async-done(((bf16[1024,2048]{1,0:T(8,128)(2,1)}), bf16[1024,2048]{1,0:T(8,128)(2,1)}) %all-reduce.13.cloned.1.call-update) | async-done | bytes 4194320 | tf_op jit(solution)/shard_map/psum | solution.py:271
  709.9 5.0 multiply_reduce_fusion.1
  715.9 3.9 multiply_convert_fusion
  719.8 27.7 %all-gather.15.cloned.1.call-done = bf16[2048,384]{1,0:T(8,128)(2,1)} async-done(((bf16[256,384]{1,0:T(8,128)(2,1)}), bf16[2048,384]{1,0:T(8,128)(2,1)}) %all-gather.15.cloned.1.call-update) | async-done | bytes 1572880 | tf_op jit(solution)/shard_map/all_gather | solution.py:144
  747.4 6.1 fusion.167
  753.6 35.3 %all-gather.17.cloned.1.call-done = bf16[2048,384]{1,0:T(8,128)(2,1)} async-done(((bf16[256,384]{1,0:T(8,128)(2,1)}), bf16[2048,384]{1,0:T(8,128)(2,1)}) %all-gather.17.cloned.1.call-update) | async-done | bytes 1572880 | tf_op jit(solution)/shard_map/all_gather | solution.py:145
  788.8 6.2 fusion.168
  795.1 38.2 %all-gather.19.cloned.1.call-done = bf16[384,2048]{1,0:T(8,128)(2,1)} async-done(((bf16[384,256]{1,0:T(8,128)(2,1)}), bf16[384,2048]{1,0:T(8,128)(2,1)}) %all-gather.19.cloned.1.call-update) | async-done | bytes 1572880 | tf_op jit(solution)/shard_map/all_gather | solution.py:146
  833.3 7.3 multiply_convert_fusion.3
  843.0 4.4 add_convert_fusion.1
  847.7 154.6 %all-reduce.15.cloned.1.call-done = bf16[1024,2048]{1,0:T(8,128)(2,1)} async-done(((bf16[1024,2048]{1,0:T(8,128)(2,1)}), bf16[1024,2048]{1,0:T(8,128)(2,1)}) %all-reduce.15.cloned.1.call-update) | async-done | bytes 4194320 | tf_op jit(solution)/shard_map/psum | solution.py:301
  1002.3 7.2 fusion.81
  1010.6 7.6 fusion.80
  1024.1 101.3 %while.41 = (s32[]{:T(128)}, f32[1024,1,1,128]{0,3,2,1:T(8,128)S(1)}, f32[8,1024,1,128]{3,1,2,0:T(8,128)}, bf16[8,1024,1,128]{3,1,2,0:T(8,128)(2,1)}, s32[8]{0:T...) while((s32[]{:T(128)}, ...), condition=%wide.region_19.22_spmd.clone, body=%wide.region_18.21_spmd.clone.sunk | while | flops 1359217664 | bytes 58524068 | solution.py:336
  1033.4 3.4 fusion.255
  1046.0 3.4 fusion.255
  1071.3 3.4 fusion.255
  1096.7 3.4 fusion.255
  1109.3 3.4 fusion.255
  1133.2 37.2 %reduce-scatter.13.cloned.1.call-done = bf16[1024,128]{0,1:T(8,128)(2,1)} async-done(((bf16[8192,128]{0,1:T(8,128)(2,1)}), bf16[1024,128]{0,1:T(8,128)(2,1)}) %reduce-scatter.13.cloned.1.call-update) | async-done | bytes 262160 | tf_op jit(solution)/shard_map/reduce_scatter | solution.py:344
  1170.4 5.8 collective-permute-start.2
  1176.2 4.6 fusion.170
  1180.8 33.2 %reduce-scatter.15.cloned.1.call-done = bf16[1024,128]{1,0:T(8,128)(2,1)} async-done(((bf16[8192,128]{1,0:T(8,128)(2,1)}), bf16[1024,128]{1,0:T(8,128)(2,1)}) %reduce-scatter.15.cloned.1.call-update) | async-done | bytes 262160 | tf_op jit(solution)/shard_map/reduce_scatter | solution.py:347
  1214.0 5.7 collective-permute-start.3
  1228.9 5.8 convolution_convert_fusion.4
  1234.8 5.9 convolution_convert_fusion.3
  1240.7 5.2 convolution_convert_fusion.2
  1246.3 4.3 convolution_convert_fusion.6
  1250.7 5.1 convolution_convert_fusion.5
  1255.9 5.5 convolution_convert_fusion
  1261.4 6.4 copy.62
  1267.8 108.1 %all-reduce.17.cloned.1.call-done = bf16[1024,2048]{1,0:T(8,128)(2,1)} async-done(((bf16[1024,2048]{1,0:T(8,128)(2,1)}), bf16[1024,2048]{1,0:T(8,128)(2,1)}) %all-reduce.17.cloned.1.call-update) | async-done | bytes 4194320 | tf_op jit(solution)/shard_map/psum | solution.py:387
  1375.9 5.7 fusion.82
  1388.1 3.9 convert_element_type.263
  1392.0 4.3 all-to-all-start
  1396.3 3.8 convolution_convert_fusion.7
  1400.2 3.9 convolution_convert_fusion.8
  1405.4 28.1 %reduce-scatter.25.cloned.1.call-done = bf16[256,384]{1,0:T(8,128)(2,1)} async-done(((bf16[2048,384]{1,0:T(8,128)(2,1)}), bf16[256,384]{1,0:T(8,128)(2,1)}) %reduce-scatter.25.cloned.1.call-update) | async-done | bytes 196624 | tf_op jit(solution)/shard_map/reduce_scatter | solution.py:430
  1435.1 39.9 %reduce-scatter.27.cloned.1.call-done = bf16[256,384]{1,0:T(8,128)(2,1)} async-done(((bf16[2048,384]{1,0:T(8,128)(2,1)}), bf16[256,384]{1,0:T(8,128)(2,1)}) %reduce-scatter.27.cloned.1.call-update) | async-done | bytes 196624 | tf_op jit(solution)/shard_map/reduce_scatter | solution.py:433
  1476.8 40.4 %reduce-scatter.29.cloned.1.call-done = bf16[384,256]{1,0:T(8,128)(2,1)} async-done(((bf16[384,2048]{1,0:T(8,128)(2,1)}), bf16[384,256]{1,0:T(8,128)(2,1)}) %reduce-scatter.29.cloned.1.call-update) | async-done | bytes 196624 | tf_op jit(solution)/shard_map/reduce_scatter | solution.py:436
  1518.8 37.6 %reduce-scatter.17.cloned.1.call-done = bf16[256,128]{1,0:T(8,128)(2,1)} async-done(((bf16[2048,128]{1,0:T(8,128)(2,1)}), bf16[256,128]{1,0:T(8,128)(2,1)}) %reduce-scatter.17.cloned.1.call-update) | async-done | bytes 65552 | tf_op jit(solution)/shard_map/reduce_scatter | solution.py:418
  1558.0 38.1 %reduce-scatter.23.cloned.1.call-done = bf16[128,256]{1,0:T(8,128)(2,1)} async-done(((bf16[128,2048]{1,0:T(8,128)(2,1)}), bf16[128,256]{1,0:T(8,128)(2,1)}) %reduce-scatter.23.cloned.1.call-update) | async-done | bytes 65552 | tf_op jit(solution)/shard_map/reduce_scatter | solution.py:427
  1597.5 85.2 %reduce-scatter.31.cloned.1.call-done = bf16[128,1024]{1,0:T(8,128)(2,1)} async-done(((bf16[2048,1024]{1,0:T(8,128)(2,1)}), bf16[128,1024]{1,0:T(8,128)(2,1)}) %reduce-scatter.31.cloned.1.call-update) | async-done | bytes 262160
  1685.8 31.7 %reduce-scatter.19.cloned.1.call-done = bf16[256,64]{0,1:T(8,128)(2,1)} async-done(((bf16[2048,64]{0,1:T(8,128)(2,1)}), bf16[256,64]{0,1:T(8,128)(2,1)}) %reduce-scatter.19.cloned.1.call-update) | async-done | bytes 32784 | tf_op jit(solution)/shard_map/reduce_scatter | solution.py:421
  1718.9 14.4 all-reduce.7
  1733.5 22.8 %reduce-scatter.21.cloned.1.call-done = bf16[256,64]{0,1:T(8,128)(2,1)} async-done(((bf16[2048,64]{0,1:T(8,128)(2,1)}), bf16[256,64]{0,1:T(8,128)(2,1)}) %reduce-scatter.21.cloned.1.call-update) | async-done | bytes 32784 | tf_op jit(solution)/shard_map/reduce_scatter | solution.py:424
  1757.7 38.2 %all-reduce.6 = (bf16[16]{0:T(256)(128)(2,1)S(1)}, bf16[16]{0:T(256)(128)(2,1)S(1)}) all-reduce(bf16[16]{0:T(256)(128)(2,1)S(1)} %dynamic-slice.9, bf16[16]{0:T(256)(128)(2,1)S(1)} %dynamic-slice.11), channel_id=1, replica_groups=mesh['span'=8,'tensor'=16] {'tensor'}, use_global_device_ids=true, to_apply=%region_40.43 | all-reduce | flops 32 | bytes 128 | tf_op jit(solution)/shard_map/psum | solution.py:388
  (496 shorter events, 238.2 us)
Async XLA Ops:
  7.2 78.6 %copy-start = (s32[64]{0:T(128)S(1)}, s32[64]{0:T(128)}, u32[]{:S(2)}) copy-start(s32[64]{0:T(128)} %param.28) | copy-start | bytes 772
  7.2 32.6 %copy-start.44 = (bf16[256,64]{0,1:T(8,128)(2,1)S(1)}, bf16[256,64]{0,1:T(8,128)(2,1)}, u32[]{:S(2)}) copy-start(bf16[256,64]{0,1:T(8,128)(2,1)} %param.30) | copy-start | bytes 98308
  7.2 61.6 %copy-start.49 = (bf16[256]{0:T(256)(128)(2,1)S(1)}, bf16[256]{0:T(256)(128)(2,1)}, u32[]{:S(2)}) copy-start(bf16[256]{0:T(256)(128)(2,1)} %param.36) | copy-start | bytes 1540
  7.2 78.3 %copy-start.2 = (s32[2,3]{1,0:T(2,128)S(1)}, s32[2,3]{1,0:T(2,128)}, u32[]{:S(2)}) copy-start(s32[2,3]{1,0:T(2,128)} %param.27) | copy-start | bytes 76
  7.2 337.9 %all-gather.9.cloned.1.call-start = ((), (), s32[]{:S(2)}) async-start(), calls=%async_computation.11 | async-start | bytes 37748736 | tf_op jit(solution)/shard_map/all_gather | solution.py:124
  8.0 443.1 %all-gather.13.cloned.1.call-start = ((), (), s32[]{:S(2)}) async-start(), calls=%async_computation.13 | async-start | bytes 2359296 | tf_op jit(solution)/shard_map/all_gather | solution.py:204
  34.0 412.7 %copy-start.26 = (bf16[2048,64]{0,1:T(8,128)(2,1)}, bf16[2048,64]{0,1:T(8,128)(2,1)S(1)}, u32[]{:S(2)}) copy-start(bf16[2048,64]{0,1:T(8,128)(2,1)S(1)} %all_gather.44) | copy-start | bytes 786436
  34.0 412.7 %collective-permute-start = (bf16[2048,64]{0,1:T(8,128)(2,1)S(1)}, bf16[2048,64]{0,1:T(8,128)(2,1)}, u32[]{:S(2)}, u32[]{:S(2)}) collective-permute-start(bf16[2048,64]{0,1:T(8,128)(2,1)S(1)} %all_gather.44), channel_id=1, source_target_pairs={{0,1},{1,0},{2,3},{3,2},{4,5},{5,4},{6,7},{7,6},{8,9},{9,8},{10,11... | collective-permute-start | bytes 786440 | tf_op jit(solution)/shard_map/ppermute | solution.py:23
  65.5 290.2 %copy-start.30 = (bf16[2048,64]{0,1:T(8,128)(2,1)}, bf16[2048,64]{0,1:T(8,128)(2,1)S(1)}, u32[]{:S(2)}) copy-start(bf16[2048,64]{0,1:T(8,128)(2,1)S(1)} %all_gather.46) | copy-start | bytes 786436
  65.5 290.2 %collective-permute-start.1 = (bf16[2048,64]{0,1:T(8,128)(2,1)S(1)}, bf16[2048,64]{0,1:T(8,128)(2,1)S(1)}, u32[]{:S(2)}, u32[]{:S(2)}) collective-permute-start(bf16[2048,64]{0,1:T(8,128)(2,1)S(1)} %all_gather.46), channel_id=1, source_target_pairs={{0,1},{1,0},{2,3},{3,2},{4,5},{5,4},{6,7},{7,6},{8,9},{9,8},{10,11... | collective-permute-start | bytes 786440 | tf_op jit(solution)/shard_map/ppermute | solution.py:23
  85.5 268.2 %copy-start.35 = (f32[8,1,256]{2,1,0:T(1,128)}, f32[8,1,256]{2,1,0:T(1,128)S(1)}, u32[]{:S(2)}) copy-start(f32[8,1,256]{2,1,0:T(1,128)S(1)} %convert_element_type.286) | copy-start | bytes 24580
  86.5 6.5 copy-start.47
  86.5 7.7 copy-start.50
  86.6 8.0 copy-start.51
  350.1 3.6 copy-start.3
  357.3 30.8 %copy-start.41 = (f32[1024]{0:T(1024)}, f32[1024]{0:T(1024)S(1)}, u32[]{:S(2)}) copy-start(f32[1024]{0:T(1024)S(1)} %add_rsqrt_fusion.2) | copy-start | bytes 12292
  360.0 151.1 %all-gather.11.cloned.1.call-start = ((), (), s32[]{:S(2)}) async-start(), calls=%async_computation.12 | async-start | bytes 2359296 | tf_op jit(solution)/shard_map/all_gather | solution.py:205
  388.0 7.3 copy-start.39
  388.0 32.2 %copy-start.40 = (bf16[256,128]{1,0:T(8,128)(2,1)S(1)}, bf16[256,128]{1,0:T(8,128)(2,1)}, u32[]{:S(2)}) copy-start(bf16[256,128]{1,0:T(8,128)(2,1)} %param.29) | copy-start | bytes 196612
  388.1 55.6 %copy-start.10 = (bf16[1024,2048]{1,0:T(8,128)(2,1)S(1)}, bf16[1024,2048]{1,0:T(8,128)(2,1)}, u32[]{:S(2)}) copy-start(bf16[1024,2048]{1,0:T(8,128)(2,1)} %copy-done.9) | copy-start | bytes 12582916
  451.0 258.9 %all-reduce.13.cloned.1.call-start = ((), (), s32[]{:S(2)}) async-start(), calls=%async_computation.14 | async-start | bytes 8388608 | tf_op jit(solution)/shard_map/psum | solution.py:271
  544.6 4.7 copy-start.14
  544.6 4.7 copy-start.15
  549.3 198.1 %all-gather.15.cloned.1.call-start = ((), (), s32[]{:S(2)}) async-start(), calls=%async_computation.15 | async-start | bytes 1769472 | tf_op jit(solution)/shard_map/all_gather | solution.py:144
  549.9 238.9 %all-gather.17.cloned.1.call-start = ((), (), s32[]{:S(2)}) async-start(), calls=%async_computation.16 | async-start | bytes 1769472 | tf_op jit(solution)/shard_map/all_gather | solution.py:145
  550.5 282.8 %all-gather.19.cloned.1.call-start = ((), (), s32[]{:S(2)}) async-start(), calls=%async_computation.17 | async-start | bytes 1769472 | tf_op jit(solution)/shard_map/all_gather | solution.py:146
  551.2 451.1 %all-reduce.15.cloned.1.call-start = ((), (), s32[]{:S(2)}) async-start(), calls=%async_computation.18 | async-start | bytes 8388608 | tf_op jit(solution)/shard_map/psum | solution.py:301
  709.9 5.1 copy-start.4
  709.9 5.9 copy-start.11
  795.1 45.6 %copy-start.21 = (bf16[2048,384]{1,0:T(8,128)(2,1)S(1)}, bf16[2048,384]{1,0:T(8,128)(2,1)}, u32[]{:S(2)}) copy-start(bf16[2048,384]{1,0:T(8,128)(2,1)} %all-gather.15.cloned.1.call-done) | copy-start | bytes 4718596
  847.5 322.9 %reduce-scatter.13.cloned.1.call-start = ((), (), s32[]{:S(2)}) async-start(), calls=%async_computation.19 | async-start | bytes 2359296 | tf_op jit(solution)/shard_map/reduce_scatter | solution.py:344
  1002.3 7.2 copy-start.5
  1002.3 7.2 copy-start.12
  1002.3 8.3 copy-start.13
  1033.4 3.4 copy-start.29
  1046.0 3.4 copy-start.29
  1071.3 3.4 copy-start.29
  1096.7 3.4 copy-start.29
  1130.9 45.3 %copy-start.19 = (bf16[2048,128]{1,0:T(8,128)(2,1)S(1)}, bf16[2048,128]{1,0:T(8,128)(2,1)}, u32[]{:S(2)}) copy-start(bf16[2048,128]{1,0:T(8,128)(2,1)} %copy-done.18) | copy-start | bytes 1572868
  1131.0 83.0 %reduce-scatter.15.cloned.1.call-start = ((), (), s32[]{:S(2)}) async-start(), calls=%async_computation.20 | async-start | bytes 2359296 | tf_op jit(solution)/shard_map/reduce_scatter | solution.py:347
  1131.5 244.4 %all-reduce.17.cloned.1.call-start = ((), (), s32[]{:S(2)}) async-start(), calls=%async_computation.21 | async-start | bytes 8388608 | tf_op jit(solution)/shard_map/psum | solution.py:387
  1133.1 87.8 %copy-start.20 = (f32[1024,128]{0,1:T(8,128)S(1)}, f32[1024,128]{0,1:T(8,128)}, u32[]{:S(2)}) copy-start(f32[1024,128]{0,1:T(8,128)} %get-tuple-element.570) | copy-start | bytes 1572868
  1133.1 87.9 %copy-start.42 = (f32[1024]{0:T(1024)S(1)}, f32[1024]{0:T(1024)}, u32[]{:S(2)}) copy-start(f32[1024]{0:T(1024)} %copy-done.41) | copy-start | bytes 12292
  1170.4 49.3 %copy-start.34 = (bf16[1024,128]{0,1:T(8,128)(2,1)S(1)}, bf16[1024,128]{0,1:T(8,128)(2,1)}, u32[]{:S(2)}) copy-start(bf16[1024,128]{0,1:T(8,128)(2,1)} %reduce-scatter.13.cloned.1.call-done) | copy-start | bytes 786436
  1170.4 49.3 %collective-permute-start.2 = (bf16[1024,128]{0,1:T(8,128)(2,1)}, bf16[1024,128]{0,1:T(8,128)(2,1)S(1)}, u32[]{:S(2)}, u32[]{:S(2)}) collective-permute-start(bf16[1024,128]{0,1:T(8,128)(2,1)} %reduce-scatter.13.cloned.1.call-done), channel_id=1, source_target_pairs={{0,1},{1,0},{2,3},{3,2},{4,5},{5,4},{6,7},{7,6},{8,9},{9,8},{10,11... | collective-permute-start | bytes 786440 | tf_op jit(solution)/shard_map/ppermute | solution.py:23
  1180.8 40.4 %copy-start.31 = (bf16[2048,64]{0,1:T(8,128)(2,1)S(1)}, bf16[2048,64]{0,1:T(8,128)(2,1)}, u32[]{:S(2)}) copy-start(bf16[2048,64]{0,1:T(8,128)(2,1)} %copy-done.30) | copy-start | bytes 786436
  1214.0 8.5 collective-permute-start.3
  1227.8 7.0 copy-start.33
  1227.8 205.6 %reduce-scatter.25.cloned.1.call-start = ((), (), s32[]{:S(2)}) async-start(), calls=%async_computation.26 | async-start | bytes 1769472 | tf_op jit(solution)/shard_map/reduce_scatter | solution.py:430
  1234.7 6.0 copy-start.53
  1234.7 240.3 %reduce-scatter.27.cloned.1.call-start = ((), (), s32[]{:S(2)}) async-start(), calls=%async_computation.27 | async-start | bytes 1769472 | tf_op jit(solution)/shard_map/reduce_scatter | solution.py:433
  1240.7 276.5 %reduce-scatter.29.cloned.1.call-start = ((), (), s32[]{:S(2)}) async-start(), calls=%async_computation.28 | async-start | bytes 1769472 | tf_op jit(solution)/shard_map/reduce_scatter | solution.py:436
  1245.9 4.7 copy-start.17
  1246.0 310.5 %reduce-scatter.17.cloned.1.call-start = ((), (), s32[]{:S(2)}) async-start(), calls=%async_computation.22 | async-start | bytes 589824 | tf_op jit(solution)/shard_map/reduce_scatter | solution.py:418
  1250.6 5.3 copy-start.48
  1250.6 345.4 %reduce-scatter.23.cloned.1.call-start = ((), (), s32[]{:S(2)}) async-start(), calls=%async_computation.25 | async-start | bytes 589824 | tf_op jit(solution)/shard_map/reduce_scatter | solution.py:427
  1255.8 427.0 %reduce-scatter.31.cloned.1.call-start = ((), (), s32[]{:S(2)}) async-start(), calls=%async_computation.29 | async-start | bytes 4456448
  1267.8 108.1 %copy-start.36 = (f32[8,1,256]{2,1,0:T(1,128)S(1)}, f32[8,1,256]{2,1,0:T(1,128)}, u32[]{:S(2)}) copy-start(f32[8,1,256]{2,1,0:T(1,128)} %copy-done.35) | copy-start | bytes 24580
  1267.8 108.1 %copy-start.38 = (f32[1024]{0:T(1024)S(1)}, f32[1024]{0:T(1024)}, u32[]{:S(2)}) copy-start(f32[1024]{0:T(1024)} %copy-done.37) | copy-start | bytes 12292
  1381.7 3.9 copy-start.46
  1392.0 405.6 %all-to-all-start = ((bf16[64,128,128]{2,1,0:T(8,128)(2,1)}), bf16[64,128,128]{2,1,0:T(8,128)(2,1)S(1)}, u32[]{:S(2)}, u32[]{:S(2)}) async-start(bf16[64,128,128]{2,1,0:T(8,128)(2,1)} %convert_element_type.263), calls=%async_computation.2 | async-start | bytes 4194304 | tf_op jit(solution)/shard_map/all_to_all | solution.py:399
  1396.3 321.3 %reduce-scatter.19.cloned.1.call-start = ((), (), s32[]{:S(2)}) async-start(), calls=%async_computation.23 | async-start | bytes 294912 | tf_op jit(solution)/shard_map/reduce_scatter | solution.py:421
  1400.1 356.2 %reduce-scatter.21.cloned.1.call-start = ((), (), s32[]{:S(2)}) async-start(), calls=%async_computation.24 | async-start | bytes 294912 | tf_op jit(solution)/shard_map/reduce_scatter | solution.py:424
  1400.2 398.6 %copy-start.1 = (s32[64]{0:T(128)S(1)}, s32[64]{0:T(128)}, u32[]{:S(2)}) copy-start(s32[64]{0:T(128)} %param.28) | copy-start | bytes 772
  (44 other events, 125.0 us)
Sparse Core Ops, SparseCore 0:
  9.7 335.3 all-gather.8
  360.1 34.9 all-gather.12
  451.1 47.1 all-gather.10
  549.4 160.4 all-reduce.12
  711.4 35.9 all-gather.14
  748.9 39.8 all-gather.16
  790.4 42.8 all-gather.18
  847.6 154.6 all-reduce.14
  1131.1 39.2 reduce-scatter.12
  1172.6 41.3 reduce-scatter.14
  1227.9 147.9 all-reduce.16
  1378.2 55.2 reduce-scatter.24
  1435.9 39.1 reduce-scatter.26
  1477.3 39.7 reduce-scatter.28
  1519.9 36.4 reduce-scatter.16
  1559.4 36.6 reduce-scatter.22
  1599.9 82.8 reduce-scatter.30
  1685.1 32.3 reduce-scatter.18
  1719.9 36.3 reduce-scatter.20
where the time goes:
time: 1820 us; the launch traced here: 1810 us
  waiting for transfers between devices  1140 us (63%)
  matrix products  223 us (12%)
  blocking collectives  197 us (11%)
  other arithmetic  101 us (6%)
  local copies, waits for them, and re-layouts  83.4 us (5%)
  starting transfers between devices  26.1 us (1%)
    all_gather x1, waiting for transfers between devices, body(): gathered = lax.all_gather(inputs, 'span', axis=0, tiled=True)  234 us
    psum x1, waiting for transfers between devices, body(): lax.psum(mlp_part.astype(jnp.bfloat16), 'tensor').astype(jnp.float32)  155 us
    psum x1, waiting for transfers between devices, body(): lax.psum(plain_dot(attended_bf, full_out).astype(jnp.bfloat16), 'tensor')  146 us
    psum x1, waiting for transfers between devices, body(): lax.psum(normed_part.astype(jnp.bfloat16), 'tensor').astype(jnp.float32)  108 us
    unnamed x20, waiting for transfers between devices  88.4 us
    reduce_scatter x1, waiting for transfers between devices, body(): lax.psum_scatter(grad_down.astype(jnp.bfloat16), 'span', scatter_dimensio...  40.4 us
    reduce_scatter x1, waiting for transfers between devices, body(): lax.psum_scatter(grad_up.astype(jnp.bfloat16), 'span', scatter_dimension=...  39.9 us
    psum x1, blocking collectives, body(): lax.psum(gain_query_part.astype(jnp.bfloat16), 'tensor').astype(jnp.float32)  38.2 us
  transfers between devices with their start and end apart: 24, of which 17 were waited for; matrix products, arithmetic and copies ran while one was open for 13% of the time, Pallas kernels for 0%

commit v1 on v0

v1 whole, which is shorter than its diff:
```python
import jax
import jax.numpy as jnp
from jax import lax
from jax.experimental import pallas as pl
from jax.experimental.pallas import tpu as pltpu
from jax.sharding import Mesh, PartitionSpec as P

SPAN = 128
MICRO = 2
HD = 128
D = 2048
ROWS = 1024
KEYS = 4096
BLK = 256

epsilon = 1e-06
rope_base = 1000000.0
score_scale = HD ** (-0.5)
log2e = 1.4426950408889634
bf16 = jnp.bfloat16
f32 = jnp.float32
SPANS = ("xl", "z")
TENSOR = ("xh", "y", "c")
CHIPS = ("xh", "y")
VMEM_LIMIT = 48 * 1024 * 1024


def swap(block):
    return lax.ppermute(block, "c", [(0, 1), (1, 0)])


def cross(block):
    return lax.ppermute(block, "xh", [(0, 1), (1, 0)])


def shift(block, axis, by):
    return lax.ppermute(block, axis, [(i, (i + by) % 4) for i in range(4)])


def onward(block, by):
    return lax.ppermute(block, "z", [(i, i + by) for i in range(4) if i + by < 4])


def backward(block, by):
    return lax.ppermute(block, "z", [(i, i - by) for i in range(4) if i - by >= 0])


def exchange(block, axes):
    return lax.all_to_all(block, axes, 0, 0, tiled=True)


def spread(block, axes, count):
    return exchange(jnp.broadcast_to(block[None], (count,) + block.shape), axes)


def plain_dot(first_op, second_op):
    return jnp.dot(first_op, second_op, preferred_element_type=f32)


def left_dot(first_op, second_op):
    return lax.dot_general(
        first_op, second_op, (((0,), (0,)), ((), ())), preferred_element_type=f32
    )


def right_dot(first_op, second_op):
    return lax.dot_general(
        first_op, second_op, (((1,), (1,)), ((), ())), preferred_element_type=f32
    )


def inverse_rms(values):
    return lax.rsqrt(jnp.mean(values * values, axis=-1, keepdims=True) + epsilon)


def rotate(values, cos_table, sin_table):
    former, latter = values[..., :64], values[..., 64:]
    return jnp.concatenate(
        [former * cos_table - latter * sin_table, latter * cos_table + former * sin_table], axis=-1
    )


def rotate_back(values, cos_table, sin_table):
    former, latter = values[..., :64], values[..., 64:]
    return jnp.concatenate(
        [former * cos_table + latter * sin_table, latter * cos_table - former * sin_table], axis=-1
    )


def norm_back(incoming, normal, inverse):
    return inverse * (incoming - normal * jnp.mean(incoming * normal, axis=-1, keepdims=True))


def block_mask(block, key_block, starts):
    key_at = key_block * BLK + lax.broadcasted_iota(jnp.int32, (BLK, BLK), 0)
    query_at = (KEYS - ROWS) + block * BLK + lax.broadcasted_iota(jnp.int32, (BLK, BLK), 1)
    return (key_at >= starts) & (key_at <= query_at)


def attend_kernel(low_ref, start_ref, q_ref, k_ref, v_ref, out_ref, full_ref, total_ref):
    for block in range(ROWS // BLK):
        cols = pl.ds(block * BLK, BLK)
        queries = q_ref[cols, :]
        starts = start_ref[:, cols]

        def step(key_block, state):
            acc, total = state
            rows = pl.ds(pl.multiple_of(key_block * BLK, BLK), BLK)
            scores = right_dot(k_ref[rows, :], queries) * (score_scale * log2e)
            weights = jnp.where(block_mask(block, key_block, starts), jnp.exp2(scores), 0.0)
            total = total + jnp.sum(weights, axis=0, keepdims=True)
            acc = acc + left_dot(v_ref[rows, :], weights.astype(bf16))
            return acc, total

        acc, total = lax.fori_loop(
            low_ref[block],
            (KEYS - ROWS) // BLK + block + 1,
            step,
            (jnp.zeros((HD, BLK), f32), jnp.zeros((1, BLK), f32)),
        )
        full = acc / total
        full_ref[:, cols] = full
        total_ref[:, cols] = jnp.log2(total)
        out_ref[cols, :] = full.T.astype(bf16)


def attend(low, starts, queries, keys, values):
    vmem = pl.BlockSpec(memory_space=pltpu.VMEM)
    return pl.pallas_call(
        attend_kernel,
        out_shape=(
            jax.ShapeDtypeStruct((ROWS, HD), bf16),
            jax.ShapeDtypeStruct((HD, ROWS), f32),
            jax.ShapeDtypeStruct((1, ROWS), f32),
        ),
        in_specs=[pl.BlockSpec(memory_space=pltpu.SMEM)] + [vmem] * 4,
        out_specs=(vmem,) * 3,
        compiler_params=pltpu.CompilerParams(vmem_limit_bytes=VMEM_LIMIT),
        cost_estimate=pl.CostEstimate(
            flops=4 * ROWS * 2048 * HD, bytes_accessed=4 << 20, transcendentals=ROWS * 2048
        ),
        name="attend",
    )(low, starts, queries, keys, values)


def attend_back_kernel(
    low_ref,
    core_ref,
    start_ref,
    q_ref,
    k_ref,
    v_ref,
    do_ref,
    full_ref,
    total_ref,
    dq_ref,
    keep_ref,
    send_ref,
    dk_ref,
    dv_ref,
):
    dk_ref[...] = jnp.zeros_like(dk_ref)
    dv_ref[...] = jnp.zeros_like(dv_ref)
    for block in range(ROWS // BLK):
        cols = pl.ds(block * BLK, BLK)
        queries = q_ref[cols, :]
        starts = start_ref[:, cols]
        incoming = do_ref[cols, :]
        total = total_ref[:, cols]
        delta = jnp.sum(incoming.astype(f32).T * full_ref[:, cols], axis=0, keepdims=True)

        def step(key_block, acc):
            rows = pl.ds(pl.multiple_of(key_block * BLK, BLK), BLK)
            keys = k_ref[rows, :]
            scores = right_dot(keys, queries) * (score_scale * log2e)
            weights = jnp.where(
                block_mask(block, key_block, starts), jnp.exp2(scores - total), 0.0
            )
            grads = right_dot(v_ref[rows, :], incoming)
            grads = (weights * (grads - delta)).astype(bf16)
            dv_ref[rows, :] += plain_dot(weights.astype(bf16), incoming)
            dk_ref[rows, :] += plain_dot(grads, queries)
            return acc + left_dot(keys, grads)

        acc = lax.fori_loop(
            low_ref[block],
            (KEYS - ROWS) // BLK + block + 1,
            step,
            jnp.zeros((HD, BLK), f32),
        )
        dq_ref[cols, :] = acc.T * score_scale

    @pl.when(core_ref[0] == 0)
    def _():
        keep_ref[...] = dk_ref[...] * score_scale
        send_ref[...] = dv_ref[...].astype(bf16)

    @pl.when(core_ref[0] == 1)
    def _():
        keep_ref[...] = dv_ref[...]
        send_ref[...] = (dk_ref[...] * score_scale).astype(bf16)


def attend_back(low, core, starts, queries, keys, values, incoming, full, total):
    vmem = pl.BlockSpec(memory_space=pltpu.VMEM)
    smem = pl.BlockSpec(memory_space=pltpu.SMEM)
    return pl.pallas_call(
        attend_back_kernel,
        out_shape=(
            jax.ShapeDtypeStruct((ROWS, HD), f32),
            jax.ShapeDtypeStruct((KEYS, HD), f32),
            jax.ShapeDtypeStruct((KEYS, HD), bf16),
        ),
        in_specs=[smem, smem] + [vmem] * 7,
        out_specs=(vmem,) * 3,
        scratch_shapes=[pltpu.VMEM((KEYS, HD), f32), pltpu.VMEM((KEYS, HD), f32)],
        compiler_params=pltpu.CompilerParams(vmem_limit_bytes=VMEM_LIMIT),
        cost_estimate=pl.CostEstimate(
            flops=10 * ROWS * 2048 * HD, bytes_accessed=8 << 20, transcendentals=ROWS * 2048
        ),
        name="attend_back",
    )(low, core, starts, queries, keys, values, incoming, full, total)


def pick_kernel(index_ref, source_ref, out_ref):
    out_ref[...] = source_ref[...].astype(out_ref.dtype)


def pick(index, source):
    count, (rows, width) = index.shape[0], source.shape[1:]
    return pl.pallas_call(
        pick_kernel,
        out_shape=jax.ShapeDtypeStruct((count, rows, width), f32),
        grid_spec=pltpu.PrefetchScalarGridSpec(
            num_scalar_prefetch=1,
            grid=(count,),
            in_specs=[pl.BlockSpec((1, rows, width), lambda i, index_ref: (index_ref[i], 0, 0))],
            out_specs=pl.BlockSpec((1, rows, width), lambda i, index_ref: (i, 0, 0)),
        ),
        name="pick",
    )(index, source)


def body(
    inputs,
    out_grad,
    lengths,
    span_order,
    w_query,
    w_key,
    w_value,
    w_out,
    w_gate,
    w_up,
    w_down,
    norm_attn,
    norm_mlp,
    norm_query,
    norm_key,
):
    xl, z, xh, y, core = (lax.axis_index(name) for name in ("xl", "z", "xh", "y", "c"))
    span_place = xl * 4 + z
    tensor_place = (xh * 4 + y) * 2 + core
    first = core == 0

    def own_rows(block):
        wide = block.reshape(8, 16, 8, D)
        return lax.dynamic_index_in_dim(wide, tensor_place, 1, keepdims=False).reshape(64, D)

    other_half = swap(jnp.where(first, w_value, w_key))
    own_half = jnp.where(first, w_key, w_value)
    kv_shard = jnp.where(
        first,
        jnp.concatenate([own_half, other_half], 1),
        jnp.concatenate([other_half, own_half], 1),
    )
    gains = jnp.concatenate([norm_attn, norm_mlp, norm_query, norm_key])
    gains = jnp.pad(gains, (0, 16 * 384 - 544)).reshape(16, 384)
    shard = jnp.concatenate(
        [jnp.concatenate([w_query, kv_shard, w_out.T], axis=1), gains], axis=0
    )
    spread_weights = spread(shard, SPANS, 8)
    attn_weights = spread_weights[:, :256].reshape(D, 384)
    gains = spread_weights[:, 256:258].reshape(8, 768).astype(f32)
    gain_attn = gains[:, :256].reshape(D)
    gain_mlp = gains[:, 256:512].reshape(D)
    gain_query = gains[:, 512:528].reshape(HD)
    gain_key = gains[:, 528:544].reshape(HD)
    qkv_weights = attn_weights[:, :256]
    out_weights = attn_weights[:, 256:]

    slot_rows = lax.all_gather(own_rows(out_grad), SPANS, axis=0, tiled=True)
    mlp_weights = lax.all_gather(
        jnp.concatenate([w_gate, w_up, w_down.T], axis=1), SPANS, axis=0, tiled=True
    )
    gate_up_weights = mlp_weights[:, :768]
    down_weights = mlp_weights[:, 768:]

    ends = jnp.cumsum(lax.dynamic_index_in_dim(lengths, xl, 0, keepdims=False))
    offset = z * ROWS + jnp.arange(ROWS, dtype=jnp.int32)
    doc_start = jnp.where(offset >= ends[1], ends[1], jnp.where(offset >= ends[0], ends[0], 0))
    frequency = jnp.power(rope_base, -2.0 * jnp.arange(HD // 2, dtype=f32) / HD)
    angles = (offset - doc_start).astype(f32)[:, None] * frequency[None, :]
    cos_table, sin_table = jnp.cos(angles), jnp.sin(angles)
    starts = doc_start - (z - 3) * ROWS
    low = starts.reshape(ROWS // BLK, BLK)[:, 0] // BLK
    starts = starts.reshape(1, ROWS)

    rows_in = inputs.astype(f32)
    inverse_one = inverse_rms(rows_in)
    normal_one = rows_in * inverse_one
    normed = (normal_one * gain_attn).astype(bf16)
    proj = plain_dot(normed, qkv_weights)
    query_proj, kv_proj = proj[:, :HD], proj[:, HD:]
    query_inv = inverse_rms(query_proj)
    query_hat = query_proj * query_inv
    query_bf = rotate(query_hat * gain_query, cos_table, sin_table).astype(bf16)
    key_inv = inverse_rms(kv_proj)
    key_hat = kv_proj * key_inv
    key_rot = rotate(key_hat * gain_key, cos_table, sin_table)
    mine = jnp.where(first, key_rot, kv_proj).astype(bf16)
    mine = jnp.concatenate([onward(mine, 3), onward(mine, 2), onward(mine, 1), mine], axis=0)
    other = swap(mine)
    all_keys = jnp.where(first, mine, other)
    all_values = jnp.where(first, other, mine)

    out_mine = jnp.concatenate(
        [
            out_weights,
            shift(out_weights, "y", 1),
            shift(out_weights, "y", -1),
            shift(out_weights, "y", 2),
        ],
        axis=1,
    )
    out_wide = jnp.concatenate([out_mine, swap(out_mine)], axis=1)
    near = jnp.stack([y, y + 3, y + 1, y + 2]) % 4
    order = jnp.concatenate([near * 2 + core, near * 2 + (1 - core)])
    head = jnp.arange(8, dtype=jnp.int32)
    place = jnp.array([0, 2, 3, 1], jnp.int32)[(head // 2 - y) % 4]
    order_back = place + jnp.where(head % 2 == core, 0, 4)

    slots = span_place * 8 + jnp.arange(8, dtype=jnp.int32)
    hit = (slots[:, None] == span_order[None, :]).astype(bf16)
    own_grad = plain_dot(hit, slot_rows.reshape(64, 8 * D)).astype(bf16).reshape(64, D)

    def gather_rows(block):
        near_rows = spread(block, CHIPS, 8).reshape(512, D)
        return near_rows, swap(near_rows)

    grad_mine, grad_other = gather_rows(own_grad)

    attended, attended_full, total = attend(low, starts, query_bf, all_keys, all_values)
    by_rows = attended.reshape(8, 2, 4, 2, 8, HD).transpose(2, 3, 1, 0, 4, 5).reshape(8, 128, HD)
    by_rows = jnp.take(exchange(by_rows, ("y", "c")), order, axis=0)
    by_rows = by_rows.transpose(1, 0, 2).reshape(128, 8 * HD)
    branch = right_dot(by_rows, out_wide).reshape(2, 64, D)
    sent = lax.dynamic_index_in_dim(branch, 1 - xh, 0, keepdims=False).astype(bf16)
    kept = lax.dynamic_index_in_dim(branch, xh, 0, keepdims=False)
    hidden = own_rows(inputs).astype(f32) + (kept + cross(sent).astype(f32))
    inverse_two = inverse_rms(hidden)
    normal_two = hidden * inverse_two
    normed_mlp = (normal_two * gain_mlp).astype(bf16)
    normed_mine, normed_other = gather_rows(normed_mlp)

    def feed(normed_rows, grad_rows):
        wide = plain_dot(normed_rows, gate_up_weights)
        gate, up = wide[:, :384], wide[:, 384:]
        sigma = jax.nn.sigmoid(gate)
        silu = gate * sigma
        activated = (silu * up).astype(bf16)
        grad_act = plain_dot(grad_rows, down_weights)
        grad_gate = grad_act * up * sigma * (1.0 + gate * (1.0 - sigma))
        grad_up = grad_act * silu
        grad_wide = jnp.concatenate([grad_gate.astype(bf16), grad_up.astype(bf16)], axis=1)
        return activated, grad_wide

    act_mine, wide_mine = feed(normed_mine, grad_mine)
    act_other, wide_other = feed(normed_other, grad_other)
    part_other = right_dot(wide_other, gate_up_weights).astype(bf16)
    part_mine = right_dot(wide_mine, gate_up_weights)
    part = (part_mine + swap(part_other).astype(f32)).astype(bf16)
    grad_normed_mlp = jnp.sum(
        exchange(part.reshape(8, 64, D), CHIPS).astype(f32), axis=0
    )

    grad_mlp_weights = jnp.concatenate(
        [
            left_dot(normed_mine, wide_mine) + left_dot(normed_other, wide_other),
            left_dot(grad_mine, act_mine) + left_dot(grad_other, act_other),
        ],
        axis=1,
    ).astype(bf16)
    grad_mlp_weights = lax.psum_scatter(
        grad_mlp_weights, SPANS, scatter_dimension=0, tiled=True
    ).astype(f32)

    chip_place = xh * 4 + y
    out_mine_rows = right_dot(act_mine, down_weights)
    own_block = lax.dynamic_slice_in_dim(out_mine_rows, chip_place * 64, 64, 0) + hidden
    out_mine_rows = lax.dynamic_update_slice_in_dim(out_mine_rows, own_block, chip_place * 64, 0)
    out_other_rows = right_dot(act_other, down_weights)
    out_cols = jnp.stack([out_mine_rows.astype(bf16), out_other_rows.astype(bf16)])
    out_cols = out_cols.reshape(2, 512, 8, 2, 128)
    sent = lax.dynamic_index_in_dim(out_cols, 1 - core, 3, keepdims=False)
    kept = lax.dynamic_index_in_dim(out_cols, core, 3, keepdims=False)
    came = swap(sent)[::-1]
    out_cols = (kept.astype(f32) + came.astype(f32)).astype(bf16)
    out_cols = out_cols.reshape(1024, 8, 128).transpose(1, 0, 2)
    out_cols = jnp.sum(exchange(out_cols, CHIPS).astype(f32), axis=0).astype(bf16)
    out_cols = out_cols.reshape(2, 8, 8, 8, 128)
    out_cols = jnp.where(first, out_cols, out_cols[::-1])
    out_cols = out_cols.transpose(2, 1, 0, 3, 4).reshape(8, 128, 128)
    every_span = lax.all_gather(out_cols, SPANS, axis=0, tiled=True)
    own_spans = lax.dynamic_slice_in_dim(span_order, span_place * 8, 8, 0)
    layer_out = pick(own_spans, every_span).reshape(ROWS, 128)

    gain_mlp_part = jnp.sum(grad_normed_mlp * normal_two, axis=0)
    grad_hidden = own_grad.astype(f32) + norm_back(
        grad_normed_mlp * gain_mlp, normal_two, inverse_two
    )
    grad_branch = grad_hidden.astype(bf16)
    across = cross(grad_branch)
    both = jnp.where(
        xh == 0,
        jnp.concatenate([grad_branch, across], 0),
        jnp.concatenate([across, grad_branch], 0),
    )
    grad_att = plain_dot(both, out_wide).astype(bf16)
    grad_att = grad_att.reshape(128, 8, HD).transpose(1, 0, 2)
    grad_att = exchange(jnp.take(grad_att, order_back, axis=0), ("y", "c"))
    grad_att = (
        grad_att.reshape(4, 2, 2, 8, 8, HD).transpose(3, 2, 0, 1, 4, 5).reshape(ROWS, HD)
    )

    grad_query_rot, keep, send = attend_back(
        low,
        core.reshape(1),
        starts,
        query_bf,
        all_keys,
        all_values,
        grad_att,
        attended_full,
        total,
    )
    grad_kv = (keep + swap(send).astype(f32)).reshape(4, ROWS, HD)
    away = grad_kv.astype(bf16)
    grad_kv = (
        grad_kv[3]
        + backward(away[2], 1).astype(f32)
        + backward(away[1], 2).astype(f32)
        + backward(away[0], 3).astype(f32)
    )
    query_norm_grad = rotate_back(grad_query_rot, cos_table, sin_table)
    gain_query_part = jnp.sum(query_norm_grad * query_hat, axis=0)
    grad_query_proj = norm_back(query_norm_grad * gain_query, query_hat, query_inv)
    key_norm_grad = rotate_back(grad_kv, cos_table, sin_table)
    gain_key_part = jnp.where(first, jnp.sum(key_norm_grad * key_hat, axis=0), 0.0)
    grad_key_proj = norm_back(key_norm_grad * gain_key, key_hat, key_inv)
    grad_kv_proj = jnp.where(first, grad_key_proj, grad_kv)
    grad_proj = jnp.concatenate([grad_query_proj.astype(bf16), grad_kv_proj.astype(bf16)], axis=1)

    part = right_dot(grad_proj, qkv_weights)
    weighted = part * normal_one
    gain_attn_part = jnp.sum(weighted, axis=0)
    row_term = jnp.sum(weighted * gain_attn, axis=1) * (1.0 / D)
    by_cols = part.astype(bf16).reshape(ROWS, 8, 2, 128)
    sent = lax.dynamic_index_in_dim(by_cols, 1 - core, 2, keepdims=False)
    kept = lax.dynamic_index_in_dim(by_cols, core, 2, keepdims=False)
    by_cols = (kept.astype(f32) + swap(sent).astype(f32)).astype(bf16).transpose(1, 0, 2)
    row_term = row_term.reshape(8, 128)
    row_term = row_term + swap(row_term)
    coarse = row_term.astype(bf16)
    fine = (row_term - coarse.astype(f32)).astype(bf16)
    extra = jnp.concatenate([coarse, fine], axis=0)
    by_cols = jnp.concatenate([by_cols, jnp.broadcast_to(extra[None], (8, 16, 128))], axis=1)
    by_cols = jnp.sum(exchange(by_cols, CHIPS).astype(f32), axis=0)
    row_term = (by_cols[ROWS : ROWS + 8] + by_cols[ROWS + 8 :]).reshape(ROWS, 1)
    grad_normed = by_cols[:ROWS]
    own_cols = lax.dynamic_slice_in_dim(inputs, tensor_place * 128, 128, 1).astype(f32)
    own_gain = lax.dynamic_slice_in_dim(gain_attn, tensor_place * 128, 128, 0)
    hidden_cols = exchange(grad_branch.reshape(64, 16, 128).transpose(1, 0, 2), TENSOR)
    hidden_cols = hidden_cols.reshape(16, 8, 8, 128).transpose(1, 0, 2, 3).reshape(ROWS, 128)
    in_grad = hidden_cols.astype(f32) + inverse_one * (
        grad_normed * own_gain - own_cols * inverse_one * row_term
    )

    branch_mine, branch_other = gather_rows(grad_branch)
    att_rows = attended.reshape(8, 8, 2, 8, HD).transpose(2, 1, 0, 3, 4).reshape(2, 512, HD)
    att_mine = jnp.where(first, att_rows[0], att_rows[1])
    att_other = jnp.where(first, att_rows[1], att_rows[0])
    grad_out = left_dot(branch_mine, att_mine) + left_dot(branch_other, att_other)
    grad_attn = jnp.concatenate(
        [left_dot(normed, grad_proj).astype(bf16), grad_out.astype(bf16)], axis=1
    ).reshape(8, 256, 384)
    gain_parts = jnp.concatenate(
        [
            gain_attn_part.reshape(8, 256),
            gain_mlp_part.reshape(8, 256),
            gain_query_part.reshape(8, 16),
            gain_key_part.reshape(8, 16),
        ],
        axis=1,
    ).astype(bf16)
    gain_parts = jnp.pad(gain_parts, ((0, 0), (0, 16 * 384 - 544))).reshape(8, 16, 384)
    grad_attn = jnp.concatenate([grad_attn, gain_parts], axis=1)
    grad_attn = jnp.sum(exchange(grad_attn, SPANS).astype(f32), axis=0)
    gain_sums = grad_attn[256:259].reshape(9, 128)[:8]
    gain_sums = jnp.sum(spread(gain_sums, TENSOR, 16), axis=0).reshape(-1)
    grad_attn = grad_attn[:256]
    grad_kv_weight = grad_attn[:, 128:256]
    low_half, high_half = grad_kv_weight[:, :64], grad_kv_weight[:, 64:]
    came = swap(jnp.where(first, high_half, low_half))
    kept = jnp.where(first, low_half, high_half)

    return (
        layer_out,
        in_grad,
        grad_attn[:, :128],
        jnp.where(first, kept, came),
        jnp.where(first, came, kept),
        grad_attn[:, 256:].T,
        grad_mlp_weights[:, :384],
        grad_mlp_weights[:, 384:768],
        grad_mlp_weights[:, 768:].T,
        gain_sums[:256],
        gain_sums[256:512],
        gain_sums[512:528],
        gain_sums[528:544],
    )


def solution(mesh):
    fine = Mesh(mesh.devices.reshape(2, 4, 2, 4, 2), ("xl", "z", "xh", "y", "c"))
    rows = P(SPANS, None)
    by_both = P(SPANS, TENSOR)
    turned = P(TENSOR, SPANS)
    lone = P(SPANS)
    return jax.shard_map(
        body,
        mesh=fine,
        in_specs=(
            rows,
            rows,
            P(),
            P(),
            by_both,
            by_both,
            by_both,
            turned,
            by_both,
            by_both,
            turned,
            lone,
            lone,
            lone,
            lone,
        ),
        out_specs=(
            by_both,
            by_both,
            by_both,
            by_both,
            by_both,
            turned,
            by_both,
            by_both,
            turned,
            lone,
            lone,
            lone,
            lone,
        ),
        check_vma=False,
    )
```

time: 1820 us -> 551 us (0.30)
  the two profiles are of different devices: /device:TPU:1 before, /device:TPU:6 now
where the time goes in v1:
time: 551 us; the launch traced here: 541 us
  waiting for transfers between devices  186 us (34%)
  starting transfers between devices  102 us (19%)
  local copies, waits for them, and re-layouts  90.2 us (16%)
  matrix products  70.2 us (13%)
  other arithmetic  59 us (11%)
  Pallas kernels  17.6 us (3%)
  between operations  15.7 us (3%)
    all_to_all x12, waiting for transfers between devices, exchange(): return lax.all_to_all(block, axes, 0, 0, tiled=True)  132 us
    all_to_all x12, starting transfers between devices, exchange(): return lax.all_to_all(block, axes, 0, 0, tiled=True)  77.5 us
    dot_general x7, matrix products, left_dot(): lax.dot_general(first_op, second_op, (((0,), (0,)), ((), ())), preferred_...  26.6 us
    unnamed x168, local copies, waits for them, and re-layouts  24.8 us
    ppermute x3, waiting for transfers between devices, backward(): lax.ppermute(block, 'z', [(i, i - by) for i in range(4) if i - by >= 0])  24.5 us
    dot_general x7, matrix products, plain_dot(): return jnp.dot(first_op, second_op, preferred_element_type=f32)  22.5 us
    dot_general x6, matrix products, right_dot(): lax.dot_general(first_op, second_op, (((1,), (1,)), ((), ())), preferred_...  21.1 us
    dynamic_slice x1, local copies, waits for them, and re-layouts, body(): kept = lax.dynamic_index_in_dim(by_cols, core, 2, keepdims=False)  11.5 us
  transfers between devices with their start and end apart: 39, of which 17 were waited for; matrix products, arithmetic and copies ran while one was open for 36% of the time, Pallas kernels for 1%

profile of v1, /device:TPU:6, one launch (start us, length us, event | category | flops | bytes accessed | tf_op | source)
XLA Modules:
  0.0 540.7 jit_solution(5979238911787291367)
XLA Ops:
  16.2 6.8 %all-to-all-start = ((bf16[8,272,384]{2,1,0:T(8,128)(2,1)}), bf16[8,272,384]{2,1,0:T(8,128)(2,1)S(1)}, u32[]{:S(2)}, u32[]{:S(2)}) async-start(bf16[8,272,384]{2,1,0:T(8,128)(2,1)} %broadcast_in_dim.43), calls=%async_computation | async-start | bytes 3342336 | tf_op jit(solution)/shard_map/all_to_all | solution.py:49
  27.5 3.1 fusion.3
  30.7 22.7 %all-to-all-done = bf16[8,272,384]{2,1,0:T(8,128)(2,1)S(1)} async-done(((bf16[8,272,384]{2,1,0:T(8,128)(2,1)}), bf16[8,272,384]{2,1,0:T(8,128)(2,1)S(1)}, u32[]{:S(2)}, u32[]{:S(2)}) %all-to-all-start) | async-done | bytes 1671200 | tf_op jit(solution)/shard_map/all_to_all | solution.py:49
  53.8 4.1 fusion.21
  58.7 2.4 fusion.56
  61.3 2.9 collective-permute-start.3
  64.2 6.8 %collective-permute-start.2 = (bf16[1024,128]{1,0:T(8,128)(2,1)S(1)}, bf16[1024,128]{1,0:T(8,128)(2,1)S(1)}, u32[]{:S(2)}, u32[]{:S(2)}) collective-permute-start(bf16[1024,128]{1,0:T(8,128)(2,1)S(1)} %fusion.67), channel_id=1, source_target_pairs={{0,32},{16,48},{1,33},{17,49},{2,34},{18,50},{3,35},{19,51},{4,36}... | collective-permute-start | bytes 786440 | tf_op jit(solution)/shard_map/ppermute | solution.py:41
  72.5 3.2 collective-permute-start.7
  77.7 8.6 %collective-permute-done.1 = bf16[1024,128]{1,0:T(8,128)(2,1)S(1)} collective-permute-done((bf16[1024,128]{1,0:T(8,128)(2,1)S(1)}, bf16[1024,128]{1,0:T(8,128)(2,1)S(1)}, u32[]{:S(2)}, u32[]{:S(2)}) %collective-permute-start.1) | collective-permute-done | bytes 262176 | tf_op jit(solution)/shard_map/ppermute | solution.py:41
  89.0 9.3 %collective-permute-done.6 = bf16[2048,128]{1,0:T(8,128)(2,1)S(1)} collective-permute-done((bf16[2048,128]{1,0:T(8,128)(2,1)S(1)}, bf16[2048,128]{1,0:T(8,128)(2,1)S(1)}, u32[]{:S(2)}, u32[]{:S(2)}) %collective-permute-start.6) | collective-permute-done | bytes 524320 | tf_op jit(solution)/shard_map/ppermute | solution.py:37
  102.8 4.8 attend.1
  108.4 4.5 all-to-all-start.1
  114.8 5.6 %all-to-all-done.1 = bf16[8,128,128]{2,1,0:T(8,128)(2,1)} async-done(((bf16[8,128,128]{2,1,0:T(8,128)(2,1)}), bf16[8,128,128]{2,1,0:T(8,128)(2,1)}, u32[]{:S(2)}, u32[]{:S(2)}) %all-to-all-start.1) | async-done | bytes 262176 | tf_op jit(solution)/shard_map/all_to_all | solution.py:49
  123.1 3.2 constant_dynamic-update-slice_fusion
  126.3 3.7 fusion.7
  133.2 8.3 %collective-permute-done.9 = bf16[64,2048]{1,0:T(8,128)(2,1)S(1)} collective-permute-done((bf16[64,2048]{1,0:T(8,128)(2,1)}, bf16[64,2048]{1,0:T(8,128)(2,1)S(1)}, u32[]{:S(2)}, u32[]{:S(2)}) %collective-permute-start.9) | collective-permute-done | bytes 262176 | tf_op jit(solution)/shard_map/ppermute | solution.py:33
  145.3 6.2 %all-to-all-start.2 = ((bf16[8,64,2048]{2,1,0:T(8,128)(2,1)}), bf16[8,64,2048]{2,1,0:T(8,128)(2,1)}, u32[]{:S(2)}, u32[]{:S(2)}) async-start(bf16[8,64,2048]{2,1,0:T(8,128)(2,1)} %broadcast_in_dim.45), calls=%async_computation.2 | async-start | bytes 4194304 | tf_op jit(solution)/shard_map/all_to_all | solution.py:49
  151.5 4.2 reshape.389
  155.7 2.7 convolution_convert_fusion
  159.6 17.2 %all-to-all-done.2 = bf16[8,64,2048]{2,1,0:T(8,128)(2,1)} async-done(((bf16[8,64,2048]{2,1,0:T(8,128)(2,1)}), bf16[8,64,2048]{2,1,0:T(8,128)(2,1)}, u32[]{:S(2)}, u32[]{:S(2)}) %all-to-all-start.2) | async-done | bytes 2097184 | tf_op jit(solution)/shard_map/all_to_all | solution.py:49
  178.3 5.7 %all-to-all-start.4 = ((bf16[8,64,2048]{2,1,0:T(8,128)(2,1)}), bf16[8,64,2048]{2,1,0:T(8,128)(2,1)}, u32[]{:S(2)}, u32[]{:S(2)}) async-start(bf16[8,64,2048]{2,1,0:T(8,128)(2,1)} %broadcast_in_dim.46), calls=%async_computation.4 | async-start | bytes 4194304 | tf_op jit(solution)/shard_map/all_to_all | solution.py:49
  184.0 25.8 %all-to-all-done.4 = bf16[8,64,2048]{2,1,0:T(8,128)(2,1)} async-done(((bf16[8,64,2048]{2,1,0:T(8,128)(2,1)}), bf16[8,64,2048]{2,1,0:T(8,128)(2,1)}, u32[]{:S(2)}, u32[]{:S(2)}) %all-to-all-start.4) | async-done | bytes 2097184 | tf_op jit(solution)/shard_map/all_to_all | solution.py:49
  209.8 4.5 fusion.14
  214.3 3.9 multiply_convert_fusion.1
  221.1 3.4 fusion.16
  224.5 3.1 multiply_convert_fusion.3
  227.6 3.1 add_convert_fusion.1
  230.8 5.8 %all-to-all-start.5 = ((bf16[8,64,2048]{2,1,0:T(8,128)(2,1)}), bf16[8,64,2048]{2,1,0:T(8,128)(2,1)}, u32[]{:S(2)}, u32[]{:S(2)}) async-start(bf16[8,64,2048]{2,1,0:T(8,128)(2,1)} %bitcast.164), calls=%async_computation.5 | async-start | bytes 4194304 | tf_op jit(solution)/shard_map/all_to_all | solution.py:49
  241.0 4.3 fusion.127
  245.3 4.7 fusion.29
  250.0 6.1 %fusion.74 = f32[2048,768]{0,1:T(8,128)} fusion(bf16[512,2048]{1,0:T(8,128)(2,1)} %bitcast.19, bf16[512,384]{1,0:T(8,128)(2,1)S(1)} %copy-done.36, bf16[512,384]{1,0:T(8,128)(2,1)S(1)} %copy-done.34), kind=kOutput, calls=%fused_computation.143 | convolution fusion | flops 1612185600 | bytes 9175040 | tf_op jit(solution)/shard_map/dot_general | solution.py:61
  256.1 6.3 %all-to-all-done.5 = bf16[8,64,2048]{2,1,0:T(8,128)(2,1)} async-done(((bf16[8,64,2048]{2,1,0:T(8,128)(2,1)}), bf16[8,64,2048]{2,1,0:T(8,128)(2,1)}, u32[]{:S(2)}, u32[]{:S(2)}) %all-to-all-start.5) | async-done | bytes 2097184 | tf_op jit(solution)/shard_map/all_to_all | solution.py:49
  268.0 5.6 %add_convert_fusion = bf16[2048,768]{0,1:T(8,128)(2,1)} fusion(f32[2048,768]{0,1:T(8,128)S(1)} %copy-done.3, bf16[512,2048]{1,0:T(8,128)(2,1)} %collective-permute-done.10, bf16[512,384]{1,0:T(8,128)(2,1)} %copy-done.38, bf16[512,384]{1,0:T(8,128)(2,1)} %copy-done.37), kind=kOutput, calls=%fused_computation.11 | convolution fusion | flops 1615331328 | bytes 12320768 | tf_op jit(solution)/shard_map/dot_general | solution.py:61
  273.6 2.8 collective-permute-done.14
  278.7 3.4 all-to-all-start.7
  282.4 4.9 add_convert_fusion.2
  289.7 7.8 %attend_back.1 = (f32[1024,128]{1,0:T(8,128)S(1)}, f32[4096,128]{1,0:T(8,128)}, bf16[4096,128]{1,0:T(8,128)(2,1)}) custom-call(s32[4]{0:T(128)S(1)} %and_select_fusion.4.low_ref, s32[1]{0:T(128)} %bitcast.37.core_ref, s32[1,1024]{1,0:T(1,128)S(1)} %fusion.93.start_ref, bf16[1024,128]{1,0:T(8,128)(2,1)S(1)} %pad_maximum_fusion.18.q_ref, ...), custom_call_target="tpu_custom_call" | custom-call | flops 2684354560 | bytes 8388608 | tf_op jit(solution)/shard_map/attend_back/pallas_call | solution.py:207
  297.5 3.0 pad_maximum_fusion
  302.2 2.7 convolution_convert_fusion.2
  304.9 2.7 stack.30
  308.2 2.5 convert_element_type.199
  310.7 2.7 stack.29
  315.0 5.6 %all-to-all-start.9 = ((bf16[8,64,2048]{2,1,0:T(8,128)(2,1)}), bf16[8,64,2048]{2,1,0:T(8,128)(2,1)}, u32[]{:S(2)}, u32[]{:S(2)}) async-start(bf16[8,64,2048]{2,1,0:T(8,128)(2,1)} %broadcast_in_dim.48), calls=%async_computation.9 | async-start | bytes 4194304 | tf_op jit(solution)/shard_map/all_to_all | solution.py:49
  331.4 8.9 %collective-permute-done.16 = bf16[1024,128]{1,0:T(8,128)(2,1)S(1)} collective-permute-done((bf16[1024,128]{1,0:T(8,128)(2,1)S(1)}, bf16[1024,128]{1,0:T(8,128)(2,1)S(1)}, u32[]{:S(2)}, u32[]{:S(2)}) %collective-permute-start.16) | collective-permute-done | bytes 262176 | tf_op jit(solution)/shard_map/ppermute | solution.py:45
  340.3 15.6 %collective-permute-done.18 = bf16[1024,128]{1,0:T(8,128)(2,1)S(1)} collective-permute-done((bf16[1024,128]{1,0:T(8,128)(2,1)S(1)}, bf16[1024,128]{1,0:T(8,128)(2,1)S(1)}, u32[]{:S(2)}, u32[]{:S(2)}) %collective-permute-start.18) | collective-permute-done | bytes 262176 | tf_op jit(solution)/shard_map/ppermute | solution.py:45
  356.1 2.5 fusion.60
  363.2 5.1 fusion.4
  368.3 7.8 %reshape.398 = bf16[1024,8,2,128]{3,2,1,0:T(2,128)(2,1)} reshape(bf16[1024,2048]{1,0:T(8,128)(2,1)} %get-tuple-element.139) | data formatting | bytes 8388608 | tf_op jit(solution)/shard_map/reshape | solution.py:468
  376.1 11.5 %constant_dynamic-slice_fusion.1 = (bf16[1024,8,1,128]{3,2,1,0:T(2,128)(2,1)}, bf16[1024,8,1,128]{3,2,1,0:T(2,128)(2,1)}) fusion(bf16[1024,8,2,128]{3,2,1,0:T(2,128)(2,1)} %reshape.398, s32[]{:T(128)S(6)} %select_n.271, s32[]{:T(128)S(6)} %select_n.272), kind=kLoop, calls=%fused_computation.216 | loop fusion | bytes 8388616 | tf_op jit(solution)/shard_map/jit(dynamic_index_in_dim)/dynamic_slice | solution.py:470
  391.6 7.3 %all-to-all-start.3 = ((bf16[8,1024,128]{2,1,0:T(8,128)(2,1)}), bf16[8,1024,128]{2,1,0:T(8,128)(2,1)S(1)}, u32[]{:S(2)}, u32[]{:S(2)}) async-start(bf16[8,1024,128]{2,1,0:T(8,128)(2,1)} %bitcast.158), calls=%async_computation.3 | async-start | bytes 4194304 | tf_op jit(solution)/shard_map/all_to_all | solution.py:49
  399.1 3.9 copy.252
  410.0 2.6 copy.231
  412.7 2.8 pad_maximum_fusion.3
  415.5 9.6 %all-to-all-done.3 = bf16[8,1024,128]{2,1,0:T(8,128)(2,1)S(1)} async-done(((bf16[8,1024,128]{2,1,0:T(8,128)(2,1)}), bf16[8,1024,128]{2,1,0:T(8,128)(2,1)S(1)}, u32[]{:S(2)}, u32[]{:S(2)}) %all-to-all-start.3) | async-done | bytes 2097184 | tf_op jit(solution)/shard_map/all_to_all | solution.py:49
  425.0 12.8 %all-to-all-start.10 = ((bf16[8,272,384]{2,1,0:T(8,128)(2,1)}), bf16[8,272,384]{2,1,0:T(8,128)(2,1)}, u32[]{:S(2)}, u32[]{:S(2)}) async-start(bf16[8,272,384]{2,1,0:T(8,128)(2,1)} %pad_maximum_fusion.3), calls=%async_computation.10 | async-start | bytes 3342336 | tf_op jit(solution)/shard_map/all_to_all | solution.py:49
  440.7 24.3 %all-to-all-done.10 = bf16[8,272,384]{2,1,0:T(8,128)(2,1)} async-done(((bf16[8,272,384]{2,1,0:T(8,128)(2,1)}), bf16[8,272,384]{2,1,0:T(8,128)(2,1)}, u32[]{:S(2)}, u32[]{:S(2)}) %all-to-all-start.10) | async-done | bytes 1671200 | tf_op jit(solution)/shard_map/all_to_all | solution.py:49
  465.0 6.0 %all-to-all-start.6 = ((bf16[16,64,128]{2,1,0:T(8,128)(2,1)}), bf16[16,64,128]{2,1,0:T(8,128)(2,1)S(1)}, u32[]{:S(2)}, u32[]{:S(2)}) async-start(bf16[16,64,128]{2,1,0:T(8,128)(2,1)} %bitcast_bitcast_fusion.1), calls=%async_computation.6 | async-start | bytes 524288 | tf_op jit(solution)/shard_map/all_to_all | solution.py:49
  471.0 3.3 fusion.10
  476.0 4.5 all-to-all-done.6
  481.1 6.2 %all-to-all-start.11 = ((f32[16,8,128]{2,1,0:T(8,128)}), f32[16,8,128]{2,1,0:T(8,128)S(1)}, u32[]{:S(2)}, u32[]{:S(2)}) async-start(f32[16,8,128]{2,1,0:T(8,128)} %broadcast_in_dim.50), calls=%async_computation.12 | async-start | bytes 131072 | tf_op jit(solution)/shard_map/all_to_all | solution.py:49
  487.2 4.0 pad_maximum_fusion.1
  492.9 7.2 %all-to-all-start.8 = ((bf16[8,1040,128]{2,1,0:T(8,128)(2,1)}), bf16[8,1040,128]{2,1,0:T(8,128)(2,1)S(1)}, u32[]{:S(2)}, u32[]{:S(2)}) async-start(bf16[8,1040,128]{2,1,0:T(8,128)(2,1)} %copy.220), calls=%async_computation.8 | async-start | bytes 4259840 | tf_op jit(solution)/shard_map/all_to_all | solution.py:49
  512.2 14.1 %all-to-all-done.8 = bf16[8,1040,128]{2,1,0:T(8,128)(2,1)S(1)} async-done(((bf16[8,1040,128]{2,1,0:T(8,128)(2,1)}), bf16[8,1040,128]{2,1,0:T(8,128)(2,1)S(1)}, u32[]{:S(2)}, u32[]{:S(2)}) %all-to-all-start.8) | async-done | bytes 2129952 | tf_op jit(solution)/shard_map/all_to_all | solution.py:49
  528.8 5.0 pick.1
  (338 shorter events, 109.3 us)
Async XLA Ops:
  7.2 7.2 %copy-start = (s32[2,3]{1,0:T(2,128)S(1)}, s32[2,3]{1,0:T(2,128)}, u32[]{:S(2)}) copy-start(s32[2,3]{1,0:T(2,128)} %param.20) | copy-start | bytes 76
  7.2 7.1 %copy-start.68 = (bf16[16]{0:T(256)(128)(2,1)S(1)}, bf16[16]{0:T(256)(128)(2,1)}, u32[]{:S(2)}) copy-start(bf16[16]{0:T(256)(128)(2,1)} %param.32) | copy-start | bytes 100
  7.2 7.0 %copy-start.69 = (bf16[16]{0:T(256)(128)(2,1)S(1)}, bf16[16]{0:T(256)(128)(2,1)}, u32[]{:S(2)}) copy-start(bf16[16]{0:T(256)(128)(2,1)} %param.31) | copy-start | bytes 100
  7.2 7.3 %copy-start.51 = (bf16[128,256]{1,0:T(8,128)(2,1)S(1)}, bf16[128,256]{1,0:T(8,128)(2,1)}, u32[]{:S(2)}) copy-start(bf16[128,256]{1,0:T(8,128)(2,1)} %param.25) | copy-start | bytes 196612
  7.3 144.3 %all-gather.8.cloned.1.call-start = ((), (), s32[]{:S(2)}) async-start(), calls=%async_computation.15 | async-start | bytes 2359296 | tf_op jit(solution)/shard_map/all_gather | solution.py:292
  7.3 7.5 %copy-start.50 = (bf16[256,128]{1,0:T(8,128)(2,1)S(1)}, bf16[256,128]{1,0:T(8,128)(2,1)}, u32[]{:S(2)}) copy-start(bf16[256,128]{1,0:T(8,128)(2,1)} %param.22) | copy-start | bytes 196612
  9.1 200.7 %all-gather.4.cloned.1.call-start = ((), (), s32[]{:S(2)}) async-start(), calls=%async_computation.13 | async-start | bytes 5308416 | tf_op jit(solution)/shard_map/all_gather | solution.py:293
  10.9 3.8 collective-permute-start
  16.2 37.1 %all-to-all-start = ((bf16[8,272,384]{2,1,0:T(8,128)(2,1)}), bf16[8,272,384]{2,1,0:T(8,128)(2,1)S(1)}, u32[]{:S(2)}, u32[]{:S(2)}) async-start(bf16[8,272,384]{2,1,0:T(8,128)(2,1)} %broadcast_in_dim.43), calls=%async_computation | async-start | bytes 3342336 | tf_op jit(solution)/shard_map/all_to_all | solution.py:49
  23.0 63.5 %copy-start.63 = (f32[64]{0:T(128)}, f32[64]{0:T(128)S(1)}, u32[]{:S(2)}) copy-start(f32[64]{0:T(128)S(1)} %multiply_power_fusion) | copy-start | bytes 772
  24.9 61.7 %copy-start.44 = (f32[1024]{0:T(1024)}, f32[1024]{0:T(1024)S(1)}, u32[]{:S(2)}) copy-start(f32[1024]{0:T(1024)S(1)} %subtract_convert_fusion.1) | copy-start | bytes 12292
  30.6 27.3 %copy-start.52 = (f32[1024]{0:T(1024)}, f32[1024]{0:T(1024)S(1)}, u32[]{:S(2)}) copy-start(f32[1024]{0:T(1024)S(1)} %add_rsqrt_fusion.2) | copy-start | bytes 12292
  53.8 18.6 %copy-start.22 = (bf16[8,256,384]{2,1,0:T(8,128)(2,1)}, bf16[8,256,384]{2,1,0:T(8,128)(2,1)S(1)}, u32[]{:S(2)}) copy-start(bf16[8,256,384]{2,1,0:T(8,128)(2,1)S(1)} %slice.232) | copy-start | bytes 4718596
  61.3 15.5 %collective-permute-start.3 = (bf16[1024,128]{1,0:T(8,128)(2,1)S(1)}, bf16[1024,128]{1,0:T(8,128)(2,1)S(1)}, u32[]{:S(2)}, u32[]{:S(2)}) collective-permute-start(bf16[1024,128]{1,0:T(8,128)(2,1)S(1)} %fusion.67), channel_id=1, source_target_pairs={{0,16},{16,32},{32,48},{1,17},{17,33},{33,49},{2,18},{18,34},{34,5... | collective-permute-start | bytes 786440 | tf_op jit(solution)/shard_map/ppermute | solution.py:41
  64.2 13.5 %collective-permute-start.2 = (bf16[1024,128]{1,0:T(8,128)(2,1)S(1)}, bf16[1024,128]{1,0:T(8,128)(2,1)S(1)}, u32[]{:S(2)}, u32[]{:S(2)}) collective-permute-start(bf16[1024,128]{1,0:T(8,128)(2,1)S(1)} %fusion.67), channel_id=1, source_target_pairs={{0,32},{16,48},{1,33},{17,49},{2,34},{18,50},{3,35},{19,51},{4,36}... | collective-permute-start | bytes 786440 | tf_op jit(solution)/shard_map/ppermute | solution.py:41
  71.0 15.3 %collective-permute-start.1 = (bf16[1024,128]{1,0:T(8,128)(2,1)S(1)}, bf16[1024,128]{1,0:T(8,128)(2,1)S(1)}, u32[]{:S(2)}, u32[]{:S(2)}) collective-permute-start(bf16[1024,128]{1,0:T(8,128)(2,1)S(1)} %fusion.67), channel_id=1, source_target_pairs={{0,48},{1,49},{2,50},{3,51},{4,52},{5,53},{6,54},{7,55},{8,56},{9,... | collective-permute-start | bytes 786440 | tf_op jit(solution)/shard_map/ppermute | solution.py:41
  72.5 16.5 %collective-permute-start.7 = (bf16[2048,128]{1,0:T(8,128)(2,1)S(1)}, bf16[2048,128]{1,0:T(8,128)(2,1)S(1)}, u32[]{:S(2)}, u32[]{:S(2)}) collective-permute-start(bf16[2048,128]{1,0:T(8,128)(2,1)S(1)} %get-tuple-element.150), channel_id=1, source_target_pairs={{0,4},{2,6},{4,0},{6,2},{1,5},{3,7},{5,1},{7,3},{8,12},{10,14},{12... | collective-permute-start | bytes 1572872 | tf_op jit(solution)/shard_map/ppermute | solution.py:37
  75.7 22.6 %collective-permute-start.6 = (bf16[2048,128]{1,0:T(8,128)(2,1)S(1)}, bf16[2048,128]{1,0:T(8,128)(2,1)S(1)}, u32[]{:S(2)}, u32[]{:S(2)}) collective-permute-start(bf16[2048,128]{1,0:T(8,128)(2,1)S(1)} %get-tuple-element.150), channel_id=1, source_target_pairs={{0,6},{2,0},{4,2},{6,4},{1,7},{3,1},{5,3},{7,5},{8,14},{10,8},{12,... | collective-permute-start | bytes 1572872 | tf_op jit(solution)/shard_map/ppermute | solution.py:37
  76.9 21.5 %collective-permute-start.5 = (bf16[2048,128]{1,0:T(8,128)(2,1)S(1)}, bf16[2048,128]{1,0:T(8,128)(2,1)S(1)}, u32[]{:S(2)}, u32[]{:S(2)}) collective-permute-start(bf16[2048,128]{1,0:T(8,128)(2,1)S(1)} %get-tuple-element.150), channel_id=1, source_target_pairs={{0,2},{2,4},{4,6},{6,0},{1,3},{3,5},{5,7},{7,1},{8,10},{10,12},{12... | collective-permute-start | bytes 1572872 | tf_op jit(solution)/shard_map/ppermute | solution.py:37
  86.4 15.9 %collective-permute-start.4 = (bf16[4096,128]{1,0:T(8,128)(2,1)S(1)}, bf16[4096,128]{1,0:T(8,128)(2,1)S(1)}, u32[]{:S(2)}, u32[]{:S(2)}) collective-permute-start(bf16[4096,128]{1,0:T(8,128)(2,1)S(1)} %pad_maximum_fusion.5), channel_id=1, source_target_pairs={{0,1},{1,0},{2,3},{3,2},{4,5},{5,4},{6,7},{7,6},{8,9},{9,8},{10,11... | collective-permute-start | bytes 3145736 | tf_op jit(solution)/shard_map/ppermute | solution.py:29
  89.0 10.9 %copy-start.27 = (bf16[2048,128]{1,0:T(8,128)(2,1)}, bf16[2048,128]{1,0:T(8,128)(2,1)S(1)}, u32[]{:S(2)}) copy-start(bf16[2048,128]{1,0:T(8,128)(2,1)S(1)} %collective-permute-done.7) | copy-start | bytes 1572868
  99.9 23.2 %collective-permute-start.8 = (bf16[2048,512]{1,0:T(8,128)(2,1)}, bf16[2048,512]{1,0:T(8,128)(2,1)}, u32[]{:S(2)}, u32[]{:S(2)}) collective-permute-start(bf16[2048,512]{1,0:T(8,128)(2,1)} %pad_maximum_fusion.2), channel_id=1, source_target_pairs={{0,1},{1,0},{2,3},{3,2},{4,5},{5,4},{6,7},{7,6},{8,9},{9,8},{10,11... | collective-permute-start | bytes 6291464 | tf_op jit(solution)/shard_map/ppermute | solution.py:29
  108.4 12.1 %all-to-all-start.1 = ((bf16[8,128,128]{2,1,0:T(8,128)(2,1)}), bf16[8,128,128]{2,1,0:T(8,128)(2,1)}, u32[]{:S(2)}, u32[]{:S(2)}) async-start(bf16[8,128,128]{2,1,0:T(8,128)(2,1)} %bitcast.14), calls=%async_computation.1 | async-start | bytes 524288 | tf_op jit(solution)/shard_map/all_to_all | solution.py:49
  131.7 9.7 %collective-permute-start.9 = (bf16[64,2048]{1,0:T(8,128)(2,1)}, bf16[64,2048]{1,0:T(8,128)(2,1)S(1)}, u32[]{:S(2)}, u32[]{:S(2)}) collective-permute-start(bf16[64,2048]{1,0:T(8,128)(2,1)} %fusion.78), channel_id=1, source_target_pairs={{0,8},{8,0},{1,9},{9,1},{2,10},{10,2},{3,11},{11,3},{4,12},{12,4},... | collective-permute-start | bytes 786440 | tf_op jit(solution)/shard_map/ppermute | solution.py:33
  133.2 9.6 %copy-start.42 = (f32[1,2,8,128]{3,1,2,0:T(2,128)}, f32[1,2,8,128]{3,1,2,0:T(2,128)S(1)}, u32[]{:S(2)}) copy-start(f32[1,2,8,128]{3,1,2,0:T(2,128)S(1)} %copy.239) | copy-start | bytes 24580
  145.3 31.5 %all-to-all-start.2 = ((bf16[8,64,2048]{2,1,0:T(8,128)(2,1)}), bf16[8,64,2048]{2,1,0:T(8,128)(2,1)}, u32[]{:S(2)}, u32[]{:S(2)}) async-start(bf16[8,64,2048]{2,1,0:T(8,128)(2,1)} %broadcast_in_dim.45), calls=%async_computation.2 | async-start | bytes 4194304 | tf_op jit(solution)/shard_map/all_to_all | solution.py:49
  159.6 18.8 %copy-start.25 = (bf16[64,2048]{1,0:T(8,128)(2,1)}, bf16[64,2048]{1,0:T(8,128)(2,1)S(1)}, u32[]{:S(2)}) copy-start(bf16[64,2048]{1,0:T(8,128)(2,1)S(1)} %reshape.390) | copy-start | bytes 786436
  178.3 31.5 %all-to-all-start.4 = ((bf16[8,64,2048]{2,1,0:T(8,128)(2,1)}), bf16[8,64,2048]{2,1,0:T(8,128)(2,1)}, u32[]{:S(2)}, u32[]{:S(2)}) async-start(bf16[8,64,2048]{2,1,0:T(8,128)(2,1)} %broadcast_in_dim.46), calls=%async_computation.4 | async-start | bytes 4194304 | tf_op jit(solution)/shard_map/all_to_all | solution.py:49
  184.0 25.8 %collective-permute-start.10 = (bf16[512,2048]{1,0:T(8,128)(2,1)}, bf16[512,2048]{1,0:T(8,128)(2,1)}, u32[]{:S(2)}, u32[]{:S(2)}) collective-permute-start(bf16[512,2048]{1,0:T(8,128)(2,1)} %bitcast.19), channel_id=1, source_target_pairs={{0,1},{1,0},{2,3},{3,2},{4,5},{5,4},{6,7},{7,6},{8,9},{9,8},{10,11... | collective-permute-start | bytes 6291464 | tf_op jit(solution)/shard_map/ppermute | solution.py:29
  209.8 4.5 collective-permute-start.12
  220.1 7.6 %collective-permute-start.13 = (bf16[512,2048]{1,0:T(8,128)(2,1)S(1)}, bf16[512,2048]{1,0:T(8,128)(2,1)S(1)}, u32[]{:S(2)}, u32[]{:S(2)}) collective-permute-start(bf16[512,2048]{1,0:T(8,128)(2,1)S(1)} %convolution_convert_fusion.1), channel_id=1, source_target_pairs={{0,1},{1,0},{2,3},{3,2},{4,5},{5,4},{6,7},{7,6},{8,9},{9,8},{10,11... | collective-permute-start | bytes 6291464 | tf_op jit(solution)/shard_map/ppermute | solution.py:29
  230.8 31.6 %all-to-all-start.5 = ((bf16[8,64,2048]{2,1,0:T(8,128)(2,1)}), bf16[8,64,2048]{2,1,0:T(8,128)(2,1)}, u32[]{:S(2)}, u32[]{:S(2)}) async-start(bf16[8,64,2048]{2,1,0:T(8,128)(2,1)} %bitcast.164), calls=%async_computation.5 | async-start | bytes 4194304 | tf_op jit(solution)/shard_map/all_to_all | solution.py:49
  250.0 14.5 %copy-start.13 = (f32[64,2048]{1,0:T(8,128)S(1)}, f32[64,2048]{1,0:T(8,128)}, u32[]{:S(2)}) copy-start(f32[64,2048]{1,0:T(8,128)} %copy-done.12) | copy-start | bytes 1572868
  256.1 8.4 %copy-start.43 = (f32[1,2,8,128]{3,1,2,0:T(2,128)S(1)}, f32[1,2,8,128]{3,1,2,0:T(2,128)}, u32[]{:S(2)}) copy-start(f32[1,2,8,128]{3,1,2,0:T(2,128)} %copy-done.42) | copy-start | bytes 24580
  256.1 8.4 %copy-start.66 = (f32[64]{0:T(128)S(1)}, f32[64]{0:T(128)}, u32[]{:S(2)}) copy-start(f32[64]{0:T(128)} %copy-done.65) | copy-start | bytes 772
  267.0 9.4 %copy-start.23 = (bf16[64,2048]{1,0:T(8,128)(2,1)}, bf16[64,2048]{1,0:T(8,128)(2,1)S(1)}, u32[]{:S(2)}) copy-start(bf16[64,2048]{1,0:T(8,128)(2,1)S(1)} %get-tuple-element.169) | copy-start | bytes 786436
  267.0 9.4 %copy-start.17 = (bf16[2048,1024]{1,0:T(8,128)(2,1)S(1)}, bf16[2048,1024]{1,0:T(8,128)(2,1)}, u32[]{:S(2)}) copy-start(bf16[2048,1024]{1,0:T(8,128)(2,1)} %constant_dynamic-update-slice_fusion) | copy-start | bytes 12582916
  267.0 9.4 %collective-permute-start.14 = (bf16[64,2048]{1,0:T(8,128)(2,1)S(1)}, bf16[64,2048]{1,0:T(8,128)(2,1)S(1)}, u32[]{:S(2)}, u32[]{:S(2)}) collective-permute-start(bf16[64,2048]{1,0:T(8,128)(2,1)S(1)} %get-tuple-element.169), channel_id=1, source_target_pairs={{0,8},{8,0},{1,9},{9,1},{2,10},{10,2},{3,11},{11,3},{4,12},{12,4},... | collective-permute-start | bytes 786440 | tf_op jit(solution)/shard_map/ppermute | solution.py:33
  278.7 10.9 %all-to-all-start.7 = ((bf16[8,128,128]{2,1,0:T(8,128)(2,1)}), bf16[8,128,128]{2,1,0:T(8,128)(2,1)S(1)}, u32[]{:S(2)}, u32[]{:S(2)}) async-start(bf16[8,128,128]{2,1,0:T(8,128)(2,1)} %broadcast_select_fusion.2), calls=%async_computation.7 | async-start | bytes 524288 | tf_op jit(solution)/shard_map/all_to_all | solution.py:49
  282.2 223.3 %reduce-scatter.2.cloned.1.call-start = ((), (), s32[]{:S(2)}) async-start(), calls=%async_computation.16 | async-start | bytes 5308416 | tf_op jit(solution)/shard_map/reduce_scatter | solution.py:394
  289.7 7.9 %copy-start.4 = (bf16[2048,768]{0,1:T(8,128)(2,1)S(1)}, bf16[2048,768]{0,1:T(8,128)(2,1)}, u32[]{:S(2)}) copy-start(bf16[2048,768]{0,1:T(8,128)(2,1)} %add_convert_fusion) | copy-start | bytes 9437188
  289.7 7.9 %copy-start.7 = (bf16[2048,384]{0,1:T(8,128)(2,1)S(1)}, bf16[2048,384]{0,1:T(8,128)(2,1)}, u32[]{:S(2)}) copy-start(bf16[2048,384]{0,1:T(8,128)(2,1)} %add_convert_fusion.2) | copy-start | bytes 4718596
  297.5 23.3 %collective-permute-start.15 = (bf16[4096,128]{1,0:T(8,128)(2,1)}, bf16[4096,128]{1,0:T(8,128)(2,1)}, u32[]{:S(2)}, u32[]{:S(2)}) collective-permute-start(bf16[4096,128]{1,0:T(8,128)(2,1)} %get-tuple-element.25), channel_id=1, source_target_pairs={{0,1},{1,0},{2,3},{3,2},{4,5},{5,4},{6,7},{7,6},{8,9},{9,8},{10,11... | collective-permute-start | bytes 3145736 | tf_op jit(solution)/shard_map/ppermute | solution.py:29
  315.0 61.1 %all-to-all-start.9 = ((bf16[8,64,2048]{2,1,0:T(8,128)(2,1)}), bf16[8,64,2048]{2,1,0:T(8,128)(2,1)}, u32[]{:S(2)}, u32[]{:S(2)}) async-start(bf16[8,64,2048]{2,1,0:T(8,128)(2,1)} %broadcast_in_dim.48), calls=%async_computation.9 | async-start | bytes 4194304 | tf_op jit(solution)/shard_map/all_to_all | solution.py:49
  324.0 16.4 %collective-permute-start.16 = (bf16[1024,128]{1,0:T(8,128)(2,1)S(1)}, bf16[1024,128]{1,0:T(8,128)(2,1)S(1)}, u32[]{:S(2)}, u32[]{:S(2)}) collective-permute-start(bf16[1024,128]{1,0:T(8,128)(2,1)S(1)} %get-tuple-element.152), channel_id=1, source_target_pairs={{16,0},{32,16},{48,32},{17,1},{33,17},{49,33},{18,2},{34,18},{50,3... | collective-permute-start | bytes 786440 | tf_op jit(solution)/shard_map/ppermute | solution.py:45
  325.3 30.7 %collective-permute-start.18 = (bf16[1024,128]{1,0:T(8,128)(2,1)S(1)}, bf16[1024,128]{1,0:T(8,128)(2,1)S(1)}, u32[]{:S(2)}, u32[]{:S(2)}) collective-permute-start(bf16[1024,128]{1,0:T(8,128)(2,1)S(1)} %get-tuple-element.153), channel_id=1, source_target_pairs={{48,0},{49,1},{50,2},{51,3},{52,4},{53,5},{54,6},{55,7},{56,8},{57... | collective-permute-start | bytes 786440 | tf_op jit(solution)/shard_map/ppermute | solution.py:45
  326.6 29.4 %collective-permute-start.17 = (bf16[1024,128]{1,0:T(8,128)(2,1)S(1)}, bf16[1024,128]{1,0:T(8,128)(2,1)S(1)}, u32[]{:S(2)}, u32[]{:S(2)}) collective-permute-start(bf16[1024,128]{1,0:T(8,128)(2,1)S(1)} %get-tuple-element.154), channel_id=1, source_target_pairs={{32,0},{48,16},{33,1},{49,17},{34,2},{50,18},{35,3},{51,19},{36,4}... | collective-permute-start | bytes 786440 | tf_op jit(solution)/shard_map/ppermute | solution.py:45
  328.4 27.7 %copy-start.45 = (f32[1024]{0:T(1024)S(1)}, f32[1024]{0:T(1024)}, u32[]{:S(2)}) copy-start(f32[1024]{0:T(1024)} %copy-done.44) | copy-start | bytes 12292
  328.4 27.7 %copy-start.64 = (f32[64]{0:T(128)S(1)}, f32[64]{0:T(128)}, u32[]{:S(2)}) copy-start(f32[64]{0:T(128)} %copy-done.63) | copy-start | bytes 772
  331.1 56.5 %collective-permute-start.11 = (bf16[2,512,8,128]{3,2,1,0:T(8,128)(2,1)}, bf16[2,512,8,128]{3,2,1,0:T(8,128)(2,1)}, u32[]{:S(2)}, u32[]{:S(2)}) collective-permute-start(bf16[2,512,8,128]{3,2,1,0:T(8,128)(2,1)} %dynamic-slice_bitcast_fusion), channel_id=1, source_target_pairs={{0,1},{1,0},{2,3},{3,2},{4,5},{5,4},{6,7},{7,6},{8,9},{9,8},{10,11... | collective-permute-start | bytes 6291464 | tf_op jit(solution)/shard_map/ppermute | solution.py:29
  376.1 11.6 %copy-start.9 = (bf16[2,512,8,2,128]{4,2,1,0,3:T(8,128)(2,1)S(1)}, bf16[2,512,8,2,128]{4,2,1,0,3:T(8,128)(2,1)}, u32[]{:S(2)}) copy-start(bf16[2,512,8,2,128]{4,2,1,0,3:T(8,128)(2,1)} %copy-done.8) | copy-start | bytes 12582916
  376.1 30.6 %collective-permute-start.21 = (bf16[512,2048]{1,0:T(8,128)(2,1)}, bf16[512,2048]{1,0:T(8,128)(2,1)}, u32[]{:S(2)}, u32[]{:S(2)}) collective-permute-start(bf16[512,2048]{1,0:T(8,128)(2,1)} %bitcast.48), channel_id=1, source_target_pairs={{0,1},{1,0},{2,3},{3,2},{4,5},{5,4},{6,7},{7,6},{8,9},{9,8},{10,11... | collective-permute-start | bytes 6291464 | tf_op jit(solution)/shard_map/ppermute | solution.py:29
  391.6 7.4 %copy-start.54 = (bf16[8,256]{1,0:T(8,128)(2,1)S(1)}, bf16[8,256]{1,0:T(8,128)(2,1)}, u32[]{:S(2)}) copy-start(bf16[8,256]{1,0:T(8,128)(2,1)} %reshape.403) | copy-start | bytes 12292
  391.6 33.4 %all-to-all-start.3 = ((bf16[8,1024,128]{2,1,0:T(8,128)(2,1)}), bf16[8,1024,128]{2,1,0:T(8,128)(2,1)S(1)}, u32[]{:S(2)}, u32[]{:S(2)}) async-start(bf16[8,1024,128]{2,1,0:T(8,128)(2,1)} %bitcast.158), calls=%async_computation.3 | async-start | bytes 4194304 | tf_op jit(solution)/shard_map/all_to_all | solution.py:49
  403.0 68.0 %collective-permute-start.19 = (bf16[1024,8,128]{2,1,0:T(8,128)(2,1)}, bf16[1024,8,128]{2,1,0:T(8,128)(2,1)}, u32[]{:S(2)}, u32[]{:S(2)}) collective-permute-start(bf16[1024,8,128]{2,1,0:T(8,128)(2,1)} %bitcast.148), channel_id=1, source_target_pairs={{0,1},{1,0},{2,3},{3,2},{4,5},{5,4},{6,7},{7,6},{8,9},{9,8},{10,11... | collective-permute-start | bytes 6291464 | tf_op jit(solution)/shard_map/ppermute | solution.py:29
  415.5 22.4 %copy-start.73 = (s32[64]{0:T(128)S(1)}, s32[64]{0:T(128)}, u32[]{:S(2)}) copy-start(s32[64]{0:T(128)} %param.21) | copy-start | bytes 772
  425.0 40.0 %all-to-all-start.10 = ((bf16[8,272,384]{2,1,0:T(8,128)(2,1)}), bf16[8,272,384]{2,1,0:T(8,128)(2,1)}, u32[]{:S(2)}, u32[]{:S(2)}) async-start(bf16[8,272,384]{2,1,0:T(8,128)(2,1)} %pad_maximum_fusion.3), calls=%async_computation.10 | async-start | bytes 3342336 | tf_op jit(solution)/shard_map/all_to_all | solution.py:49
  437.9 90.9 %all-gather.6.cloned.1.call-start = ((), (), s32[]{:S(2)}) async-start(), calls=%async_computation.14 | async-start | bytes 2359296 | tf_op jit(solution)/shard_map/all_gather | solution.py:414
  439.4 1.3 collective-permute-start.20
  465.0 15.5 %all-to-all-start.6 = ((bf16[16,64,128]{2,1,0:T(8,128)(2,1)}), bf16[16,64,128]{2,1,0:T(8,128)(2,1)S(1)}, u32[]{:S(2)}, u32[]{:S(2)}) async-start(bf16[16,64,128]{2,1,0:T(8,128)(2,1)} %bitcast_bitcast_fusion.1), calls=%async_computation.6 | async-start | bytes 524288 | tf_op jit(solution)/shard_map/all_to_all | solution.py:49
  481.1 11.8 %all-to-all-start.11 = ((f32[16,8,128]{2,1,0:T(8,128)}), f32[16,8,128]{2,1,0:T(8,128)S(1)}, u32[]{:S(2)}, u32[]{:S(2)}) async-start(f32[16,8,128]{2,1,0:T(8,128)} %broadcast_in_dim.50), calls=%async_computation.12 | async-start | bytes 131072 | tf_op jit(solution)/shard_map/all_to_all | solution.py:49
  492.9 33.4 %all-to-all-start.8 = ((bf16[8,1040,128]{2,1,0:T(8,128)(2,1)}), bf16[8,1040,128]{2,1,0:T(8,128)(2,1)S(1)}, u32[]{:S(2)}, u32[]{:S(2)}) async-start(bf16[8,1040,128]{2,1,0:T(8,128)(2,1)} %copy.220), calls=%async_computation.8 | async-start | bytes 4259840 | tf_op jit(solution)/shard_map/all_to_all | solution.py:49
  500.3 2.7 collective-permute-start.22
  526.6 7.2 %copy-start.1 = (s32[2,3]{1,0:T(2,128)S(1)}, s32[2,3]{1,0:T(2,128)}, u32[]{:S(2)}) copy-start(s32[2,3]{1,0:T(2,128)} %param.20) | copy-start | bytes 76
  (49 other events, 169.8 us)
Sparse Core Ops, SparseCore 0:
  10.3 58.3 all-gather.7
  70.3 64.2 all-gather.3
  300.7 92.2 reduce-scatter.1
  440.7 44.6 all-gather.5

commit v2 on v1

v2 whole, which is shorter than its diff:
```python
import jax
import jax.numpy as jnp
from jax import lax
from jax.experimental import pallas as pl
from jax.experimental.pallas import tpu as pltpu
from jax.sharding import Mesh, PartitionSpec as P

SPAN = 128
MICRO = 2
HD = 128
D = 2048
ROWS = 1024
KEYS = 4096
BLK = 256
KEY_BLK = 512

epsilon = 1e-06
rope_base = 1000000.0
score_scale = HD ** (-0.5)
log2e = 1.4426950408889634
bf16 = jnp.bfloat16
f32 = jnp.float32
SPANS = ("xl", "z")
TENSOR = ("xh", "y", "c")
CHIPS = ("xh", "y")
MIB = 1024 * 1024


def swap(block):
    return lax.ppermute(block, "c", [(0, 1), (1, 0)])


def far_span(block):
    return lax.ppermute(block, "xl", [(0, 1), (1, 0)])


def onward(block, by):
    return lax.ppermute(block, "z", [(i, i + by) for i in range(4) if i + by < 4])


def backward(block, by):
    return lax.ppermute(block, "z", [(i, i - by) for i in range(4) if i - by >= 0])


def exchange(block, axes):
    return lax.all_to_all(block, axes, 0, 0, tiled=True)


def spread(block, axes, count):
    return exchange(jnp.broadcast_to(block[None], (count,) + block.shape), axes)


def after(block, *earlier):
    return lax.optimization_barrier((block,) + earlier)[0]


def plain_dot(first_op, second_op):
    return jnp.dot(first_op, second_op, preferred_element_type=f32)


def left_dot(first_op, second_op):
    return lax.dot_general(
        first_op, second_op, (((0,), (0,)), ((), ())), preferred_element_type=f32
    )


def right_dot(first_op, second_op):
    return lax.dot_general(
        first_op, second_op, (((1,), (1,)), ((), ())), preferred_element_type=f32
    )


def inverse_rms(values):
    return lax.rsqrt(jnp.mean(values * values, axis=-1, keepdims=True) + epsilon)


def rotate_back(values, cos_table, sin_table):
    former, latter = values[..., :64], values[..., 64:]
    return jnp.concatenate(
        [former * cos_table + latter * sin_table, latter * cos_table - former * sin_table], axis=-1
    )


def norm_back(incoming, normal, inverse):
    return inverse * (incoming - normal * jnp.mean(incoming * normal, axis=-1, keepdims=True))


def block_mask(block, key_block, starts):
    key_at = key_block * KEY_BLK + lax.broadcasted_iota(jnp.int32, (KEY_BLK, BLK), 0)
    query_at = (KEYS - ROWS) + block * BLK + lax.broadcasted_iota(jnp.int32, (KEY_BLK, BLK), 1)
    return (key_at >= starts) & (key_at <= query_at)


def attend_kernel(low_ref, start_ref, q_ref, k_ref, v_ref, out_ref, full_ref, total_ref):
    for block in range(ROWS // BLK):
        cols = pl.ds(block * BLK, BLK)
        queries = q_ref[cols, :]
        starts = start_ref[:, cols]

        def step(key_block, state):
            acc, total = state
            rows = pl.ds(pl.multiple_of(key_block * KEY_BLK, KEY_BLK), KEY_BLK)
            scores = right_dot(k_ref[rows, :], queries) * (score_scale * log2e)
            weights = jnp.where(block_mask(block, key_block, starts), jnp.exp2(scores), 0.0)
            total = total + jnp.sum(weights, axis=0, keepdims=True)
            acc = acc + left_dot(v_ref[rows, :], weights.astype(bf16))
            return acc, total

        acc, total = lax.fori_loop(
            low_ref[block],
            (KEYS - ROWS + (block + 1) * BLK + KEY_BLK - 1) // KEY_BLK,
            step,
            (jnp.zeros((HD, BLK), f32), jnp.zeros((1, BLK), f32)),
        )
        full = acc / total
        full_ref[:, cols] = full
        total_ref[:, cols] = jnp.log2(total)
        out_ref[cols, :] = full.T.astype(bf16)


def attend(low, starts, queries, keys, values):
    vmem = pl.BlockSpec(memory_space=pltpu.VMEM)
    return pl.pallas_call(
        attend_kernel,
        out_shape=(
            jax.ShapeDtypeStruct((ROWS, HD), bf16),
            jax.ShapeDtypeStruct((HD, ROWS), f32),
            jax.ShapeDtypeStruct((1, ROWS), f32),
        ),
        in_specs=[pl.BlockSpec(memory_space=pltpu.SMEM)] + [vmem] * 4,
        out_specs=(vmem,) * 3,
        compiler_params=pltpu.CompilerParams(vmem_limit_bytes=16 * MIB),
        cost_estimate=pl.CostEstimate(
            flops=4 * ROWS * 2048 * HD, bytes_accessed=4 << 20, transcendentals=ROWS * 2048
        ),
        name="attend",
    )(low, starts, queries, keys, values)


def attend_back_kernel(
    low_ref,
    core_ref,
    start_ref,
    q_ref,
    k_ref,
    v_ref,
    do_ref,
    full_ref,
    total_ref,
    dq_ref,
    keep_ref,
    send_ref,
    dk_ref,
    dv_ref,
):
    dk_ref[...] = jnp.zeros_like(dk_ref)
    dv_ref[...] = jnp.zeros_like(dv_ref)
    for block in range(ROWS // BLK):
        cols = pl.ds(block * BLK, BLK)
        queries = q_ref[cols, :]
        starts = start_ref[:, cols]
        incoming = do_ref[cols, :]
        total = total_ref[:, cols]
        delta = jnp.sum(incoming.astype(f32).T * full_ref[:, cols], axis=0, keepdims=True)

        def step(key_block, acc):
            rows = pl.ds(pl.multiple_of(key_block * KEY_BLK, KEY_BLK), KEY_BLK)
            keys = k_ref[rows, :]
            scores = right_dot(keys, queries) * (score_scale * log2e)
            weights = jnp.where(
                block_mask(block, key_block, starts), jnp.exp2(scores - total), 0.0
            )
            grads = right_dot(v_ref[rows, :], incoming)
            grads = (weights * (grads - delta)).astype(bf16)
            dv_ref[rows, :] += plain_dot(weights.astype(bf16), incoming)
            dk_ref[rows, :] += plain_dot(grads, queries)
            return acc + left_dot(keys, grads)

        acc = lax.fori_loop(
            low_ref[block],
            (KEYS - ROWS + (block + 1) * BLK + KEY_BLK - 1) // KEY_BLK,
            step,
            jnp.zeros((HD, BLK), f32),
        )
        dq_ref[cols, :] = acc.T * score_scale

    @pl.when(core_ref[0] == 0)
    def _():
        keep_ref[...] = dk_ref[...] * score_scale
        send_ref[...] = dv_ref[...].astype(bf16)

    @pl.when(core_ref[0] == 1)
    def _():
        keep_ref[...] = dv_ref[...]
        send_ref[...] = (dk_ref[...] * score_scale).astype(bf16)


def attend_back(low, core, starts, queries, keys, values, incoming, full, total):
    vmem = pl.BlockSpec(memory_space=pltpu.VMEM)
    smem = pl.BlockSpec(memory_space=pltpu.SMEM)
    return pl.pallas_call(
        attend_back_kernel,
        out_shape=(
            jax.ShapeDtypeStruct((ROWS, HD), f32),
            jax.ShapeDtypeStruct((KEYS, HD), f32),
            jax.ShapeDtypeStruct((KEYS, HD), bf16),
        ),
        in_specs=[smem, smem] + [vmem] * 7,
        out_specs=(vmem,) * 3,
        scratch_shapes=[pltpu.VMEM((KEYS, HD), f32), pltpu.VMEM((KEYS, HD), f32)],
        compiler_params=pltpu.CompilerParams(vmem_limit_bytes=28 * MIB),
        cost_estimate=pl.CostEstimate(
            flops=10 * ROWS * 2048 * HD, bytes_accessed=8 << 20, transcendentals=ROWS * 2048
        ),
        name="attend_back",
    )(low, core, starts, queries, keys, values, incoming, full, total)


def colour_kernel(place_ref, column_ref, row_ref, out_ref):
    down_at = lax.broadcasted_iota(jnp.int32, (64, 64), 0)
    across_at = lax.broadcasted_iota(jnp.int32, (64, 64), 1)
    same_slots = (down_at >> 3) == (across_at >> 3)
    same_spans = (column_ref[...] >> 3) == (row_ref[...] >> 3)
    colour = jnp.zeros((64, 1), jnp.int32)
    for _ in range(3):
        colour_row = jnp.sum(
            jnp.where(down_at == across_at, colour, 0).astype(f32), axis=0, keepdims=True
        ).astype(jnp.int32)
        alike = colour == colour_row

        def partner(group):
            near = group & alike
            rank_down = jnp.sum(
                jnp.where(near & (across_at < down_at), 1.0, 0.0), axis=1, keepdims=True
            ).astype(jnp.int32)
            rank_across = jnp.sum(
                jnp.where(near & (down_at < across_at), 1.0, 0.0), axis=0, keepdims=True
            ).astype(jnp.int32)
            return jnp.where(near & ((rank_down ^ 1) == rank_across), 1.0, 0.0)

        by_slot = partner(same_slots)
        jump = plain_dot(by_slot, partner(same_spans))
        label = lax.broadcasted_iota(jnp.int32, (64, 128), 0).astype(f32)
        for turn in range(5):
            label = jnp.minimum(label, plain_dot(jump, label))
            if turn < 4:
                jump = plain_dot(jump, jump)
        bit = jnp.where(label > plain_dot(by_slot, label), 1, 0)
        colour = colour * 2 + bit[:, :1]
    colour_row = jnp.sum(
        jnp.where(down_at == across_at, colour, 0).astype(f32), axis=0, keepdims=True
    )
    own = place_ref[0]
    same_row = (down_at & 7) == (across_at & 7)
    slot_colour = jnp.sum(
        jnp.where(down_at == own * 8 + (across_at >> 3), colour, 0).astype(f32),
        axis=0,
        keepdims=True,
    ).astype(jnp.int32)
    owner = jnp.sum(
        jnp.where(same_slots & (colour == own), column_ref[...] >> 3, 0).astype(f32),
        axis=0,
        keepdims=True,
    ).astype(jnp.int32)
    span_colour = jnp.sum(
        jnp.where(row_ref[...] == own * 8 + (down_at >> 3), colour_row, 0.0),
        axis=1,
        keepdims=True,
    ).astype(jnp.int32)
    for index, match in enumerate(
        (
            slot_colour == (down_at >> 3),
            owner == (down_at >> 3),
            span_colour == (across_at >> 3),
        )
    ):
        out_ref[index] = jnp.where(match & same_row, 1.0, 0.0).astype(bf16)


def routes(place, span_order):
    vmem = pl.BlockSpec(memory_space=pltpu.VMEM)
    return pl.pallas_call(
        colour_kernel,
        out_shape=jax.ShapeDtypeStruct((3, 64, 64), bf16),
        in_specs=[pl.BlockSpec(memory_space=pltpu.SMEM), vmem, vmem],
        out_specs=vmem,
        name="routes",
    )(place.reshape(1), span_order.reshape(64, 1), span_order.reshape(1, 64))


def project_kernel(
    place_ref,
    rows_ref,
    gain_ref,
    query_ref,
    kv_ref,
    cos_ref,
    sin_ref,
    gain_query_ref,
    gain_key_ref,
    normed_ref,
    inverse_ref,
    query_out_ref,
    kv_out_ref,
    query_hat_ref,
    query_inv_ref,
    key_hat_ref,
    key_inv_ref,
):
    rows = rows_ref[...].astype(f32)
    inverse = inverse_rms(rows)
    normed = (rows * inverse * gain_ref[...]).astype(bf16)
    inverse_ref[...] = inverse
    normed_ref[...] = normed
    cos, sin = cos_ref[...], sin_ref[...]

    def turned(values):
        return values * cos + pltpu.roll(values, 64, 1) * sin

    kv = plain_dot(normed, kv_ref[...])
    inverse = inverse_rms(kv)
    hat = kv * inverse
    key_hat_ref[...] = hat
    key_inv_ref[...] = inverse
    key = turned(hat * gain_key_ref[...])
    kv_out_ref[...] = jnp.where(place_ref[0] == 0, key, kv).astype(bf16)
    query = plain_dot(normed, query_ref[...])
    inverse = inverse_rms(query)
    hat = query * inverse
    query_hat_ref[...] = hat
    query_inv_ref[...] = inverse
    query_out_ref[...] = turned(hat * gain_query_ref[...]).astype(bf16)


def project(core, rows, gain, query_weights, kv_weights, cos, sin, gain_query, gain_key):
    wide = pl.BlockSpec((256, D), lambda i: (i, 0))
    head = pl.BlockSpec((256, HD), lambda i: (i, 0))
    one = pl.BlockSpec((256, 1), lambda i: (i, 0))
    weight = pl.BlockSpec((D, HD), lambda i: (0, 0))
    small = pl.BlockSpec((1, HD), lambda i: (0, 0))
    column = pltpu.HBM((ROWS, 1), f32)
    return pl.pallas_call(
        project_kernel,
        grid=(4,),
        out_shape=(
            pltpu.HBM((ROWS, D), bf16),
            column,
            jax.ShapeDtypeStruct((ROWS, HD), bf16),
            jax.ShapeDtypeStruct((ROWS, HD), bf16),
            pltpu.HBM((ROWS, HD), f32),
            column,
            pltpu.HBM((ROWS, HD), f32),
            column,
        ),
        in_specs=[
            pl.BlockSpec(memory_space=pltpu.SMEM),
            wide,
            pl.BlockSpec((1, D), lambda i: (0, 0)),
            weight,
            weight,
            head,
            head,
            small,
            small,
        ],
        out_specs=(wide, one, head, head, head, one, head, one),
        compiler_params=pltpu.CompilerParams(vmem_limit_bytes=20 * MIB),
        cost_estimate=pl.CostEstimate(
            flops=4 * ROWS * D * HD, bytes_accessed=12 << 20, transcendentals=0
        ),
        name="project",
    )(core, rows, gain, query_weights, kv_weights, cos, sin, gain_query, gain_key)


def turned_columns(block):
    return jnp.concatenate(
        [block[:, at * 256 : at * 256 + 256] for at in (0, 4, 1, 5, 2, 6, 3, 7)], axis=1
    )


def turned_place(index):
    return (index % 2) * 4 + index // 2


def feed_kernel(normed_ref, grad_ref, near_ref, far_ref, act_ref, wide_ref, part_ref):
    normed, grad = turned_columns(normed_ref[...]), turned_columns(grad_ref[...])
    for index, weight_ref in enumerate((near_ref, far_ref)):
        gate = plain_dot(normed, weight_ref[:, :384])
        up = plain_dot(normed, weight_ref[:, 384:768])
        grad_act = plain_dot(grad, weight_ref[:, 768:])
        sigma = jax.nn.sigmoid(gate)
        silu = gate * sigma
        grad_gate = (grad_act * up * sigma * (1.0 + gate * (1.0 - sigma))).astype(bf16)
        grad_up = (grad_act * silu).astype(bf16)
        act_ref[:, index * 384 : index * 384 + 384] = (silu * up).astype(bf16)
        wide_ref[:, index * 768 : index * 768 + 384] = grad_gate
        wide_ref[:, index * 768 + 384 : index * 768 + 768] = grad_up
    part = right_dot(wide_ref[:, :768], near_ref[:, :768])
    part = part + right_dot(wide_ref[:, 768:], far_ref[:, :768])
    for index in range(8):
        at = turned_place(index) * 256
        part_ref[:, at : at + 256] = part[:, index * 256 : index * 256 + 256].astype(bf16)


def feed(normed, grad, near, far):
    tile = pl.BlockSpec((256, D), lambda i: (i, 0))
    weight = pl.BlockSpec((D, 1152), lambda i: (0, 0))
    return pl.pallas_call(
        feed_kernel,
        grid=(2,),
        out_shape=(
            jax.ShapeDtypeStruct((512, 768), bf16),
            jax.ShapeDtypeStruct((512, 1536), bf16),
            jax.ShapeDtypeStruct((512, D), bf16),
        ),
        in_specs=[tile, tile, weight, weight],
        out_specs=(
            pl.BlockSpec((256, 768), lambda i: (i, 0)),
            pl.BlockSpec((256, 1536), lambda i: (i, 0)),
            tile,
        ),
        compiler_params=pltpu.CompilerParams(vmem_limit_bytes=44 * MIB),
        cost_estimate=pl.CostEstimate(
            flops=2 * 512 * D * 3840, bytes_accessed=18 << 20, transcendentals=512 * 768
        ),
        name="feed",
    )(normed, grad, near, far)


def weights_grad_kernel(normed_ref, grad_ref, wide_ref, act_ref, *refs):
    came_ref, out_ref, wide_turned_ref, act_turned_ref = refs if len(refs) == 4 else (None, *refs)

    @pl.when(pl.program_id(0) == 0)
    def _():
        wide_turned_ref[...] = wide_ref[...].T
        act_turned_ref[...] = act_ref[...].T

    wide = plain_dot(wide_turned_ref[...], normed_ref[...])
    down = plain_dot(act_turned_ref[...], grad_ref[...])
    if came_ref is not None:
        wide = wide + came_ref[0, :768, :].astype(f32)
        down = down + came_ref[0, 768:, :].astype(f32)
    out_ref[0, :768, :] = wide.astype(bf16)
    out_ref[0, 768:, :] = down.astype(bf16)


def weights_grad(normed, grad, wide, act, half, came=None):
    tile = pl.BlockSpec((512, 256), lambda i: (0, i))
    out = pl.BlockSpec((1, 1152, 256), lambda i: (i % 4 * 2 + i // 4, 0, 0))
    return pl.pallas_call(
        weights_grad_kernel,
        grid=(8,),
        out_shape=jax.ShapeDtypeStruct((8, 1152, 256), bf16),
        in_specs=[
            tile,
            tile,
            pl.BlockSpec((512, 768), lambda i: (0, half)),
            pl.BlockSpec((512, 384), lambda i: (0, half)),
        ]
        + ([] if came is None else [out]),
        out_specs=out,
        scratch_shapes=[pltpu.VMEM((768, 512), bf16), pltpu.VMEM((384, 512), bf16)],
        compiler_params=pltpu.CompilerParams(vmem_limit_bytes=20 * MIB),
        cost_estimate=pl.CostEstimate(
            flops=2 * 512 * D * 1152, bytes_accessed=10 << 20, transcendentals=0
        ),
        name="weights_grad",
    )(normed, grad, wide, act, *(() if came is None else (came,)))


def down_kernel(place_ref, act_ref, near_ref, far_ref, hidden_ref, out_ref, total_ref):
    chip = place_ref[0]
    total = right_dot(act_ref[:, :384], near_ref[...])
    total_ref[...] = total + right_dot(act_ref[:, 384:], far_ref[...])

    @pl.when(pl.program_id(0) == chip // 4)
    def _():
        rows = pl.ds(pl.multiple_of((chip % 4) * 64, 64), 64)
        total_ref[rows, :] += turned_columns(hidden_ref[...])

    for index in range(8):
        cols = total_ref[:, index * 256 : index * 256 + 256]
        out_ref[turned_place(index)] = cols.astype(bf16)


def down(chip, act, near, far, hidden):
    weight = pl.BlockSpec((D, 384), lambda i: (0, 2))
    return pl.pallas_call(
        down_kernel,
        grid=(2,),
        out_shape=jax.ShapeDtypeStruct((8, 512, 256), bf16),
        in_specs=[
            pl.BlockSpec(memory_space=pltpu.SMEM),
            pl.BlockSpec((256, 768), lambda i: (i, 0)),
            weight,
            weight,
            pl.BlockSpec((64, D), lambda i: (0, 0)),
        ],
        out_specs=pl.BlockSpec((8, 256, 256), lambda i: (0, i, 0)),
        scratch_shapes=[pltpu.VMEM((256, D), f32)],
        compiler_params=pltpu.CompilerParams(vmem_limit_bytes=24 * MIB),
        cost_estimate=pl.CostEstimate(
            flops=2 * 512 * D * 768, bytes_accessed=8 << 20, transcendentals=0
        ),
        name="down",
    )(chip, act, near, far, hidden)


def input_part_kernel(
    place_ref,
    near_ref,
    far_ref,
    near_weight_ref,
    far_weight_ref,
    rows_ref,
    inverse_ref,
    gain_ref,
    hidden_ref,
    mlp_ref,
    head_ref,
    out_ref,
    total_ref,
    term_ref,
    sum_ref,
):
    step = pl.program_id(0)
    part = right_dot(near_ref[...], near_weight_ref[...])
    part = part + right_dot(far_ref[...], far_weight_ref[...])
    inverse = inverse_ref[...]
    gain = gain_ref[...]
    weighted = part * (rows_ref[...].astype(f32) * inverse)
    term = jnp.sum(weighted * gain, axis=1, keepdims=True) * (1.0 / D)
    term_ref[pl.ds(step, 1), :] = jnp.broadcast_to(term, (256, 128)).T[:1, :]
    sums = jnp.sum(weighted.reshape(32, 8, D), axis=0)

    @pl.when(step == 0)
    def _():
        sum_ref[...] = sums

    @pl.when(step > 0)
    def _():
        sum_ref[...] += sums

    total_ref[...] = part * (gain * inverse)
    hidden = hidden_ref[...]
    for span in range(2):
        own = pl.ds(pl.multiple_of(span * 128 + place_ref[0] * 16, 16), 16)
        total_ref[own, :] += hidden[span * 16 : span * 16 + 16, :]
    rows = pl.ds(pl.multiple_of(step * 256, 256), 256)
    for index in range(8):
        cols = total_ref[:, index * 256 : index * 256 + 256]
        out_ref[index, rows, :] = cols.astype(bf16)

    @pl.when(step == 1)
    def _():
        terms = term_ref[:2, :]
        coarse = terms.astype(bf16).astype(f32)
        totals = jnp.sum(sum_ref[...], axis=0, keepdims=True)
        extra = jnp.concatenate(
            [coarse, terms - coarse]
            + [totals[:, index * 256 : index * 256 + 256] for index in range(8)]
            + [mlp_ref[...], head_ref[...], jnp.zeros((11, 256), f32)],
            axis=0,
        ).astype(bf16)
        for index in range(8):
            out_ref[index, 512:, :] = extra


def input_part(place, near, far, near_weight, far_weight, rows, inverse, gain, hidden, mlp, head):
    def fixed(*shape):
        return pl.BlockSpec(shape, lambda i, place_ref: (0,) * len(shape))

    def tile(*shape):
        return pl.BlockSpec(shape, lambda i, place_ref: (i, 0))

    def own(*shape):
        return pl.BlockSpec(shape, lambda i, place_ref: (place_ref[1] * 2 + i, 0))

    return pl.pallas_call(
        input_part_kernel,
        out_shape=jax.ShapeDtypeStruct((8, 544, 256), bf16),
        grid_spec=pltpu.PrefetchScalarGridSpec(
            num_scalar_prefetch=1,
            grid=(2,),
            in_specs=[
                tile(256, 256),
                tile(256, 256),
                fixed(D, 256),
                fixed(D, 256),
                own(256, D),
                own(256, 1),
                fixed(1, D),
                tile(32, D),
                fixed(8, 256),
                fixed(1, 256),
            ],
            out_specs=fixed(8, 544, 256),
            scratch_shapes=[
                pltpu.VMEM((256, D), f32),
                pltpu.VMEM((8, 256), f32),
                pltpu.VMEM((8, D), f32),
            ],
        ),
        compiler_params=pltpu.CompilerParams(vmem_limit_bytes=28 * MIB),
        cost_estimate=pl.CostEstimate(
            flops=2 * ROWS * D * 256, bytes_accessed=8 << 20, transcendentals=0
        ),
        name="input_part",
    )(place, near, far, near_weight, far_weight, rows, inverse, gain, hidden, mlp, head)


def attention_grads_kernel(normed_ref, grad_ref, grad_out_ref, out_ref, turned_ref):
    @pl.when(pl.program_id(0) == 0)
    def _():
        turned_ref[...] = grad_ref[...].T

    out_ref[0, :256, :] = plain_dot(turned_ref[...], normed_ref[...]).astype(bf16)
    out_ref[0, 256:, :] = grad_out_ref[...]


def attention_grads(normed, grad_proj, grad_out):
    return pl.pallas_call(
        attention_grads_kernel,
        grid=(8,),
        out_shape=jax.ShapeDtypeStruct((8, 384, 256), bf16),
        in_specs=[
            pl.BlockSpec((ROWS, 256), lambda i: (0, i)),
            pl.BlockSpec((ROWS, 256), lambda i: (0, 0)),
            pl.BlockSpec((HD, 256), lambda i: (0, i)),
        ],
        out_specs=pl.BlockSpec((1, 384, 256), lambda i: (i % 4 * 2 + i // 4, 0, 0)),
        scratch_shapes=[pltpu.VMEM((256, ROWS), bf16)],
        compiler_params=pltpu.CompilerParams(vmem_limit_bytes=12 * MIB),
        cost_estimate=pl.CostEstimate(
            flops=2 * ROWS * D * 256, bytes_accessed=8 << 20, transcendentals=0
        ),
        name="attention_grads",
    )(normed, grad_proj, grad_out)


def body(
    inputs,
    out_grad,
    lengths,
    span_order,
    w_query,
    w_key,
    w_value,
    w_out,
    w_gate,
    w_up,
    w_down,
    norm_attn,
    norm_mlp,
    norm_query,
    norm_key,
):
    xl, z, xh, y, core = (lax.axis_index(name) for name in ("xl", "z", "xh", "y", "c"))
    span_place = xl * 4 + z
    chip = xh * 4 + y
    first = core == 0

    def by_core(near, far, axis=0):
        join = jnp.stack if axis is None else lambda parts: jnp.concatenate(parts, axis=axis)
        return jnp.where(first, join([near, far]), join([far, near]))

    def split(block):
        near = lax.dynamic_slice_in_dim(block, core * 512, 512, 0)
        far = lax.dynamic_slice_in_dim(block, (1 - core) * 512, 512, 0)
        return near, far

    def chip_major(block):
        return block.reshape(4, 8, 16, -1).transpose(1, 0, 2, 3).reshape(512, -1)

    def span_major(block):
        return block.reshape(8, 4, 16, -1).transpose(1, 0, 2, 3).reshape(512, -1)

    gains = jnp.concatenate([norm_attn, norm_mlp, norm_query, norm_key])
    gains = jnp.pad(gains, (0, 16 * 256 - 544)).reshape(16, 256)
    shard = jnp.concatenate(
        [jnp.concatenate([w_query, w_key, w_value], axis=1), gains], axis=0
    )
    spread_weights = spread(shard, SPANS, 8)
    qkv_weights = spread_weights[:, :256].reshape(D, 256)
    gains = spread_weights[:, 256:259].reshape(8, 768).astype(f32)
    gain_attn = gains[:, :256].reshape(1, D)
    gain_mlp = gains[:, 256:512].reshape(1, D)
    gain_query = gains[:, 512:528].reshape(1, HD)
    gain_key = gains[:, 528:544].reshape(1, HD)
    query_weights = qkv_weights[:, :128]
    key_half, value_half = qkv_weights[:, 128:192], qkv_weights[:, 192:256]
    other_half = swap(jnp.where(first, value_half, key_half))
    kv_weights = by_core(jnp.where(first, key_half, value_half), other_half, 1)

    route = routes(span_place, span_order)

    def reorder(index, rows):
        return plain_dot(route[index], rows).astype(bf16)

    moving = lax.dynamic_index_in_dim(
        out_grad.reshape(8, 16, 8, D), chip * 2 + core, 1, keepdims=False
    ).reshape(64, D)
    moving = reorder(0, moving).reshape(8, 8, D)
    spread_out = jnp.broadcast_to(w_out.reshape(1, 16, D), (8, 16, D))
    moving = jnp.concatenate([moving, spread_out], axis=1)
    moving = exchange(after(moving, qkv_weights), SPANS)
    gain_attn = after(gain_attn, moving)
    out_weights = moving[:, 8:].reshape(8, HD, 256)
    moving = moving[:, :8].reshape(64, D)

    ends = jnp.cumsum(lax.dynamic_index_in_dim(lengths, xl, 0, keepdims=False))
    offset = z * ROWS + jnp.arange(ROWS, dtype=jnp.int32)
    doc_start = jnp.where(offset >= ends[1], ends[1], jnp.where(offset >= ends[0], ends[0], 0))
    frequency = jnp.power(rope_base, -2.0 * jnp.arange(HD // 2, dtype=f32) / HD)
    angles = (offset - doc_start).astype(f32)[:, None] * frequency[None, :]
    cos_table, sin_table = jnp.cos(angles), jnp.sin(angles)
    starts = doc_start - (z - 3) * ROWS
    low = starts.reshape(ROWS // BLK, BLK)[:, 0] // KEY_BLK
    starts = starts.reshape(1, ROWS)

    normed, inverse_one, query_bf, own_kv, query_hat, query_inv, key_hat, key_inv = project(
        core.reshape(1),
        inputs,
        gain_attn,
        query_weights,
        kv_weights,
        jnp.concatenate([cos_table, cos_table], axis=1),
        jnp.concatenate([-sin_table, sin_table], axis=1),
        gain_query,
        gain_key,
    )
    moving = after(reorder(1, moving), own_kv)
    moving = exchange(moving.reshape(8, 8, D), SPANS).reshape(64, D)
    moving = reorder(2, moving).reshape(8, 8, D)
    near = lax.dynamic_slice_in_dim(moving, core * 4, 4, 0)
    far = lax.dynamic_slice_in_dim(moving, (1 - core) * 4, 4, 0)
    own_grad = by_core(near, swap(far), 1).reshape(64, D)
    grad_mine = spread(own_grad, CHIPS, 8).reshape(512, D)

    mine = jnp.concatenate(
        [onward(own_kv, 3), onward(own_kv, 2), onward(own_kv, 1), own_kv], axis=0
    )
    mine = after(mine, own_grad)
    other = swap(mine)
    all_keys = jnp.where(first, mine, other)
    all_values = jnp.where(first, other, mine)

    mlp_shard = after(jnp.concatenate([w_gate, w_up, w_down.T], axis=1), qkv_weights)
    far_shard = far_span(mlp_shard)
    mlp_shard = jnp.where(
        xl == 0,
        jnp.concatenate([mlp_shard, far_shard]),
        jnp.concatenate([far_shard, mlp_shard]),
    )
    near_weights = lax.all_gather(after(mlp_shard, mine), "z", axis=0, tiled=True)
    far_weights = swap(near_weights)

    out_weights = out_weights.transpose(1, 0, 2).reshape(HD, D)
    out_two = jnp.concatenate([out_weights, swap(out_weights)], axis=0)

    attended, attended_full, total = attend(low, starts, query_bf, all_keys, all_values)
    att_near, att_far = split(attended)
    att_two = jnp.concatenate(
        [chip_major(att_near), swap(chip_major(att_far))], axis=1
    )
    branch = plain_dot(att_two, out_two).astype(bf16)
    branch = after(branch, grad_mine).reshape(8, 64, D)
    branch = jnp.sum(exchange(branch, CHIPS).astype(f32), axis=0)
    own_rows = lax.dynamic_slice_in_dim(inputs, core * 512, 512, 0).reshape(4, 8, 16, D)
    own_rows = lax.dynamic_index_in_dim(own_rows, chip, 1, keepdims=False).reshape(64, D)
    hidden = own_rows.astype(f32) + branch
    inverse_two = inverse_rms(hidden)
    normal_two = hidden * inverse_two
    normed_mlp = (normal_two * gain_mlp).astype(bf16)
    normed_mine = spread(normed_mlp, CHIPS, 8).reshape(512, D)

    act, wide, part = feed(normed_mine, grad_mine, near_weights, far_weights)
    part = exchange(part.reshape(8, 64, D), CHIPS)
    came = swap(weights_grad(normed_mine, grad_mine, wide, act, 1))
    out_cols = down(chip.reshape(1), act, near_weights, far_weights, hidden)
    mlp_grads = weights_grad(normed_mine, grad_mine, wide, act, 0, came)
    part, mlp_grads, out_cols = lax.optimization_barrier((part, mlp_grads, out_cols))
    grad_normed_mlp = jnp.sum(part.astype(f32), axis=0)

    def scatter_weights(block):
        block = lax.psum_scatter(block, "z", scatter_dimension=0, tiled=True)
        sent = lax.dynamic_index_in_dim(block, 1 - xl, 0, keepdims=False)
        kept = lax.dynamic_index_in_dim(block, xl, 0, keepdims=False)
        return kept, sent

    mlp_grads, mlp_sent = scatter_weights(mlp_grads)

    gain_mlp_part = jnp.sum(grad_normed_mlp * normal_two, axis=0)
    grad_hidden = own_grad.astype(f32) + norm_back(
        grad_normed_mlp * gain_mlp, normal_two, inverse_two
    )
    branch_mine = spread(grad_hidden.astype(bf16), CHIPS, 8).reshape(512, D)
    grad_two = right_dot(branch_mine, out_two).astype(bf16)
    grad_att = by_core(span_major(grad_two[:, :HD]), span_major(swap(grad_two[:, HD:])))

    out_cols = exchange(after(out_cols, branch_mine), CHIPS)
    out_cols = jnp.sum(out_cols.astype(f32), axis=0).astype(bf16)
    near = jnp.where(first, out_cols[:, :128], out_cols[:, 128:])
    far = jnp.where(first, out_cols[:, 128:], out_cols[:, :128])
    out_cols = by_core(near, swap(far), None).reshape(2, 8, 4, 2, 8, 128)
    out_rows = jnp.concatenate(
        [out_cols[:, index // 2, :, index % 2].reshape(64, 128) for index in range(16)], axis=1
    )

    def unorder(index, rows):
        return left_dot(route[index], rows).astype(bf16)

    out_rows = exchange(unorder(2, out_rows).reshape(8, 8, D), SPANS).reshape(64, D)
    out_rows = unorder(1, out_rows).reshape(8, 8, D)

    grad_query_rot, keep, send = attend_back(
        low,
        core.reshape(1),
        starts,
        query_bf,
        all_keys,
        all_values,
        grad_att,
        attended_full,
        total,
    )
    grad_out = left_dot(att_two, branch_mine)
    grad_out = (grad_out[:HD] + swap(grad_out[HD:].astype(bf16)).astype(f32)).astype(bf16)
    grad_kv = (keep + swap(send).astype(f32)).reshape(4, ROWS, HD)
    away = grad_kv.astype(bf16)
    grad_kv = (
        grad_kv[3]
        + backward(away[2], 1).astype(f32)
        + backward(away[1], 2).astype(f32)
        + backward(away[0], 3).astype(f32)
    )
    grad_kv = after(grad_kv, mlp_sent)
    query_norm_grad = rotate_back(grad_query_rot, cos_table, sin_table)
    gain_query_part = jnp.sum(query_norm_grad * query_hat, axis=0)
    grad_query_proj = norm_back(query_norm_grad * gain_query, query_hat, query_inv)
    key_norm_grad = rotate_back(grad_kv, cos_table, sin_table)
    gain_key_part = jnp.where(first, jnp.sum(key_norm_grad * key_hat, axis=0), 0.0)
    grad_key_proj = norm_back(key_norm_grad * gain_key, key_hat, key_inv)
    grad_kv_proj = jnp.where(first, grad_key_proj, grad_kv)
    grad_proj = jnp.concatenate([grad_query_proj.astype(bf16), grad_kv_proj.astype(bf16)], axis=1)

    grad_near, grad_far = split(grad_proj)
    near_weight = jnp.concatenate([query_weights, kv_weights], axis=1)
    by_cols = input_part(
        jnp.stack([chip, core]),
        grad_near,
        swap(grad_far),
        near_weight,
        swap(near_weight),
        inputs,
        inverse_one,
        gain_attn,
        grad_hidden,
        gain_mlp_part.reshape(8, 256),
        jnp.concatenate([gain_query_part, gain_key_part]).reshape(1, 256),
    )
    grad_proj = after(grad_proj, by_cols)
    by_cols = jnp.sum(exchange(by_cols, CHIPS).astype(f32), axis=0)
    row_term = (by_cols[512:514] + by_cols[514:516]).reshape(512, 1)
    own_inverse = lax.dynamic_slice_in_dim(inverse_one, core * 512, 512, 0)
    own_cols = lax.dynamic_slice(inputs, (core * 512, chip * 256), (512, 256)).astype(f32)
    in_grad = by_cols[:512] - own_cols * (own_inverse * own_inverse * row_term)
    near = jnp.where(first, in_grad[:, :128], in_grad[:, 128:])
    far = jnp.where(first, in_grad[:, 128:], in_grad[:, :128])
    in_grad = by_core(near, swap(far))
    gain_sums = jnp.concatenate(
        [
            by_cols[516:524],
            by_cols[524:532],
            by_cols[532, :128].reshape(8, 16),
            by_cols[532, 128:].reshape(8, 16),
        ],
        axis=1,
    )
    gain_sums = gain_sums + swap(gain_sums)
    coarse = gain_sums.astype(bf16)
    extra = jnp.concatenate(
        [coarse, (gain_sums - coarse.astype(f32)).astype(bf16), jnp.zeros((8, 960), bf16)], axis=1
    )
    extra = jnp.pad(extra[:, None], ((0, 0), (0, 7), (0, 0)))
    out_rows = exchange(jnp.concatenate([out_rows, extra], axis=1), SPANS)
    gain_sums = jnp.sum(out_rows[:, 8].astype(f32), axis=0)
    gain_sums = gain_sums[:544] + gain_sums[544:1088]
    layer_out = unorder(0, out_rows[:, :8].reshape(64, D))
    layer_out = jnp.stack(
        [layer_out[:, at * 128 : at * 128 + 128].reshape(8, 8, 128) for at in range(16)],
        axis=1,
    )
    layer_out = layer_out.reshape(ROWS, 128).astype(f32)

    grad_attn = attention_grads(normed, grad_proj, grad_out)
    grad_attn, attn_sent = scatter_weights(grad_attn)
    grad_attn = grad_attn.astype(f32) + far_span(attn_sent).astype(f32)
    grad_kv_weight = grad_attn[128:256]
    low_half, high_half = grad_kv_weight[:64], grad_kv_weight[64:]
    came = swap(jnp.where(first, high_half, low_half))
    kept = jnp.where(first, low_half, high_half)
    mlp_grads = mlp_grads.astype(f32) + far_span(after(mlp_sent, by_cols)).astype(f32)

    return (
        layer_out,
        in_grad,
        grad_attn[:128].T,
        jnp.where(first, kept, came).T,
        jnp.where(first, came, kept).T,
        grad_attn[256:],
        mlp_grads[:384].T,
        mlp_grads[384:768].T,
        mlp_grads[768:],
        gain_sums[:256],
        gain_sums[256:512],
        gain_sums[512:528],
        gain_sums[528:544],
    )


def solution(mesh):
    fine = Mesh(mesh.devices.reshape(2, 4, 2, 4, 2), ("xl", "z", "xh", "y", "c"))
    rows = P(SPANS, None)
    by_both = P(SPANS, TENSOR)
    turned = P(TENSOR, SPANS)
    lone = P(SPANS)
    return jax.shard_map(
        body,
        mesh=fine,
        in_specs=(
            rows,
            rows,
            P(),
            P(),
            by_both,
            by_both,
            by_both,
            turned,
            by_both,
            by_both,
            turned,
            lone,
            lone,
            lone,
            lone,
        ),
        out_specs=(
            by_both,
            by_both,
            by_both,
            by_both,
            by_both,
            turned,
            by_both,
            by_both,
            turned,
            lone,
            lone,
            lone,
            lone,
        ),
        check_vma=False,
    )
```

time: 551 us -> 466 us (0.85)
  the two profiles are of different devices: /device:TPU:6 before, /device:TPU:1 now
where the time goes in v2:
time: 466 us; the launch traced here: 457 us
  waiting for transfers between devices  115 us (25%)
  starting transfers between devices  95.1 us (20%)
  Pallas kernels  66.2 us (14%)
  blocking collectives  63.8 us (14%)
  other arithmetic  50 us (11%)
  local copies, waits for them, and re-layouts  41.1 us (9%)
  between operations  15.5 us (3%)
  matrix products  9.96 us (2%)
    all_to_all x10, waiting for transfers between devices, exchange(): return lax.all_to_all(block, axes, 0, 0, tiled=True)  72.1 us
    all_to_all x2, blocking collectives, exchange(): return lax.all_to_all(block, axes, 0, 0, tiled=True)  63.8 us
    all_to_all x10, starting transfers between devices, exchange(): return lax.all_to_all(block, axes, 0, 0, tiled=True)  59.5 us
    unnamed x152, local copies, waits for them, and re-layouts  19.6 us
    ppermute x16, starting transfers between devices, swap(): return lax.ppermute(block, 'c', [(0, 1), (1, 0)])  18.9 us
    pallas_call x1, Pallas kernels, feed(): pl.pallas_call(feed_kernel, grid=(2,), out_shape=(jax.ShapeDtypeStruct((5...  15.2 us
    all_gather x1, waiting for transfers between devices, body(): lax.all_gather(after(mlp_shard, mine), 'z', axis=0, tiled=True)  14.9 us
    pallas_call x2, Pallas kernels, weights_grad(): pl.pallas_call(weights_grad_kernel, grid=(8,), out_shape=jax.ShapeDtypeSt...  14.3 us
  transfers between devices with their start and end apart: 38, of which 17 were waited for; matrix products, arithmetic and copies ran while one was open for 17% of the time, Pallas kernels for 10%

profile of v2, /device:TPU:1, one launch (start us, length us, event | category | flops | bytes accessed | tf_op | source)
XLA Modules:
  0.0 456.6 jit_solution(7137740571155735210)
XLA Ops:
  11.9 6.8 %all-to-all-start = ((bf16[8,272,256]{2,1,0:T(8,128)(2,1)}), bf16[8,272,256]{2,1,0:T(8,128)(2,1)}, u32[]{:S(2)}, u32[]{:S(2)}) async-start(bf16[8,272,256]{2,1,0:T(8,128)(2,1)} %broadcast_in_dim.60), calls=%async_computation | async-start | bytes 2228224 | tf_op jit(solution)/shard_map/all_to_all | solution.py:46
  21.7 4.6 %routes.1 = bf16[3,64,64]{2,1,0:T(8,128)(2,1)} custom-call(s32[1]{0:T(128)} %bitcast.place_ref, s32[64,1]{1,0:T(8,128)} %copy.73.column_ref, s32[1,64]{1,0:T(1,128)} %bitcast.280), custom_call_target="tpu_custom_call" | custom-call | tf_op jit(solution)/shard_map/routes/pallas_call | solution.py:282
  27.5 1.9 fusion.10
  31.7 2.7 all-to-all-done
  35.7 4.2 all-to-all-start.1
  42.6 1.7 collective-permute-start.8
  44.6 2.2 maximum_select_fusion.1.kv_ref
  46.8 4.6 %all-to-all-done.1 = bf16[8,24,2048]{2,1,0:T(8,128)(2,1)} async-done(((bf16[8,24,2048]{2,1,0:T(8,128)(2,1)}), bf16[8,24,2048]{2,1,0:T(8,128)(2,1)}, u32[]{:S(2)}, u32[]{:S(2)}) %all-to-all-start.1) | async-done | bytes 786464 | tf_op jit(solution)/shard_map/all_to_all | solution.py:46
  51.4 2.2 copy-done.2
  53.6 5.7 %project.1 = (bf16[1024,2048]{1,0:T(8,128)(2,1)}, f32[1024,1]{1,0:T(8,128)}, bf16[1024,128]{1,0:T(8,128)(2,1)S(1)}, bf16[1024,128]{1,0:T(8,128)(2,1)S(1)}, f32[1...) custom-call(s32[1]{0:T(128)} %bitcast.12.place_ref.core_ref, ...), custom_call_target="tpu_custom_call" | custom-call | flops 1073741824 | bytes 12582912 | tf_op jit(solution)/shard_map/project/pallas_call | solution.py:342
  59.3 2.0 convolution_convert_fusion.5
  61.3 4.3 all-to-all-start.2
  65.6 3.0 maximum_select_fusion
  68.6 4.5 collective-permute-start.1
  74.5 2.5 collective-permute-start.3
  77.2 2.4 collective-permute-start.4
  79.7 3.4 collective-permute-done.1
  85.0 2.8 collective-permute-start.5
  87.8 1.6 broadcast_in_dim.64
  89.4 6.4 %all-to-all-start.3 = ((bf16[8,64,2048]{2,1,0:T(8,128)(2,1)}), bf16[8,64,2048]{2,1,0:T(8,128)(2,1)S(1)}, u32[]{:S(2)}, u32[]{:S(2)}) async-start(bf16[8,64,2048]{2,1,0:T(8,128)(2,1)} %broadcast_in_dim.64), calls=%async_computation.3 | async-start | bytes 4194304 | tf_op jit(solution)/shard_map/all_to_all | solution.py:46
  102.3 1.7 broadcast_select_fusion
  104.0 3.8 attend.1
  110.2 2.1 convolution_convert_fusion
  112.4 9.7 %all-to-all-done.3 = bf16[8,64,2048]{2,1,0:T(8,128)(2,1)S(1)} async-done(((bf16[8,64,2048]{2,1,0:T(8,128)(2,1)}), bf16[8,64,2048]{2,1,0:T(8,128)(2,1)S(1)}, u32[]{:S(2)}, u32[]{:S(2)}) %all-to-all-start.3) | async-done | bytes 2097184 | tf_op jit(solution)/shard_map/all_to_all | solution.py:46
  122.1 5.0 %all-to-all-start.4 = ((bf16[8,64,2048]{2,1,0:T(8,128)(2,1)}), bf16[8,64,2048]{2,1,0:T(8,128)(2,1)}, u32[]{:S(2)}, u32[]{:S(2)}) async-start(bf16[8,64,2048]{2,1,0:T(8,128)(2,1)} %bitcast.238), calls=%async_computation.4 | async-start | bytes 4194304 | tf_op jit(solution)/shard_map/all_to_all | solution.py:46
  127.2 14.9 %all-gather.2.cloned.1.call-done.near_ref = bf16[2048,1152]{1,0:T(8,128)(2,1)} async-done(((bf16[512,1152]{1,0:T(8,128)(2,1)}), bf16[2048,1152]{1,0:T(8,128)(2,1)}) %all-gather.2.cloned.1.call-update) | async-done | bytes 4718608 | tf_op jit(solution)/shard_map/all_gather | solution.py:755
  142.7 1.7 constant_dynamic-slice_fusion.5
  146.7 6.8 %all-to-all-done.4 = bf16[8,64,2048]{2,1,0:T(8,128)(2,1)} async-done(((bf16[8,64,2048]{2,1,0:T(8,128)(2,1)}), bf16[8,64,2048]{2,1,0:T(8,128)(2,1)}, u32[]{:S(2)}, u32[]{:S(2)}) %all-to-all-start.4) | async-done | bytes 2097184 | tf_op jit(solution)/shard_map/all_to_all | solution.py:46
  153.4 2.0 convert_reduce_fusion.2
  158.3 31.9 %all_to_all.60 = bf16[8,64,2048]{2,1,0:T(8,128)(2,1)S(1)} all-to-all(bf16[8,64,2048]{2,1,0:T(8,128)(2,1)S(1)} %broadcast_in_dim.65), channel_id=1, replica_groups=mesh['xl'=2,'z'=4,'xh'=2,'y'=4,'c'=2] {'xh','y'}, dimensions={0} | all-to-all | bytes 4194304 | tf_op jit(solution)/shard_map/all_to_all | solution.py:46
  190.2 15.2 %feed.1 = (bf16[512,768]{1,0:T(8,128)(2,1)S(1)}, bf16[512,1536]{1,0:T(8,128)(2,1)S(1)}, bf16[512,2048]{1,0:T(8,128)(2,1)S(1)}) custom-call(bf16[512,2048]{1,0:T(8,128)(2,1)S(1)} %bitcast.220, bf16[512,2048]{1,0:T(8,128)(2,1)S(1)} %bitcast.217, bf16[2048,1152]{1,0:T(8,128)(2,1)} %all-gather.2.cloned.1.call-done.near_ref, ...), custom_call_target="tpu_custom_call" | custom-call | flops 8053063680 | bytes 18874368 | tf_op jit(solution)/shard_map/feed/pallas_call | solution.py:408
  205.4 1.4 copy-done.15
  206.8 6.6 %weights_grad.2 = bf16[8,1152,256]{2,1,0:T(8,128)(2,1)} custom-call(bf16[512,2048]{1,0:T(8,128)(2,1)S(1)} %bitcast.221, bf16[512,2048]{1,0:T(8,128)(2,1)S(1)} %bitcast.218, bf16[512,1536]{1,0:T(8,128)(2,1)S(1)} %get-tuple-element.55.wide_ref, bf16[512,768]{1,0:T(8,128)(2,1)S(1)} %get-tuple-element.56.act_ref), custom_call_target="tpu_custom_call" | custom-call | flops 2415919104 | bytes 10485760 | tf_op jit(solution)/shard_map/weights_grad/pallas_call | solution.py:450
  213.4 2.4 collective-permute-start.10
  215.9 4.3 all-to-all-start.6
  220.3 2.3 copy-done.9
  222.6 5.6 %down.1 = bf16[8,512,256]{2,1,0:T(8,128)(2,1)} custom-call(s32[1]{0:T(128)} %bitcast.37.place_ref, bf16[512,768]{1,0:T(8,128)(2,1)S(1)} %get-tuple-element.56.act_ref, bf16[2048,1152]{1,0:T(8,128)(2,1)S(1)} %copy-done.9, bf16[2048,1152]{1,0:T(8,128)(2,1)} %collective-permute-done.9.far_ref, f32[64,2048]{1,0:T(8,128)S(1)} %get-tuple-element.140.hidden_ref), custom_call_target="tpu_custom_call" | custom-call | flops 1610612736 | bytes 8388608 | tf_op jit(solution)/shard_map/down/pallas_call | solution.py:488
  228.2 7.7 %weights_grad.3 = bf16[8,1152,256]{2,1,0:T(8,128)(2,1)S(1)} custom-call(bf16[512,2048]{1,0:T(8,128)(2,1)S(1)} %bitcast.222, bf16[512,2048]{1,0:T(8,128)(2,1)S(1)} %bitcast.219, bf16[512,1536]{1,0:T(8,128)(2,1)S(1)} %copy-done.8, bf16[512,768]{1,0:T(8,128)(2,1)S(1)} %get-tuple-element.56.act_ref, bf16[8,1152,256]{2,1,0:T(8,128)(2,1)} %collective-permute-done.10.refs_0_), custom_call_target="tpu_custom_call" | custom-call | flops 2415919104 | bytes 10485760 | tf_op jit(solution)/shard_map/weights_grad/pallas_call | solution.py:450
  235.9 2.2 copy-done.6
  238.1 8.6 %all-to-all-done.6 = bf16[8,64,2048]{2,1,0:T(8,128)(2,1)} async-done(((bf16[8,64,2048]{2,1,0:T(8,128)(2,1)}), bf16[8,64,2048]{2,1,0:T(8,128)(2,1)}, u32[]{:S(2)}, u32[]{:S(2)}) %all-to-all-start.6) | async-done | bytes 2097184 | tf_op jit(solution)/shard_map/all_to_all | solution.py:46
  246.8 2.1 convert_reduce_fusion.1
  251.6 31.9 %all_to_all.61 = bf16[8,64,2048]{2,1,0:T(8,128)(2,1)S(1)} all-to-all(bf16[8,64,2048]{2,1,0:T(8,128)(2,1)S(1)} %broadcast_in_dim.66), channel_id=1, replica_groups=mesh['xl'=2,'z'=4,'xh'=2,'y'=4,'c'=2] {'xh','y'}, dimensions={0} | all-to-all | bytes 4194304 | tf_op jit(solution)/shard_map/all_to_all | solution.py:46
  284.8 2.5 collective-permute-start.12
  288.4 6.0 %attend_back.1 = (f32[1024,128]{1,0:T(8,128)S(1)}, f32[4096,128]{1,0:T(8,128)S(1)}, bf16[4096,128]{1,0:T(8,128)(2,1)}) custom-call(s32[4]{0:T(128)S(1)} %and_select_fusion.low_ref, s32[1]{0:T(128)} %bitcast.12.place_ref.core_ref, s32[1,1024]{1,0:T(1,128)S(1)} %fusion.40.start_ref, bf16[1024,128]{1,0:T(8,128)(2,1)S(1)} %copy-done.23, ...), custom_call_target="tpu_custom_call" | custom-call | flops 2684354560 | bytes 8388608 | tf_op jit(solution)/shard_map/attend_back/pallas_call | solution.py:201
  294.8 4.4 all-to-all-start.8
  299.5 2.9 fusion.51
  308.0 17.5 %all-to-all-done.8 = bf16[8,512,256]{2,1,0:T(8,128)(2,1)} async-done(((bf16[8,512,256]{2,1,0:T(8,128)(2,1)}), bf16[8,512,256]{2,1,0:T(8,128)(2,1)}, u32[]{:S(2)}, u32[]{:S(2)}) %all-to-all-start.8) | async-done | bytes 2097184 | tf_op jit(solution)/shard_map/all_to_all | solution.py:46
  325.5 2.0 reduce_sum.121
  332.3 13.8 %all-to-all-start.9 = ((bf16[8,8,2048]{2,1,0:T(8,128)(2,1)}), bf16[8,8,2048]{2,1,0:T(8,128)(2,1)S(1)}, u32[]{:S(2)}, u32[]{:S(2)}) async-start(bf16[8,8,2048]{2,1,0:T(8,128)(2,1)} %fusion.2), calls=%async_computation.9 | async-start | bytes 524288 | tf_op jit(solution)/shard_map/all_to_all | solution.py:46
  346.1 1.9 dynamic-slice_bitcast_fusion
  348.0 2.5 fusion.17
  354.0 6.1 %input_part.1 = bf16[8,544,256]{2,1,0:T(8,128)(2,1)} custom-call(s32[2]{0:T(128)S(1)} %pad_add_fusion.place_ref, bf16[512,256]{1,0:T(8,128)(2,1)S(1)} %get-tuple-element.160.near_ref, bf16[512,256]{1,0:T(8,128)(2,1)S(1)} %collective-permute-done.17.far_ref, bf16[2048,256]{1,0:T(8,128)(2,1)S(1)} %pad_maximum_fusion.2.near_weight_ref, ...), custom_call_target="tpu_custom_call" | custom-call | flops 1073741824 | bytes 8388608 | tf_op jit(solution)/shard_map/input_part/pallas_call | solution.py:579
  360.1 5.5 %all-to-all-start.10 = ((bf16[8,544,256]{2,1,0:T(8,128)(2,1)}), bf16[8,544,256]{2,1,0:T(8,128)(2,1)}, u32[]{:S(2)}, u32[]{:S(2)}) async-start(bf16[8,544,256]{2,1,0:T(8,128)(2,1)} %input_part.1), calls=%async_computation.11 | async-start | bytes 4456448 | tf_op jit(solution)/shard_map/all_to_all | solution.py:46
  365.6 2.3 fusion.29
  371.1 22.1 %all-to-all-done.10 = bf16[8,544,256]{2,1,0:T(8,128)(2,1)} async-done(((bf16[8,544,256]{2,1,0:T(8,128)(2,1)}), bf16[8,544,256]{2,1,0:T(8,128)(2,1)}, u32[]{:S(2)}, u32[]{:S(2)}) %all-to-all-start.10) | async-done | bytes 2228256 | tf_op jit(solution)/shard_map/all_to_all | solution.py:46
  393.3 2.0 convert_reduce_fusion
  400.2 4.7 %all-to-all-start.11 = ((bf16[8,16,2048]{2,1,0:T(8,128)(2,1)}), bf16[8,16,2048]{2,1,0:T(8,128)(2,1)S(1)}, u32[]{:S(2)}, u32[]{:S(2)}) async-start(bf16[8,16,2048]{2,1,0:T(8,128)(2,1)} %copy.86), calls=%async_computation.12 | async-start | bytes 1048576 | tf_op jit(solution)/shard_map/all_to_all | solution.py:46
  406.2 2.2 copy-done.14
  408.4 4.9 %attention_grads.1 = bf16[8,384,256]{2,1,0:T(8,128)(2,1)} custom-call(bf16[1024,2048]{1,0:T(8,128)(2,1)S(1)} %copy-done.14, bf16[1024,256]{1,0:T(8,128)(2,1)S(1)} %pad_maximum_fusion.6.grad_ref, bf16[128,2048]{1,0:T(8,128)(2,1)S(1)} %fusion.4.grad_out_ref), custom_call_target="tpu_custom_call" | custom-call | flops 1073741824 | bytes 8388608 | tf_op jit(solution)/shard_map/attention_grads/pallas_call | solution.py:622
  413.4 1.5 collective-permute-start.24
  414.9 1.9 maximum_select_fusion.2
  419.5 8.2 %collective-permute-done.24 = bf16[1152,256]{1,0:T(8,128)(2,1)} collective-permute-done((bf16[1152,256]{1,0:T(8,128)(2,1)S(1)}, bf16[1152,256]{1,0:T(8,128)(2,1)}, u32[]{:S(2)}, u32[]{:S(2)}) %collective-permute-start.24) | collective-permute-done | bytes 589856 | tf_op jit(solution)/shard_map/ppermute | solution.py:34
  428.9 10.2 %reduce-scatter.5.cloned.1.call-done = bf16[2,384,256]{2,1,0:T(8,128)(2,1)} async-done(((bf16[8,384,256]{2,1,0:T(8,128)(2,1)}), bf16[2,384,256]{2,1,0:T(8,128)(2,1)}) %reduce-scatter.5.cloned.1.call-update) | async-done | bytes 393232 | tf_op jit(solution)/shard_map/reduce_scatter | solution.py:786
  445.2 2.4 collective-permute-start.23
  (304 shorter events, 74.1 us)
Async XLA Ops:
  7.2 11.5 %copy-start = (s32[2,3]{1,0:T(2,128)S(1)}, s32[2,3]{1,0:T(2,128)}, u32[]{:S(2)}) copy-start(s32[2,3]{1,0:T(2,128)} %param.17) | copy-start | bytes 76
  7.2 12.3 %copy-start.52 = (s32[64]{0:T(128)S(1)}, s32[64]{0:T(128)}, u32[]{:S(2)}) copy-start(s32[64]{0:T(128)} %param.18) | copy-start | bytes 772
  7.2 13.0 %copy-start.51 = (bf16[128,256]{1,0:T(8,128)(2,1)S(1)}, bf16[128,256]{1,0:T(8,128)(2,1)}, u32[]{:S(2)}) copy-start(bf16[128,256]{1,0:T(8,128)(2,1)} %param.22) | copy-start | bytes 196612
  8.1 12.1 %copy-start.48 = (bf16[384,256]{1,0:T(8,128)(2,1)S(1)}, bf16[384,256]{1,0:T(8,128)(2,1)}, u32[]{:S(2)}) copy-start(bf16[384,256]{1,0:T(8,128)(2,1)} %param.25) | copy-start | bytes 589828
  11.9 22.5 %all-to-all-start = ((bf16[8,272,256]{2,1,0:T(8,128)(2,1)}), bf16[8,272,256]{2,1,0:T(8,128)(2,1)}, u32[]{:S(2)}, u32[]{:S(2)}) async-start(bf16[8,272,256]{2,1,0:T(8,128)(2,1)} %broadcast_in_dim.60), calls=%async_computation | async-start | bytes 2228224 | tf_op jit(solution)/shard_map/all_to_all | solution.py:46
  35.7 15.7 %all-to-all-start.1 = ((bf16[8,24,2048]{2,1,0:T(8,128)(2,1)}), bf16[8,24,2048]{2,1,0:T(8,128)(2,1)}, u32[]{:S(2)}, u32[]{:S(2)}) async-start(bf16[8,24,2048]{2,1,0:T(8,128)(2,1)} %pad_maximum_fusion.3), calls=%async_computation.1 | async-start | bytes 1572864 | tf_op jit(solution)/shard_map/all_to_all | solution.py:46
  41.7 2.9 collective-permute-start
  42.6 23.0 %collective-permute-start.8 = (bf16[256,1152]{1,0:T(8,128)(2,1)}, bf16[256,1152]{1,0:T(8,128)(2,1)}, u32[]{:S(2)}, u32[]{:S(2)}) collective-permute-start(bf16[256,1152]{1,0:T(8,128)(2,1)} %pad_maximum_fusion.7), channel_id=1, source_target_pairs={{0,64},{64,0},{1,65},{65,1},{2,66},{66,2},{3,67},{67,3},{4,68},{68... | collective-permute-start | bytes 1769480 | tf_op jit(solution)/shard_map/ppermute | solution.py:34
  44.4 14.9 %copy-start.10 = (bf16[2048,128]{1,0:T(8,128)(2,1)}, bf16[2048,128]{1,0:T(8,128)(2,1)S(1)}, u32[]{:S(2)}) copy-start(bf16[2048,128]{1,0:T(8,128)(2,1)S(1)} %slice.374.query_ref) | copy-start | bytes 1572868
  46.8 12.5 %copy-start.12 = (bf16[2048,128]{1,0:T(8,128)(2,1)}, bf16[2048,128]{1,0:T(8,128)(2,1)S(1)}, u32[]{:S(2)}) copy-start(bf16[2048,128]{1,0:T(8,128)(2,1)S(1)} %maximum_select_fusion.1.kv_ref) | copy-start | bytes 1572868
  53.6 5.7 %copy-start.44 = (bf16[3,64,64]{2,1,0:T(8,128)(2,1)S(1)}, bf16[3,64,64]{2,1,0:T(8,128)(2,1)}, u32[]{:S(2)}) copy-start(bf16[3,64,64]{2,1,0:T(8,128)(2,1)} %routes.1) | copy-start | bytes 73732
  59.3 44.7 %copy-start.22 = (bf16[1024,128]{1,0:T(8,128)(2,1)}, bf16[1024,128]{1,0:T(8,128)(2,1)S(1)}, u32[]{:S(2)}) copy-start(bf16[1024,128]{1,0:T(8,128)(2,1)S(1)} %get-tuple-element.46.q_ref) | copy-start | bytes 786436
  61.3 15.7 %all-to-all-start.2 = ((bf16[8,8,2048]{2,1,0:T(8,128)(2,1)}), bf16[8,8,2048]{2,1,0:T(8,128)(2,1)S(1)}, u32[]{:S(2)}, u32[]{:S(2)}) async-start(bf16[8,8,2048]{2,1,0:T(8,128)(2,1)} %bitcast.18), calls=%async_computation.2 | async-start | bytes 524288 | tf_op jit(solution)/shard_map/all_to_all | solution.py:46
  65.6 76.5 %all-gather.2.cloned.1.call-start = ((), (), s32[]{:S(2)}) async-start(), calls=%async_computation.14 | async-start | bytes 5898240 | tf_op jit(solution)/shard_map/all_gather | solution.py:755
  68.6 14.5 %collective-permute-start.1 = (bf16[1024,128]{1,0:T(8,128)(2,1)S(1)}, bf16[1024,128]{1,0:T(8,128)(2,1)S(1)}, u32[]{:S(2)}, u32[]{:S(2)}) collective-permute-start(bf16[1024,128]{1,0:T(8,128)(2,1)S(1)} %get-tuple-element.47), channel_id=1, source_target_pairs={{0,48},{1,49},{2,50},{3,51},{4,52},{5,53},{6,54},{7,55},{8,56},{9,... | collective-permute-start | bytes 786440 | tf_op jit(solution)/shard_map/ppermute | solution.py:38
  73.2 10.0 %collective-permute-start.2 = (bf16[1024,128]{1,0:T(8,128)(2,1)S(1)}, bf16[1024,128]{1,0:T(8,128)(2,1)S(1)}, u32[]{:S(2)}, u32[]{:S(2)}) collective-permute-start(bf16[1024,128]{1,0:T(8,128)(2,1)S(1)} %get-tuple-element.47), channel_id=1, source_target_pairs={{0,32},{16,48},{1,33},{17,49},{2,34},{18,50},{3,35},{19,51},{4,36}... | collective-permute-start | bytes 786440 | tf_op jit(solution)/shard_map/ppermute | solution.py:38
  74.5 9.4 %collective-permute-start.3 = (bf16[1024,128]{1,0:T(8,128)(2,1)S(1)}, bf16[1024,128]{1,0:T(8,128)(2,1)S(1)}, u32[]{:S(2)}, u32[]{:S(2)}) collective-permute-start(bf16[1024,128]{1,0:T(8,128)(2,1)S(1)} %get-tuple-element.47), channel_id=1, source_target_pairs={{0,16},{16,32},{32,48},{1,17},{17,33},{33,49},{2,18},{18,34},{34,5... | collective-permute-start | bytes 786440 | tf_op jit(solution)/shard_map/ppermute | solution.py:38
  77.2 7.7 %collective-permute-start.4 = (bf16[4,8,2048]{2,1,0:T(8,128)(2,1)S(1)}, bf16[4,8,2048]{2,1,0:T(8,128)(2,1)S(1)}, u32[]{:S(2)}, u32[]{:S(2)}) collective-permute-start(bf16[4,8,2048]{2,1,0:T(8,128)(2,1)S(1)} %get-tuple-element.188), channel_id=1, source_target_pairs={{0,1},{1,0},{2,3},{3,2},{4,5},{5,4},{6,7},{7,6},{8,9},{9,8},{10,11... | collective-permute-start | bytes 393224 | tf_op jit(solution)/shard_map/ppermute | solution.py:30
  85.0 17.3 %collective-permute-start.5 = (bf16[4096,128]{1,0:T(8,128)(2,1)}, bf16[4096,128]{1,0:T(8,128)(2,1)}, u32[]{:S(2)}, u32[]{:S(2)}) collective-permute-start(bf16[4096,128]{1,0:T(8,128)(2,1)} %pad_maximum_fusion), channel_id=1, source_target_pairs={{0,1},{1,0},{2,3},{3,2},{4,5},{5,4},{6,7},{7,6},{8,9},{9,8},{10,11... | collective-permute-start | bytes 3145736 | tf_op jit(solution)/shard_map/ppermute | solution.py:30
  89.4 32.7 %all-to-all-start.3 = ((bf16[8,64,2048]{2,1,0:T(8,128)(2,1)}), bf16[8,64,2048]{2,1,0:T(8,128)(2,1)S(1)}, u32[]{:S(2)}, u32[]{:S(2)}) async-start(bf16[8,64,2048]{2,1,0:T(8,128)(2,1)} %broadcast_in_dim.64), calls=%async_computation.3 | async-start | bytes 4194304 | tf_op jit(solution)/shard_map/all_to_all | solution.py:46
  101.9 8.3 %copy-start.42 = (bf16[128,8,256]{0,2,1:T(8,128)(2,1)}, bf16[128,8,256]{0,2,1:T(8,128)(2,1)S(1)}, u32[]{:S(2)}) copy-start(bf16[128,8,256]{0,2,1:T(8,128)(2,1)S(1)} %copy.78) | copy-start | bytes 1572868
  101.9 7.2 %collective-permute-start.7 = (bf16[128,2048]{0,1:T(8,128)(2,1)S(1)}, bf16[128,2048]{0,1:T(8,128)(2,1)S(1)}, u32[]{:S(2)}, u32[]{:S(2)}) collective-permute-start(bf16[128,2048]{0,1:T(8,128)(2,1)S(1)} %bitcast.247), channel_id=1, source_target_pairs={{0,1},{1,0},{2,3},{3,2},{4,5},{5,4},{6,7},{7,6},{8,9},{9,8},{10,11... | collective-permute-start | bytes 1572872 | tf_op jit(solution)/shard_map/ppermute | solution.py:30
  108.6 1.6 collective-permute-start.6
  109.2 12.9 %copy-start.38 = (bf16[8,4,16,128]{3,2,1,0:T(8,128)(2,1)}, bf16[8,4,16,128]{3,2,1,0:T(8,128)(2,1)S(1)}, u32[]{:S(2)}) copy-start(bf16[8,4,16,128]{3,2,1,0:T(8,128)(2,1)S(1)} %copy.76) | copy-start | bytes 393220
  110.2 11.9 %copy-start.49 = (bf16[512,128]{1,0:T(8,128)(2,1)}, bf16[512,128]{1,0:T(8,128)(2,1)S(1)}, u32[]{:S(2)}) copy-start(bf16[512,128]{1,0:T(8,128)(2,1)S(1)} %collective-permute-done.6) | copy-start | bytes 393220
  122.1 31.3 %all-to-all-start.4 = ((bf16[8,64,2048]{2,1,0:T(8,128)(2,1)}), bf16[8,64,2048]{2,1,0:T(8,128)(2,1)}, u32[]{:S(2)}, u32[]{:S(2)}) async-start(bf16[8,64,2048]{2,1,0:T(8,128)(2,1)} %bitcast.238), calls=%async_computation.4 | async-start | bytes 4194304 | tf_op jit(solution)/shard_map/all_to_all | solution.py:46
  142.1 48.1 %collective-permute-start.9 = (bf16[2048,1152]{1,0:T(8,128)(2,1)}, bf16[2048,1152]{1,0:T(8,128)(2,1)}, u32[]{:S(2)}, u32[]{:S(2)}) collective-permute-start(bf16[2048,1152]{1,0:T(8,128)(2,1)} %all-gather.2.cloned.1.call-done.near_ref), channel_id=1, source_target_pairs={{0,1},{1,0},{2,3},{3,2},{4,5},{5,4},{6,7},{7,6},{8,9},{9,8},{10,11... | collective-permute-start | bytes 14155784 | tf_op jit(solution)/shard_map/ppermute | solution.py:30
  190.2 16.6 %copy-start.4 = (bf16[8,64,2048]{2,1,0:T(8,128)(2,1)}, bf16[8,64,2048]{2,1,0:T(8,128)(2,1)S(1)}, u32[]{:S(2)}) copy-start(bf16[8,64,2048]{2,1,0:T(8,128)(2,1)S(1)} %all_to_all.60) | copy-start | bytes 6291460
  206.8 6.6 %copy-start.7 = (bf16[512,1536]{1,0:T(8,128)(2,1)}, bf16[512,1536]{1,0:T(8,128)(2,1)S(1)}, u32[]{:S(2)}) copy-start(bf16[512,1536]{1,0:T(8,128)(2,1)S(1)} %get-tuple-element.55.wide_ref) | copy-start | bytes 4718596
  213.4 14.8 %collective-permute-start.10 = (bf16[8,1152,256]{2,1,0:T(8,128)(2,1)}, bf16[8,1152,256]{2,1,0:T(8,128)(2,1)}, u32[]{:S(2)}, u32[]{:S(2)}) collective-permute-start(bf16[8,1152,256]{2,1,0:T(8,128)(2,1)} %weights_grad.2), channel_id=1, source_target_pairs={{0,1},{1,0},{2,3},{3,2},{4,5},{5,4},{6,7},{7,6},{8,9},{9,8},{10,11... | collective-permute-start | bytes 14155784 | tf_op jit(solution)/shard_map/ppermute | solution.py:30
  215.9 30.9 %all-to-all-start.6 = ((bf16[8,64,2048]{2,1,0:T(8,128)(2,1)}), bf16[8,64,2048]{2,1,0:T(8,128)(2,1)}, u32[]{:S(2)}, u32[]{:S(2)}) async-start(bf16[8,64,2048]{2,1,0:T(8,128)(2,1)} %bitcast.223), calls=%async_computation.6 | async-start | bytes 4194304 | tf_op jit(solution)/shard_map/all_to_all | solution.py:46
  220.2 125.8 %reduce-scatter.3.cloned.1.call-start = ((), (), s32[]{:S(2)}) async-start(), calls=%async_computation.15 | async-start | bytes 5898240 | tf_op jit(solution)/shard_map/reduce_scatter | solution.py:786
  222.6 5.6 %copy-start.5 = (bf16[8,64,2048]{2,1,0:T(8,128)(2,1)S(1)}, bf16[8,64,2048]{2,1,0:T(8,128)(2,1)}, u32[]{:S(2)}) copy-start(bf16[8,64,2048]{2,1,0:T(8,128)(2,1)} %copy-done.4) | copy-start | bytes 6291460
  222.6 5.6 %copy-start.8 = (bf16[512,1536]{1,0:T(8,128)(2,1)S(1)}, bf16[512,1536]{1,0:T(8,128)(2,1)}, u32[]{:S(2)}) copy-start(bf16[512,1536]{1,0:T(8,128)(2,1)} %copy-done.7) | copy-start | bytes 4718596
  251.6 31.9 %copy-start.43 = (bf16[128,8,256]{0,2,1:T(8,128)(2,1)S(1)}, bf16[128,8,256]{0,2,1:T(8,128)(2,1)}, u32[]{:S(2)}) copy-start(bf16[128,8,256]{0,2,1:T(8,128)(2,1)} %copy-done.42) | copy-start | bytes 1572868
  251.6 31.9 %copy-start.54 = (bf16[128,2048]{0,1:T(8,128)(2,1)S(1)}, bf16[128,2048]{0,1:T(8,128)(2,1)}, u32[]{:S(2)}) copy-start(bf16[128,2048]{0,1:T(8,128)(2,1)} %copy-done.53) | copy-start | bytes 1572868
  284.8 3.5 collective-permute-start.12
  294.5 5.0 %collective-permute-start.13 = (bf16[4096,128]{1,0:T(8,128)(2,1)}, bf16[4096,128]{1,0:T(8,128)(2,1)}, u32[]{:S(2)}, u32[]{:S(2)}) collective-permute-start(bf16[4096,128]{1,0:T(8,128)(2,1)} %get-tuple-element.67), channel_id=1, source_target_pairs={{0,1},{1,0},{2,3},{3,2},{4,5},{5,4},{6,7},{7,6},{8,9},{9,8},{10,11... | collective-permute-start | bytes 3145736 | tf_op jit(solution)/shard_map/ppermute | solution.py:30
  294.8 30.7 %all-to-all-start.8 = ((bf16[8,512,256]{2,1,0:T(8,128)(2,1)}), bf16[8,512,256]{2,1,0:T(8,128)(2,1)}, u32[]{:S(2)}, u32[]{:S(2)}) async-start(bf16[8,512,256]{2,1,0:T(8,128)(2,1)} %down.1), calls=%async_computation.8 | async-start | bytes 4194304 | tf_op jit(solution)/shard_map/all_to_all | solution.py:46
  299.4 7.8 %copy-start.11 = (bf16[2048,128]{1,0:T(8,128)(2,1)S(1)}, bf16[2048,128]{1,0:T(8,128)(2,1)}, u32[]{:S(2)}) copy-start(bf16[2048,128]{1,0:T(8,128)(2,1)} %copy-done.10) | copy-start | bytes 1572868
  299.4 7.8 %copy-start.13 = (bf16[2048,128]{1,0:T(8,128)(2,1)S(1)}, bf16[2048,128]{1,0:T(8,128)(2,1)}, u32[]{:S(2)}) copy-start(bf16[2048,128]{1,0:T(8,128)(2,1)} %copy-done.12) | copy-start | bytes 1572868
  302.4 5.4 %copy-start.40 = (f32[1024,1]{1,0:T(8,128)S(1)}, f32[1024,1]{1,0:T(8,128)}, u32[]{:S(2)}) copy-start(f32[1024,1]{1,0:T(8,128)} %get-tuple-element.60) | copy-start | bytes 12292
  303.3 25.3 %collective-permute-start.14 = (bf16[1024,128]{1,0:T(8,128)(2,1)}, bf16[1024,128]{1,0:T(8,128)(2,1)}, u32[]{:S(2)}, u32[]{:S(2)}) collective-permute-start(bf16[1024,128]{1,0:T(8,128)(2,1)} %get-tuple-element.146), channel_id=1, source_target_pairs={{16,0},{32,16},{48,32},{17,1},{33,17},{49,33},{18,2},{34,18},{50,3... | collective-permute-start | bytes 786440 | tf_op jit(solution)/shard_map/ppermute | solution.py:42
  304.6 24.1 %collective-permute-start.15 = (bf16[1024,128]{1,0:T(8,128)(2,1)}, bf16[1024,128]{1,0:T(8,128)(2,1)}, u32[]{:S(2)}, u32[]{:S(2)}) collective-permute-start(bf16[1024,128]{1,0:T(8,128)(2,1)} %get-tuple-element.148), channel_id=1, source_target_pairs={{32,0},{48,16},{33,1},{49,17},{34,2},{50,18},{35,3},{51,19},{36,4}... | collective-permute-start | bytes 786440 | tf_op jit(solution)/shard_map/ppermute | solution.py:42
  305.9 23.7 %collective-permute-start.16 = (bf16[1024,128]{1,0:T(8,128)(2,1)}, bf16[1024,128]{1,0:T(8,128)(2,1)}, u32[]{:S(2)}, u32[]{:S(2)}) collective-permute-start(bf16[1024,128]{1,0:T(8,128)(2,1)} %get-tuple-element.147), channel_id=1, source_target_pairs={{48,0},{49,1},{50,2},{51,3},{52,4},{53,5},{54,6},{55,7},{56,8},{57... | collective-permute-start | bytes 786440 | tf_op jit(solution)/shard_map/ppermute | solution.py:42
  307.3 45.4 %collective-permute-start.18 = (bf16[2048,256]{1,0:T(8,128)(2,1)S(1)}, bf16[2048,256]{1,0:T(8,128)(2,1)}, u32[]{:S(2)}, u32[]{:S(2)}) collective-permute-start(bf16[2048,256]{1,0:T(8,128)(2,1)S(1)} %pad_maximum_fusion.2.near_weight_ref), channel_id=1, source_target_pairs={{0,1},{1,0},{2,3},{3,2},{4,5},{5,4},{6,7},{7,6},{8,9},{9,8},{10,11... | collective-permute-start | bytes 3145736 | tf_op jit(solution)/shard_map/ppermute | solution.py:30
  327.5 3.4 collective-permute-start.11
  332.3 27.8 %all-to-all-start.9 = ((bf16[8,8,2048]{2,1,0:T(8,128)(2,1)}), bf16[8,8,2048]{2,1,0:T(8,128)(2,1)S(1)}, u32[]{:S(2)}, u32[]{:S(2)}) async-start(bf16[8,8,2048]{2,1,0:T(8,128)(2,1)} %fusion.2), calls=%async_computation.9 | async-start | bytes 524288 | tf_op jit(solution)/shard_map/all_to_all | solution.py:46
  352.3 1.6 collective-permute-start.17
  360.1 5.5 %copy-start.39 = (bf16[8,4,16,128]{3,2,1,0:T(8,128)(2,1)S(1)}, bf16[8,4,16,128]{3,2,1,0:T(8,128)(2,1)}, u32[]{:S(2)}) copy-start(bf16[8,4,16,128]{3,2,1,0:T(8,128)(2,1)} %copy-done.38) | copy-start | bytes 393220
  360.1 5.5 %copy-start.50 = (bf16[512,128]{1,0:T(8,128)(2,1)S(1)}, bf16[512,128]{1,0:T(8,128)(2,1)}, u32[]{:S(2)}) copy-start(bf16[512,128]{1,0:T(8,128)(2,1)} %copy-done.49) | copy-start | bytes 393220
  360.1 33.2 %all-to-all-start.10 = ((bf16[8,544,256]{2,1,0:T(8,128)(2,1)}), bf16[8,544,256]{2,1,0:T(8,128)(2,1)}, u32[]{:S(2)}, u32[]{:S(2)}) async-start(bf16[8,544,256]{2,1,0:T(8,128)(2,1)} %input_part.1), calls=%async_computation.11 | async-start | bytes 4456448 | tf_op jit(solution)/shard_map/all_to_all | solution.py:46
  370.1 34.9 %collective-permute-start.21 = (bf16[128,2048]{1,0:T(8,128)(2,1)}, bf16[128,2048]{1,0:T(8,128)(2,1)}, u32[]{:S(2)}, u32[]{:S(2)}) collective-permute-start(bf16[128,2048]{1,0:T(8,128)(2,1)} %slice.571), channel_id=1, source_target_pairs={{0,1},{1,0},{2,3},{3,2},{4,5},{5,4},{6,7},{7,6},{8,9},{9,8},{10,11... | collective-permute-start | bytes 1572872 | tf_op jit(solution)/shard_map/ppermute | solution.py:30
  395.9 3.0 collective-permute-start.19
  398.1 6.9 %copy-start.30 = (f32[256,2048]{1,0:T(8,128)S(1)}, f32[256,2048]{1,0:T(8,128)}, u32[]{:S(2)}) copy-start(f32[256,2048]{1,0:T(8,128)} %copy-done.29) | copy-start | bytes 6291460
  398.8 16.0 %collective-permute-start.20 = (f32[512,128]{1,0:T(8,128)}, f32[512,128]{1,0:T(8,128)}, u32[]{:S(2)}, u32[]{:S(2)}) collective-permute-start(f32[512,128]{1,0:T(8,128)} %get-tuple-element.158), channel_id=1, source_target_pairs={{0,1},{1,0},{2,3},{3,2},{4,5},{5,4},{6,7},{7,6},{8,9},{9,8},{10,11... | collective-permute-start | bytes 786440 | tf_op jit(solution)/shard_map/ppermute | solution.py:30
  400.2 16.6 %all-to-all-start.11 = ((bf16[8,16,2048]{2,1,0:T(8,128)(2,1)}), bf16[8,16,2048]{2,1,0:T(8,128)(2,1)S(1)}, u32[]{:S(2)}, u32[]{:S(2)}) async-start(bf16[8,16,2048]{2,1,0:T(8,128)(2,1)} %copy.86), calls=%async_computation.12 | async-start | bytes 1048576 | tf_op jit(solution)/shard_map/all_to_all | solution.py:46
  404.9 34.1 %reduce-scatter.5.cloned.1.call-start = ((), (), s32[]{:S(2)}) async-start(), calls=%async_computation.16 | async-start | bytes 1966080 | tf_op jit(solution)/shard_map/reduce_scatter | solution.py:786
  413.3 14.3 %copy-start.36 = (bf16[2,1152,256]{2,1,0:T(8,128)(2,1)S(1)}, bf16[2,1152,256]{2,1,0:T(8,128)(2,1)}, u32[]{:S(2)}) copy-start(bf16[2,1152,256]{2,1,0:T(8,128)(2,1)} %reduce-scatter.3.cloned.1.call-done) | copy-start | bytes 3538948
  413.4 14.3 %collective-permute-start.24 = (bf16[1152,256]{1,0:T(8,128)(2,1)S(1)}, bf16[1152,256]{1,0:T(8,128)(2,1)}, u32[]{:S(2)}, u32[]{:S(2)}) collective-permute-start(bf16[1152,256]{1,0:T(8,128)(2,1)S(1)} %copy-done.37), channel_id=1, source_target_pairs={{0,64},{64,0},{1,65},{65,1},{2,66},{66,2},{3,67},{67,3},{4,68},{68... | collective-permute-start | bytes 1769480 | tf_op jit(solution)/shard_map/ppermute | solution.py:34
  439.0 6.1 %copy-start.45 = (bf16[2,384,256]{2,1,0:T(8,128)(2,1)S(1)}, bf16[2,384,256]{2,1,0:T(8,128)(2,1)}, u32[]{:S(2)}) copy-start(bf16[2,384,256]{2,1,0:T(8,128)(2,1)} %reduce-scatter.5.cloned.1.call-done) | copy-start | bytes 1179652
  440.0 5.1 %collective-permute-start.22 = (bf16[384,256]{1,0:T(8,128)(2,1)S(1)}, bf16[384,256]{1,0:T(8,128)(2,1)S(1)}, u32[]{:S(2)}, u32[]{:S(2)}) collective-permute-start(bf16[384,256]{1,0:T(8,128)(2,1)S(1)} %dynamic-slice_bitcast_fusion.1), channel_id=1, source_target_pairs={{0,64},{64,0},{1,65},{65,1},{2,66},{66,2},{3,67},{67,3},{4,68},{68... | collective-permute-start | bytes 589832 | tf_op jit(solution)/shard_map/ppermute | solution.py:34
  441.3 8.4 %copy-start.1 = (s32[2,3]{1,0:T(2,128)S(1)}, s32[2,3]{1,0:T(2,128)}, u32[]{:S(2)}) copy-start(s32[2,3]{1,0:T(2,128)} %param.17) | copy-start | bytes 76
  445.2 3.8 collective-permute-start.23
  (29 other events, 81.9 us)
Sparse Core Ops, SparseCore 0:
  85.1 56.8 all-gather.1
  246.9 51.8 reduce-scatter.2
  413.5 25.4 reduce-scatter.4
